TPU v7x, 256 devices: a whole 4x4x8 slice. The times are simulated.
256 devices in a mesh: layer: 32 (over y, z), feat: 8 (over x, core).
Axes of the slice: x: 4, y: 4, z: 8, core: 2. Of those that a mesh axis runs over, the one named last changes fastest.
Arguments:
- encoder: bfloat16 [32, 2304, 8192], P('layer', None, 'feat'), may hold values from -0.125 to 0.125
- decoder: bfloat16 [32, 8192, 2304], P('layer', 'feat'), may hold values from -1 to 1
- chosen: int32 [128], replicated, may hold values from 0 to 8191
Outputs:
- virtual: bfloat16 [32, 128, 8192], P('layer', None, 'feat')
Inputs may be any that keep to these rules, and one draw needn't show every extreme that they name: `chosen`: each index names one of the source layer's 8192 features.
All inputs are finite; a program needn't handle non-finite values.
Results may differ from a plain program's by a relative error of at most 0.015.
Values may be sent and summed in bfloat16 or wider, within the bound.
No kernel may reach another device: no remote copies, remote signals or barrier semaphores. Data moves between devices by JAX's collectives and lax.ppermute only.
A program may use at most 128 MiB of HBM per device.

v0:
```python
import jax
import jax.numpy as jnp
from jax import lax
from jax.sharding import PartitionSpec as P


def entering(shard, axis, join, neutral):
    place = lax.axis_index(axis)
    gathered = lax.all_gather(shard.astype(jnp.bfloat16), axis)
    state = jnp.zeros_like(shard) + jnp.asarray(neutral, shard.dtype)

    def one(hop, state):
        return join(state, lax.dynamic_index_in_dim(gathered, hop, 0, False).astype(shard.dtype))

    return lax.fori_loop(0, place, one, state)


def combine_add(earlier, later):
    return earlier + later


def running_rows(rows):
    term = rows.astype(jnp.float32)
    return entering(term, "layer", combine_add, jnp.zeros(rows.shape, jnp.float32))


def local(encoder, decoder, chosen):
    feat_rows = decoder.shape[1]
    offset = chosen - lax.axis_index("feat") * feat_rows
    inside = (offset >= 0) & (offset < feat_rows)
    taken = jnp.take(decoder[0], jnp.clip(offset, 0, feat_rows - 1), axis=0)
    picked = jnp.where(
        inside[:, None], taken.astype(jnp.float32), jnp.zeros(taken.shape, jnp.float32)
    )
    enc_local = encoder[0]
    whole = lax.psum(picked.astype(jnp.bfloat16), "feat")
    prefix_low = running_rows(whole).astype(jnp.bfloat16)
    result = jnp.dot(prefix_low, enc_local, preferred_element_type=jnp.float32)
    return result.astype(jnp.bfloat16)[None]


def solution(mesh):
    placed = (P("layer", None, "feat"), P("layer", "feat", None), P())
    return jax.shard_map(
        local, mesh=mesh, in_specs=placed, out_specs=P("layer", None, "feat"), check_vma=False
    )
```

profile of v0, /device:TPU:248, one launch (start us, length us, event | category | flops | bytes accessed | tf_op | source)
XLA Modules:
  0.0 279.3 jit_solution(5179851171796864949)
XLA Ops:
  6.5 0.0 all-reduce.2.cloned.1.call-start
  6.5 0.7 compare_and_fusion
  7.2 4.5 %gather_fusion = bf16[128,2304]{1,0:T(8,128)(2,1)S(1)} fusion(bf16[1024,2304]{1,0:T(8,128)(2,1)} %bitcast.17, s32[1024]{0:T(1024)S(1)} %pad_clamp_fusion), kind=kCustom, calls=%fused_computation | custom fusion | bytes 1180160 | tf_op jit(solution)/shard_map/jit(_take)/gather | solution.py:31
  11.7 1.2 fusion.8
  12.9 0.0 all-reduce.2.cloned.1.call-update
  12.9 0.0 all-gather.2.cloned.1.call-start
  13.0 66.4 %all-reduce.2.cloned.1.call-done = bf16[1,128,2304]{2,1,0:T(8,128)(2,1)} async-done(((bf16[1,128,2304]{2,1,0:T(8,128)(2,1)}), bf16[1,128,2304]{2,1,0:T(8,128)(2,1)}) %all-reduce.2.cloned.1.call-update) | async-done | bytes 589840 | tf_op jit(solution)/shard_map/psum | solution.py:36
  79.4 0.0 all-gather.2.cloned.1.call-update
  79.4 148.8 %all-gather.2.cloned.1.call-done = bf16[32,128,2304]{2,1,0:T(8,128)(2,1)} async-done(((bf16[1,128,2304]{2,1,0:T(8,128)(2,1)}), bf16[32,128,2304]{2,1,0:T(8,128)(2,1)}) %all-gather.2.cloned.1.call-update) | async-done | bytes 18874384 | tf_op jit(solution)/shard_map/all_gather | solution.py:9
  228.2 0.1 broadcast.7
  228.3 40.3 %while.10 = (s32[]{:T(128)}, f32[128,2304]{1,0:T(8,128)S(1)}, s32[]{:T(128)}, bf16[32,128,2304]{2,1,0:T(8,128)(2,1)}, s32[]{:T(128)}, /*index=5*/s32[]{:T(128)}, s32[]{:T(128)}) while((s32[]{:T(128)}, f32[128,2304]{1,0:T(8,128)S(1)}, s32[]{:T(128)}, bf16[32,128,2304]{2,1,0:T(8,128)(2,1)}, s32[]{:T(128)}, /*index=5*/s32[]{:T(128)}, ...), condition=%wide.region_2.3_spmd, body=%wide.region_1.2_spmd.sunk | while | flops 589829 | bytes 2949243 | solution.py:15
  228.3 1.3 convert_add_fusion.2
  229.6 1.3 convert_add_fusion.2
  230.9 1.3 convert_add_fusion.2
  232.2 1.3 convert_add_fusion.2
  233.5 1.3 convert_add_fusion.2
  234.8 1.3 convert_add_fusion.2
  236.1 1.3 convert_add_fusion.2
  237.4 1.3 convert_add_fusion.2
  238.7 1.3 convert_add_fusion.2
  240.0 1.3 convert_add_fusion.2
  241.3 1.3 convert_add_fusion.2
  242.6 1.3 convert_add_fusion.2
  243.9 1.3 convert_add_fusion.2
  245.2 1.3 convert_add_fusion.2
  246.5 1.3 convert_add_fusion.2
  247.8 1.3 convert_add_fusion.2
  249.1 1.3 convert_add_fusion.2
  250.4 1.3 convert_add_fusion.2
  251.7 1.3 convert_add_fusion.2
  253.0 1.3 convert_add_fusion.2
  254.3 1.3 convert_add_fusion.2
  255.6 1.3 convert_add_fusion.2
  256.9 1.3 convert_add_fusion.2
  258.2 1.3 convert_add_fusion.2
  259.5 1.3 convert_add_fusion.2
  260.8 1.3 convert_add_fusion.2
  262.1 1.3 convert_add_fusion.2
  263.4 1.3 convert_add_fusion.2
  264.7 1.3 convert_add_fusion.2
  266.0 1.3 convert_add_fusion.2
  267.3 1.3 convert_add_fusion.2
  268.6 3.8 %fusion.5 = bf16[1,128,1024]{2,1,0:T(8,128)(2,1)} fusion(bf16[1,2304,1024]{2,1,0:T(8,128)(2,1)} %param.5, f32[128,2304]{1,0:T(8,128)S(1)} %get-tuple-element.28), kind=kOutput, calls=%fused_computation.6 | convolution fusion | flops 604405760 | bytes 6160384 | tf_op jit(solution)/shard_map/dot_general | solution.py:38
  (1 shorter events, 0.0 us)
Async XLA Ops:
  6.5 72.9 %all-reduce.2.cloned.1.call-start = ((), (), s32[]{:S(2)}) async-start(), calls=%async_computation | async-start | bytes 1179648 | tf_op jit(solution)/shard_map/psum | solution.py:36
  12.9 215.3 %all-gather.2.cloned.1.call-start = ((), (), s32[]{:S(2)}) async-start(), calls=%async_computation.1 | async-start | bytes 19464192 | tf_op jit(solution)/shard_map/all_gather | solution.py:9
Sparse Core Ops, SparseCore 0:
  13.0 66.3 all-reduce.1
  82.0 146.1 all-gather.1
where the time goes:
time: 281 us; the launch traced here: 279 us
  waiting for transfers between devices  215 us (77%)
  other arithmetic  41.5 us (15%)
  between operations  13.4 us (5%)
  local copies, waits for them, and re-layouts  4.57 us (2%)
  matrix products  3.83 us (1%)
    all_gather x1, waiting for transfers between devices, entering(): gathered = lax.all_gather(shard.astype(jnp.bfloat16), axis)  149 us
    psum x1, waiting for transfers between devices, local(): whole = lax.psum(picked.astype(jnp.bfloat16), 'feat')  66.4 us
    add x31, other arithmetic, combine_add(): return earlier + later  39.6 us
  transfers between devices with their start and end apart: 2, of which 2 were waited for; matrix products, arithmetic and copies ran while one was open for 0% of the time, Pallas kernels for 0%

commit v1 on v0

v1 whole, which is shorter than its diff:
```python
import jax
import jax.numpy as jnp
from jax import lax
from jax.sharding import PartitionSpec as P

BF = jnp.bfloat16
F32 = jnp.float32


def local(encoder, decoder, chosen):
    enc, dec = encoder[0], decoder[0]
    feats, width = dec.shape
    k = chosen.shape[0]
    half, rows = width // 2, k // 4
    feat, layer = lax.axis_index("feat"), lax.axis_index("layer")
    x, c = feat // 2, feat % 2
    z = layer % 8

    def feat_step(v, move):
        return lax.ppermute(v, "feat", [(i, move(i)) for i in range(8)])

    def layer_step(v, move):
        return lax.ppermute(v, "layer", [(i, move(i)) for i in range(32)])

    def swap_cores(v):
        return feat_step(v, lambda i: i ^ 1)

    def along_x(v, d):
        return feat_step(v, lambda i: (i + 2 * d) % 8)

    offset = chosen - feat * feats
    onehot = (offset[:, None] == jnp.arange(feats)[None, :]).astype(BF)

    def picked(side):
        part = lax.dynamic_slice_in_dim(dec, side * half, half, 1)
        return jnp.dot(onehot, part, preferred_element_type=F32).astype(BF)

    away = swap_cores(picked(1 - c))
    mine = picked(c) + away

    def chunk(d):
        return lax.dynamic_slice_in_dim(mine, rows * ((x + d) % 4), rows, 0)

    got = [along_x(chunk(d), d) for d in (1, 2, 3)]
    total = chunk(0).astype(F32)
    for g in got:
        total = total + g.astype(F32)

    before = jnp.zeros_like(total)
    for bit, move in ((1, lambda i: i ^ 1), (2, lambda i: i ^ 2), (4, lambda i: i ^ 7)):
        other = layer_step(total.astype(BF), move).astype(F32)
        before = before + jnp.where((z & bit) != 0, other, 0.0)
        total = total + other
    low = total.astype(BF)
    for d in (1, 2, 3):
        pairs = [(i, i + 8 * d) for i in range(32 - 8 * d)]
        before = before + lax.ppermute(low, "layer", pairs).astype(F32)
    prefix = before.astype(BF)

    whole = jnp.zeros((k, half), BF)
    for d in (0, 1, 2, 3):
        piece = along_x(prefix, d) if d else prefix
        whole = lax.dynamic_update_slice_in_dim(whole, piece, rows * ((x - d) % 4), 0)
    other_half = swap_cores(whole)

    def product(v, side):
        part = lax.dynamic_slice_in_dim(enc, side * half, half, 0)
        return jnp.dot(v, part, preferred_element_type=F32)

    result = product(whole, c) + product(other_half, 1 - c)
    return result.astype(BF)[None]


def solution(mesh):
    placed = (P("layer", None, "feat"), P("layer", "feat", None), P())
    return jax.shard_map(
        local, mesh=mesh, in_specs=placed, out_specs=P("layer", None, "feat"), check_vma=False
    )
```

time: 281 us -> 62.2 us (0.22)
  the two profiles are of different devices: /device:TPU:248 before, /device:TPU:1 now
where the time goes in v1:
time: 62.2 us; the launch traced here: 62 us
  starting transfers between devices  31.8 us (51%)
  waiting for transfers between devices  19.6 us (32%)
  matrix products  9.51 us (15%)
  other arithmetic  0.89 us (1%)
    ppermute x8, starting transfers between devices, feat_step(): return lax.ppermute(v, 'feat', [(i, move(i)) for i in range(8)])  17.8 us
    ppermute x8, waiting for transfers between devices, feat_step(): return lax.ppermute(v, 'feat', [(i, move(i)) for i in range(8)])  9.26 us
    ppermute x3, waiting for transfers between devices, layer_step(): return lax.ppermute(v, 'layer', [(i, move(i)) for i in range(32)])  8.94 us
    ppermute x3, starting transfers between devices, local(): before = before + lax.ppermute(low, 'layer', pairs).astype(F32)  8.41 us
    ppermute x3, starting transfers between devices, layer_step(): return lax.ppermute(v, 'layer', [(i, move(i)) for i in range(32)])  5.54 us
    dot_general x2, matrix products, product(): return jnp.dot(v, part, preferred_element_type=F32)  5.08 us
    dot_general x2, matrix products, picked(): return jnp.dot(onehot, part, preferred_element_type=F32).astype(BF)  4.43 us
    ppermute x3, waiting for transfers between devices, local(): before = before + lax.ppermute(low, 'layer', pairs).astype(F32)  1.35 us
  transfers between devices with their start and end apart: 14, of which 11 were waited for; matrix products, arithmetic and copies ran while one was open for 0% of the time, Pallas kernels for 0%

profile of v1, /device:TPU:1, one launch (start us, length us, event | category | flops | bytes accessed | tf_op | source)
XLA Modules:
  0.0 62.0 jit_solution(15108614051505051981)
XLA Ops:
  0.0 0.7 %broadcast_subtract_fusion = s32[128]{0:T(128)S(1)} fusion(s32[128]{0:T(128)} %param.5, s32[]{:T(128)S(6)} %mul.33), kind=kLoop, calls=%fused_computation.46 | loop fusion | flops 128 | bytes 1028 | tf_op jit(solution)/shard_map/sub | solution.py:31
  0.7 2.2 %convolution_convert_fusion = bf16[128,1152]{1,0:T(8,128)(2,1)S(1)} fusion(bf16[1,1024,2304]{2,1,0:T(8,128)(2,1)} %param.4, s32[]{:T(128)S(6)} %select_n.99, s32[128]{0:T(128)S(1)} %broadcast_subtract_fusion), kind=kOutput, calls=%fused_computation | convolution fusion | flops 302268416 | bytes 2654724 | tf_op jit(solution)/shard_map/dot_general | solution.py:36
  2.9 3.3 %collective-permute-start = (bf16[128,1152]{1,0:T(8,128)(2,1)S(1)}, bf16[128,1152]{1,0:T(8,128)(2,1)S(1)}, u32[]{:S(2)}, u32[]{:S(2)}) collective-permute-start(bf16[128,1152]{1,0:T(8,128)(2,1)S(1)} %convolution_convert_fusion), channel_id=1, source_target_pairs={{0,1},{1,0},{2,3},{3,2},{4,5},{5,4},{6,7},{7,6},{8,9},{9,8},{10,11... | collective-permute-start | bytes 884744 | tf_op jit(solution)/shard_map/ppermute | solution.py:20
  6.2 1.2 %collective-permute-done = bf16[128,1152]{1,0:T(8,128)(2,1)S(1)} collective-permute-done((bf16[128,1152]{1,0:T(8,128)(2,1)S(1)}, bf16[128,1152]{1,0:T(8,128)(2,1)S(1)}, u32[]{:S(2)}, u32[]{:S(2)}) %collective-permute-start) | collective-permute-done | bytes 294944 | tf_op jit(solution)/shard_map/ppermute | solution.py:20
  7.4 2.2 %fusion = bf16[128,1152]{1,0:T(8,128)(2,1)S(1)} fusion(bf16[128,1152]{1,0:T(8,128)(2,1)S(1)} %collective-permute-done, bf16[1,1024,2304]{2,1,0:T(8,128)(2,1)} %param.4, s32[]{:T(128)S(6)} %select_n.98, s32[128]{0:T(128)S(1)} %broadcast_subtract_fusion), kind=kOutput, calls=%fused_computation.2 | convolution fusion | flops 302415872 | bytes 2949636 | tf_op jit(solution)/shard_map/dot_general | solution.py:36
  9.7 0.1 collective-permute-start.1
  9.8 2.7 %collective-permute-start.3 = (bf16[32,1152]{1,0:T(8,128)(2,1)S(1)}, bf16[32,1152]{1,0:T(8,128)(2,1)S(1)}, u32[]{:S(2)}, u32[]{:S(2)}) collective-permute-start(bf16[32,1152]{1,0:T(8,128)(2,1)S(1)} %get-tuple-element.10), channel_id=1, source_target_pairs={{0,6},{1,7},{2,0},{3,1},{4,2},{5,3},{6,4},{7,5},{8,14},{9,15},{10,... | collective-permute-start | bytes 221192 | tf_op jit(solution)/shard_map/ppermute | solution.py:20
  12.4 0.0 collective-permute-start.2
  12.4 1.7 %collective-permute-done.1 = bf16[32,1152]{1,0:T(8,128)(2,1)S(1)} collective-permute-done((bf16[32,1152]{1,0:T(8,128)(2,1)S(1)}, bf16[32,1152]{1,0:T(8,128)(2,1)S(1)}, u32[]{:S(2)}, u32[]{:S(2)}) %collective-permute-start.1) | collective-permute-done | bytes 73760 | tf_op jit(solution)/shard_map/ppermute | solution.py:20
  14.2 1.4 %collective-permute-done.3 = bf16[32,1152]{1,0:T(8,128)(2,1)S(1)} collective-permute-done((bf16[32,1152]{1,0:T(8,128)(2,1)S(1)}, bf16[32,1152]{1,0:T(8,128)(2,1)S(1)}, u32[]{:S(2)}, u32[]{:S(2)}) %collective-permute-start.3) | collective-permute-done | bytes 73760 | tf_op jit(solution)/shard_map/ppermute | solution.py:20
  15.5 1.6 %collective-permute-done.2 = bf16[32,1152]{1,0:T(8,128)(2,1)S(1)} collective-permute-done((bf16[32,1152]{1,0:T(8,128)(2,1)S(1)}, bf16[32,1152]{1,0:T(8,128)(2,1)S(1)}, u32[]{:S(2)}, u32[]{:S(2)}) %collective-permute-start.2) | collective-permute-done | bytes 73760 | tf_op jit(solution)/shard_map/ppermute | solution.py:20
  17.2 0.1 collective-permute-start.4
  17.3 3.2 %collective-permute-done.4 = bf16[32,1152]{1,0:T(8,128)(2,1)S(1)} collective-permute-done((bf16[32,1152]{1,0:T(8,128)(2,1)S(1)}, bf16[32,1152]{1,0:T(8,128)(2,1)S(1)}, u32[]{:S(2)}, u32[]{:S(2)}) %collective-permute-start.4) | collective-permute-done | bytes 73760 | tf_op jit(solution)/shard_map/ppermute | solution.py:23
  20.5 1.5 %collective-permute-start.5 = (bf16[32,1152]{1,0:T(8,128)(2,1)S(1)}, bf16[32,1152]{1,0:T(8,128)(2,1)S(1)}, u32[]{:S(2)}, u32[]{:S(2)}) collective-permute-start(bf16[32,1152]{1,0:T(8,128)(2,1)S(1)} %fusion.29), channel_id=1, source_target_pairs={{0,16},{8,24},{16,0},{24,8},{32,48},{40,56},{48,32},{56,40},{64,80... | collective-permute-start | bytes 221192 | tf_op jit(solution)/shard_map/ppermute | solution.py:23
  22.0 3.5 %collective-permute-done.5 = bf16[32,1152]{1,0:T(8,128)(2,1)S(1)} collective-permute-done((bf16[32,1152]{1,0:T(8,128)(2,1)S(1)}, bf16[32,1152]{1,0:T(8,128)(2,1)S(1)}, u32[]{:S(2)}, u32[]{:S(2)}) %collective-permute-start.5) | collective-permute-done | bytes 73760 | tf_op jit(solution)/shard_map/ppermute | solution.py:23
  25.5 3.9 %collective-permute-start.6 = (bf16[32,1152]{1,0:T(8,128)(2,1)S(1)}, bf16[32,1152]{1,0:T(8,128)(2,1)S(1)}, u32[]{:S(2)}, u32[]{:S(2)}) collective-permute-start(bf16[32,1152]{1,0:T(8,128)(2,1)S(1)} %fusion.30), channel_id=1, source_target_pairs={{0,56},{8,48},{16,40},{24,32},{32,24},{40,16},{48,8},{56,0},{64,12... | collective-permute-start | bytes 221192 | tf_op jit(solution)/shard_map/ppermute | solution.py:23
  29.4 2.3 %collective-permute-done.6 = bf16[32,1152]{1,0:T(8,128)(2,1)S(1)} collective-permute-done((bf16[32,1152]{1,0:T(8,128)(2,1)S(1)}, bf16[32,1152]{1,0:T(8,128)(2,1)S(1)}, u32[]{:S(2)}, u32[]{:S(2)}) %collective-permute-start.6) | collective-permute-done | bytes 73760 | tf_op jit(solution)/shard_map/ppermute | solution.py:23
  31.8 4.6 %collective-permute-start.9 = (bf16[32,1152]{1,0:T(8,128)(2,1)S(1)}, bf16[32,1152]{1,0:T(8,128)(2,1)S(1)}, u32[]{:S(2)}, u32[]{:S(2)}) collective-permute-start(bf16[32,1152]{1,0:T(8,128)(2,1)S(1)} %fusion.28), channel_id=1, source_target_pairs={{0,192},{8,200},{16,208},{24,216},{32,224},{40,232},{48,240},{56,2... | collective-permute-start | bytes 221192 | tf_op jit(solution)/shard_map/ppermute | solution.py:57
  36.4 1.3 %collective-permute-start.8 = (bf16[32,1152]{1,0:T(8,128)(2,1)S(1)}, bf16[32,1152]{1,0:T(8,128)(2,1)S(1)}, u32[]{:S(2)}, u32[]{:S(2)}) collective-permute-start(bf16[32,1152]{1,0:T(8,128)(2,1)S(1)} %fusion.28), channel_id=1, source_target_pairs={{0,128},{8,136},{16,144},{24,152},{32,160},{40,168},{48,176},{56,1... | collective-permute-start | bytes 221192 | tf_op jit(solution)/shard_map/ppermute | solution.py:57
  37.7 2.5 %collective-permute-start.7 = (bf16[32,1152]{1,0:T(8,128)(2,1)S(1)}, bf16[32,1152]{1,0:T(8,128)(2,1)S(1)}, u32[]{:S(2)}, u32[]{:S(2)}) collective-permute-start(bf16[32,1152]{1,0:T(8,128)(2,1)S(1)} %fusion.28), channel_id=1, source_target_pairs={{0,64},{8,72},{16,80},{24,88},{32,96},{40,104},{48,112},{56,120},{... | collective-permute-start | bytes 221192 | tf_op jit(solution)/shard_map/ppermute | solution.py:57
  40.2 0.0 collective-permute-done.9
  40.3 0.0 collective-permute-done.8
  40.3 1.3 %collective-permute-done.7 = bf16[32,1152]{1,0:T(8,128)(2,1)S(1)} collective-permute-done((bf16[32,1152]{1,0:T(8,128)(2,1)S(1)}, bf16[32,1152]{1,0:T(8,128)(2,1)S(1)}, u32[]{:S(2)}, u32[]{:S(2)}) %collective-permute-start.7) | collective-permute-done | bytes 73760 | tf_op jit(solution)/shard_map/ppermute | solution.py:57
  41.6 0.1 constant_dynamic-update-slice_fusion.3
  41.7 1.2 %collective-permute-start.10 = (bf16[32,1152]{1,0:T(8,128)(2,1)S(1)}, bf16[32,1152]{1,0:T(8,128)(2,1)S(1)}, u32[]{:S(2)}, u32[]{:S(2)}) collective-permute-start(bf16[32,1152]{1,0:T(8,128)(2,1)S(1)} %get-tuple-element.6), channel_id=1, source_target_pairs={{0,2},{1,3},{2,4},{3,5},{4,6},{5,7},{6,0},{7,1},{8,10},{9,11},{10,... | collective-permute-start | bytes 221192 | tf_op jit(solution)/shard_map/ppermute | solution.py:20
  43.0 1.4 %collective-permute-start.11 = (bf16[32,1152]{1,0:T(8,128)(2,1)S(1)}, bf16[32,1152]{1,0:T(8,128)(2,1)S(1)}, u32[]{:S(2)}, u32[]{:S(2)}) collective-permute-start(bf16[32,1152]{1,0:T(8,128)(2,1)S(1)} %get-tuple-element.6), channel_id=1, source_target_pairs={{0,4},{1,5},{2,6},{3,7},{4,0},{5,1},{6,2},{7,3},{8,12},{9,13},{10,... | collective-permute-start | bytes 221192 | tf_op jit(solution)/shard_map/ppermute | solution.py:20
  44.4 1.1 %collective-permute-start.12 = (bf16[32,1152]{1,0:T(8,128)(2,1)S(1)}, bf16[32,1152]{1,0:T(8,128)(2,1)S(1)}, u32[]{:S(2)}, u32[]{:S(2)}) collective-permute-start(bf16[32,1152]{1,0:T(8,128)(2,1)S(1)} %get-tuple-element.6), channel_id=1, source_target_pairs={{0,6},{1,7},{2,0},{3,1},{4,2},{5,3},{6,4},{7,5},{8,14},{9,15},{10,... | collective-permute-start | bytes 221192 | tf_op jit(solution)/shard_map/ppermute | solution.py:20
  45.5 0.7 %collective-permute-done.10 = bf16[32,1152]{1,0:T(8,128)(2,1)S(1)} collective-permute-done((bf16[32,1152]{1,0:T(8,128)(2,1)S(1)}, bf16[32,1152]{1,0:T(8,128)(2,1)S(1)}, u32[]{:S(2)}, u32[]{:S(2)}) %collective-permute-start.10) | collective-permute-done | bytes 73760 | tf_op jit(solution)/shard_map/ppermute | solution.py:20
  46.2 1.4 %collective-permute-done.11 = bf16[32,1152]{1,0:T(8,128)(2,1)S(1)} collective-permute-done((bf16[32,1152]{1,0:T(8,128)(2,1)S(1)}, bf16[32,1152]{1,0:T(8,128)(2,1)S(1)}, u32[]{:S(2)}, u32[]{:S(2)}) %collective-permute-start.11) | collective-permute-done | bytes 73760 | tf_op jit(solution)/shard_map/ppermute | solution.py:20
  47.7 0.0 collective-permute-done.12
  47.7 8.0 %collective-permute-start.13 = (bf16[128,1152]{1,0:T(8,128)(2,1)S(1)}, bf16[128,1152]{1,0:T(8,128)(2,1)S(1)}, u32[]{:S(2)}, u32[]{:S(2)}) collective-permute-start(bf16[128,1152]{1,0:T(8,128)(2,1)S(1)} %constant_dynamic-update-slice_fusion), channel_id=1, source_target_pairs={{0,1},{1,0},{2,3},{3,2},{4,5},{5,4},{6,7},{7,6},{8,9},{9,8},{10,11... | collective-permute-start | bytes 884744 | tf_op jit(solution)/shard_map/ppermute | solution.py:20
  55.7 1.2 %collective-permute-done.13 = bf16[128,1152]{1,0:T(8,128)(2,1)S(1)} collective-permute-done((bf16[128,1152]{1,0:T(8,128)(2,1)S(1)}, bf16[128,1152]{1,0:T(8,128)(2,1)S(1)}, u32[]{:S(2)}, u32[]{:S(2)}) %collective-permute-start.13) | collective-permute-done | bytes 294944 | tf_op jit(solution)/shard_map/ppermute | solution.py:20
  56.9 2.2 %fusion.1 = f32[128,1024]{1,0:T(8,128)S(1)} fusion(bf16[128,1152]{1,0:T(8,128)(2,1)S(1)} %collective-permute-done.13, bf16[1,2304,1024]{2,1,0:T(8,128)(2,1)} %param.3, s32[]{:T(128)S(6)} %select_n.99), kind=kOutput, calls=%fused_computation.3 | convolution fusion | flops 301989888 | bytes 3178500 | tf_op jit(solution)/shard_map/dot_general | solution.py:68
  59.1 2.9 %fusion.17 = bf16[1,128,1024]{2,1,0:T(8,128)(2,1)} fusion(f32[128,1024]{1,0:T(8,128)S(1)} %fusion.1, bf16[128,1152]{1,0:T(8,128)(2,1)S(1)} %constant_dynamic-update-slice_fusion, bf16[1,2304,1024]{2,1,0:T(8,128)(2,1)} %param.3, s32[]{:T(128)S(6)} %select_n.98), kind=kOutput, calls=%fused_computation.15 | convolution fusion | flops 302252032 | bytes 3440644 | tf_op jit(solution)/shard_map/dot_general | solution.py:68
  (9 shorter events, 0.2 us)
Async XLA Ops:
  2.9 4.5 %collective-permute-start = (bf16[128,1152]{1,0:T(8,128)(2,1)S(1)}, bf16[128,1152]{1,0:T(8,128)(2,1)S(1)}, u32[]{:S(2)}, u32[]{:S(2)}) collective-permute-start(bf16[128,1152]{1,0:T(8,128)(2,1)S(1)} %convolution_convert_fusion), channel_id=1, source_target_pairs={{0,1},{1,0},{2,3},{3,2},{4,5},{5,4},{6,7},{7,6},{8,9},{9,8},{10,11... | collective-permute-start | bytes 884744 | tf_op jit(solution)/shard_map/ppermute | solution.py:20
  9.7 4.5 %collective-permute-start.1 = (bf16[32,1152]{1,0:T(8,128)(2,1)S(1)}, bf16[32,1152]{1,0:T(8,128)(2,1)S(1)}, u32[]{:S(2)}, u32[]{:S(2)}) collective-permute-start(bf16[32,1152]{1,0:T(8,128)(2,1)S(1)} %get-tuple-element.9), channel_id=1, source_target_pairs={{0,2},{1,3},{2,4},{3,5},{4,6},{5,7},{6,0},{7,1},{8,10},{9,11},{10,... | collective-permute-start | bytes 221192 | tf_op jit(solution)/shard_map/ppermute | solution.py:20
  9.8 5.8 %collective-permute-start.3 = (bf16[32,1152]{1,0:T(8,128)(2,1)S(1)}, bf16[32,1152]{1,0:T(8,128)(2,1)S(1)}, u32[]{:S(2)}, u32[]{:S(2)}) collective-permute-start(bf16[32,1152]{1,0:T(8,128)(2,1)S(1)} %get-tuple-element.10), channel_id=1, source_target_pairs={{0,6},{1,7},{2,0},{3,1},{4,2},{5,3},{6,4},{7,5},{8,14},{9,15},{10,... | collective-permute-start | bytes 221192 | tf_op jit(solution)/shard_map/ppermute | solution.py:20
  12.4 4.7 %collective-permute-start.2 = (bf16[32,1152]{1,0:T(8,128)(2,1)S(1)}, bf16[32,1152]{1,0:T(8,128)(2,1)S(1)}, u32[]{:S(2)}, u32[]{:S(2)}) collective-permute-start(bf16[32,1152]{1,0:T(8,128)(2,1)S(1)} %get-tuple-element.11), channel_id=1, source_target_pairs={{0,4},{1,5},{2,6},{3,7},{4,0},{5,1},{6,2},{7,3},{8,12},{9,13},{10,... | collective-permute-start | bytes 221192 | tf_op jit(solution)/shard_map/ppermute | solution.py:20
  17.2 3.3 %collective-permute-start.4 = (bf16[32,1152]{1,0:T(8,128)(2,1)S(1)}, bf16[32,1152]{1,0:T(8,128)(2,1)S(1)}, u32[]{:S(2)}, u32[]{:S(2)}) collective-permute-start(bf16[32,1152]{1,0:T(8,128)(2,1)S(1)} %get-tuple-element.7), channel_id=1, source_target_pairs={{0,8},{8,0},{16,24},{24,16},{32,40},{40,32},{48,56},{56,48},{64,72... | collective-permute-start | bytes 221192 | tf_op jit(solution)/shard_map/ppermute | solution.py:23
  20.5 5.0 %collective-permute-start.5 = (bf16[32,1152]{1,0:T(8,128)(2,1)S(1)}, bf16[32,1152]{1,0:T(8,128)(2,1)S(1)}, u32[]{:S(2)}, u32[]{:S(2)}) collective-permute-start(bf16[32,1152]{1,0:T(8,128)(2,1)S(1)} %fusion.29), channel_id=1, source_target_pairs={{0,16},{8,24},{16,0},{24,8},{32,48},{40,56},{48,32},{56,40},{64,80... | collective-permute-start | bytes 221192 | tf_op jit(solution)/shard_map/ppermute | solution.py:23
  25.5 6.2 %collective-permute-start.6 = (bf16[32,1152]{1,0:T(8,128)(2,1)S(1)}, bf16[32,1152]{1,0:T(8,128)(2,1)S(1)}, u32[]{:S(2)}, u32[]{:S(2)}) collective-permute-start(bf16[32,1152]{1,0:T(8,128)(2,1)S(1)} %fusion.30), channel_id=1, source_target_pairs={{0,56},{8,48},{16,40},{24,32},{32,24},{40,16},{48,8},{56,0},{64,12... | collective-permute-start | bytes 221192 | tf_op jit(solution)/shard_map/ppermute | solution.py:23
  31.8 8.5 %collective-permute-start.9 = (bf16[32,1152]{1,0:T(8,128)(2,1)S(1)}, bf16[32,1152]{1,0:T(8,128)(2,1)S(1)}, u32[]{:S(2)}, u32[]{:S(2)}) collective-permute-start(bf16[32,1152]{1,0:T(8,128)(2,1)S(1)} %fusion.28), channel_id=1, source_target_pairs={{0,192},{8,200},{16,208},{24,216},{32,224},{40,232},{48,240},{56,2... | collective-permute-start | bytes 221192 | tf_op jit(solution)/shard_map/ppermute | solution.py:57
  36.4 3.8 %collective-permute-start.8 = (bf16[32,1152]{1,0:T(8,128)(2,1)S(1)}, bf16[32,1152]{1,0:T(8,128)(2,1)S(1)}, u32[]{:S(2)}, u32[]{:S(2)}) collective-permute-start(bf16[32,1152]{1,0:T(8,128)(2,1)S(1)} %fusion.28), channel_id=1, source_target_pairs={{0,128},{8,136},{16,144},{24,152},{32,160},{40,168},{48,176},{56,1... | collective-permute-start | bytes 221192 | tf_op jit(solution)/shard_map/ppermute | solution.py:57
  37.7 3.9 %collective-permute-start.7 = (bf16[32,1152]{1,0:T(8,128)(2,1)S(1)}, bf16[32,1152]{1,0:T(8,128)(2,1)S(1)}, u32[]{:S(2)}, u32[]{:S(2)}) collective-permute-start(bf16[32,1152]{1,0:T(8,128)(2,1)S(1)} %fusion.28), channel_id=1, source_target_pairs={{0,64},{8,72},{16,80},{24,88},{32,96},{40,104},{48,112},{56,120},{... | collective-permute-start | bytes 221192 | tf_op jit(solution)/shard_map/ppermute | solution.py:57
  41.7 4.5 %collective-permute-start.10 = (bf16[32,1152]{1,0:T(8,128)(2,1)S(1)}, bf16[32,1152]{1,0:T(8,128)(2,1)S(1)}, u32[]{:S(2)}, u32[]{:S(2)}) collective-permute-start(bf16[32,1152]{1,0:T(8,128)(2,1)S(1)} %get-tuple-element.6), channel_id=1, source_target_pairs={{0,2},{1,3},{2,4},{3,5},{4,6},{5,7},{6,0},{7,1},{8,10},{9,11},{10,... | collective-permute-start | bytes 221192 | tf_op jit(solution)/shard_map/ppermute | solution.py:20
  43.0 4.7 %collective-permute-start.11 = (bf16[32,1152]{1,0:T(8,128)(2,1)S(1)}, bf16[32,1152]{1,0:T(8,128)(2,1)S(1)}, u32[]{:S(2)}, u32[]{:S(2)}) collective-permute-start(bf16[32,1152]{1,0:T(8,128)(2,1)S(1)} %get-tuple-element.6), channel_id=1, source_target_pairs={{0,4},{1,5},{2,6},{3,7},{4,0},{5,1},{6,2},{7,3},{8,12},{9,13},{10,... | collective-permute-start | bytes 221192 | tf_op jit(solution)/shard_map/ppermute | solution.py:20
  44.4 3.3 %collective-permute-start.12 = (bf16[32,1152]{1,0:T(8,128)(2,1)S(1)}, bf16[32,1152]{1,0:T(8,128)(2,1)S(1)}, u32[]{:S(2)}, u32[]{:S(2)}) collective-permute-start(bf16[32,1152]{1,0:T(8,128)(2,1)S(1)} %get-tuple-element.6), channel_id=1, source_target_pairs={{0,6},{1,7},{2,0},{3,1},{4,2},{5,3},{6,4},{7,5},{8,14},{9,15},{10,... | collective-permute-start | bytes 221192 | tf_op jit(solution)/shard_map/ppermute | solution.py:20
  47.7 9.2 %collective-permute-start.13 = (bf16[128,1152]{1,0:T(8,128)(2,1)S(1)}, bf16[128,1152]{1,0:T(8,128)(2,1)S(1)}, u32[]{:S(2)}, u32[]{:S(2)}) collective-permute-start(bf16[128,1152]{1,0:T(8,128)(2,1)S(1)} %constant_dynamic-update-slice_fusion), channel_id=1, source_target_pairs={{0,1},{1,0},{2,3},{3,2},{4,5},{5,4},{6,7},{7,6},{8,9},{9,8},{10,11... | collective-permute-start | bytes 884744 | tf_op jit(solution)/shard_map/ppermute | solution.py:20

commit v2 on v1

v2 whole, which is shorter than its diff:
```python
import jax
import jax.numpy as jnp
from jax import lax
from jax.experimental import pallas as pl
from jax.experimental.pallas import tpu as pltpu
from jax.sharding import PartitionSpec as P

BF = jnp.bfloat16
F32 = jnp.float32
MIB = 2**20
PARTS = 3


def pick_kernel(flip, chosen_ref, dec_ref, out_ref, hot_ref, buf_ref, list_ref, sems):
    k, feats = hot_ref.shape
    half = out_ref.shape[1]
    wide = half // PARTS
    feat = lax.axis_index("feat")
    side = (feat + flip) % 2
    listed = pltpu.make_async_copy(chosen_ref, list_ref, sems.at[PARTS])
    listed.start()
    copies = []
    for p in range(PARTS):
        at = pl.multiple_of(side * half + p * wide, 128)
        copies.append(
            pltpu.make_async_copy(
                dec_ref.at[:, pl.ds(at, wide)], buf_ref.at[:, pl.ds(p * wide, wide)], sems.at[p]
            )
        )
    for copy in copies:
        copy.start()
    listed.wait()
    offset = list_ref[...] - feat * feats
    down = jnp.broadcast_to(offset, (k, k)).T
    lane = lax.broadcasted_iota(jnp.int32, (k, k), 1)
    for j in range(feats // k):
        hot_ref[:, j * k : (j + 1) * k] = (down == lane + j * k).astype(F32).astype(BF)
    for p in range(PARTS):
        cols = slice(p * wide, (p + 1) * wide)
        copies[p].wait()
        out_ref[:, cols] = jnp.dot(hot_ref[...], buf_ref[:, cols], preferred_element_type=F32).astype(BF)


def pick(chosen, dec, flip):
    feats, width = dec.shape
    k, half = chosen.shape[1], width // 2
    return pl.pallas_call(
        lambda *refs: pick_kernel(flip, *refs),
        in_specs=[pl.BlockSpec(memory_space=pltpu.HBM)] * 2,
        out_specs=pl.BlockSpec(memory_space=pltpu.VMEM),
        out_shape=jax.ShapeDtypeStruct((k, half), BF),
        scratch_shapes=[
            pltpu.VMEM((k, feats), BF),
            pltpu.VMEM((feats, half), BF),
            pltpu.VMEM((1, k), jnp.int32),
            pltpu.SemaphoreType.DMA((PARTS + 1,)),
        ],
        compiler_params=pltpu.CompilerParams(vmem_limit_bytes=8 * MIB),
        cost_estimate=pl.CostEstimate(flops=2 * k * feats * half, bytes_accessed=2 * feats * half, transcendentals=0),
        name=f"pick{flip}",
    )(chosen, dec)


def fetch_kernel(enc_ref, out_ref, sem):
    copy = pltpu.make_async_copy(enc_ref, out_ref, sem)
    copy.start()
    copy.wait()


def fetch(enc):
    return pl.pallas_call(
        fetch_kernel,
        in_specs=[pl.BlockSpec(memory_space=pltpu.HBM)],
        out_specs=pl.BlockSpec(memory_space=pltpu.VMEM),
        out_shape=jax.ShapeDtypeStruct(enc.shape, enc.dtype),
        scratch_shapes=[pltpu.SemaphoreType.DMA],
        compiler_params=pltpu.CompilerParams(vmem_limit_bytes=8 * MIB),
        cost_estimate=pl.CostEstimate(flops=0, bytes_accessed=4 * enc.size, transcendentals=0),
        name="fetch",
    )(enc)


def product_kernel(flip, *refs):
    left_ref, enc_ref = refs[:2]
    out_ref = refs[-1]
    half = left_ref.shape[1]
    side = (lax.axis_index("feat") + flip) % 2
    at = pl.multiple_of(side * half, 128)
    tile = 256
    for j in range(out_ref.shape[1] // tile):
        cols = slice(j * tile, (j + 1) * tile)
        part = jnp.dot(left_ref[...], enc_ref[pl.ds(at, half), cols], preferred_element_type=F32)
        if flip:
            part = part + refs[2][:, cols]
        out_ref[:, cols] = part.astype(out_ref.dtype)


def product(left, enc, flip, *more):
    k, half = left.shape
    n = enc.shape[1]
    return pl.pallas_call(
        lambda *refs: product_kernel(flip, *refs),
        in_specs=[pl.BlockSpec(memory_space=pltpu.VMEM)] * (2 + len(more)),
        out_specs=pl.BlockSpec(memory_space=pltpu.VMEM),
        out_shape=jax.ShapeDtypeStruct((k, n), BF if flip else F32),
        compiler_params=pltpu.CompilerParams(vmem_limit_bytes=16 * MIB),
        cost_estimate=pl.CostEstimate(flops=2 * k * n * half, bytes_accessed=2 * half * n, transcendentals=0),
        name=f"product{flip}",
    )(left, enc, *more)


def local(encoder, decoder, chosen):
    enc = pltpu.with_memory_space_constraint(encoder[0], pltpu.HBM)
    dec = pltpu.with_memory_space_constraint(decoder[0], pltpu.HBM)
    k = chosen.shape[0]
    chosen = pltpu.with_memory_space_constraint(chosen.reshape(1, k), pltpu.HBM)
    rows = k // 4
    feat, layer = lax.axis_index("feat"), lax.axis_index("layer")
    x = feat // 2
    y, z = layer // 8, layer % 8

    def feat_step(v, move):
        return lax.ppermute(v, "feat", [(i, move(i)) for i in range(8)])

    def along_x(v, d):
        return feat_step(v, lambda i: (i + 2 * d) % 8)

    def along_z(v, move):
        return lax.ppermute(v, "layer", [(i, i // 8 * 8 + move(i % 8) % 8) for i in range(32)])

    def along_y(v, d):
        return lax.ppermute(v, "layer", [(i, (i + 8 * d) % 32) for i in range(32)])

    away = feat_step(pick(chosen, dec, 1), lambda i: i ^ 1)
    mine = pick(chosen, dec, 0) + away

    def chunk(d):
        return lax.dynamic_slice_in_dim(mine, rows * ((x + d) % 4), rows, 0)

    got = [along_x(chunk(d), d) for d in (2, 1, 3)]
    total = chunk(0).astype(F32)
    for g in got:
        total = total + g.astype(F32)

    near = fetch(enc)

    before = jnp.zeros_like(total)

    def join(arrivals, before, total):
        for lower, v in arrivals:
            v = v.astype(F32)
            before = before + jnp.where(lower, v, 0.0)
            total = total + v
        return before, total

    before, total = join([(z % 2 == 1, along_z(total.astype(BF), lambda i: i ^ 1))], before, total)
    low = total.astype(BF)
    across = along_z(low, lambda i: i + 3 if i % 2 else i - 3)
    up = along_z(low, lambda i: i + 2)
    down = along_z(low, lambda i: i - 2)
    before, total = join([(z >= 4, across), (z >= 2, up), (z >= 6, down)], before, total)
    low = total.astype(BF)
    arrivals = [(y >= d, along_y(low, d)) for d in (2, 1, 3)]
    before, total = join(arrivals, before, total)
    prefix, near = lax.optimization_barrier((before.astype(BF), near))

    whole = jnp.zeros((k, prefix.shape[1]), BF)
    for d in (0, 2, 1, 3):
        piece = along_x(prefix, d) if d else prefix
        whole = lax.dynamic_update_slice_in_dim(whole, piece, rows * ((x + 4 - d) % 4), 0)
    other = feat_step(whole, lambda i: i ^ 1)
    result = product(other, near, 1, product(whole, near, 0))
    return result[None]


def solution(mesh):
    placed = (P("layer", None, "feat"), P("layer", "feat", None), P())
    return jax.shard_map(
        local, mesh=mesh, in_specs=placed, out_specs=P("layer", None, "feat"), check_vma=False
    )
```

time: 62.2 us -> 56.6 us (0.910)
  matrix products: 9.51 us -> 0 us
  Pallas kernels: 0 us -> 8.27 us
  waiting for transfers between devices: 19.6 us -> 12.5 us
  local copies, waits for them, and re-layouts: 0.1 us -> 4.57 us
  starting transfers between devices: 31.8 us -> 30.7 us
    dot_general x4 -> x0, matrix products: 9.51 us -> none  [the longest x2 5.08 us: product(): return jnp.dot(v, part, preferred_element_type=F32)]
    pallas_call x0 -> x5, Pallas kernels: none -> 8.27 us  [the longest x2 4.18 us: pick(): pl.pallas_call(lambda *refs: pick_kernel(flip, *refs), in_specs=[pl.Block...]
    ppermute x6 -> x7, waiting for transfers between devices: 10.3 us -> 5.29 us  [the longest x4 5.28 us: along_z(): lax.ppermute(v, 'layer', [(i, i // 8 * 8 + move(i % 8) % 8) for i in rang...]
    unnamed x0 -> x4, local copies, waits for them, and re-layouts: none -> 4.45 us
    ppermute x8, waiting for transfers between devices: 9.26 us -> 7.2 us  [feat_step(): return lax.ppermute(v, 'feat', [(i, move(i)) for i in range(8)])]
    ppermute x8, starting transfers between devices: 17.8 us -> 15.8 us  [feat_step(): return lax.ppermute(v, 'feat', [(i, move(i)) for i in range(8)])]
    ppermute x6 -> x7, starting transfers between devices: 13.9 us -> 14.8 us  [the longest x4 10.4 us: along_z(): lax.ppermute(v, 'layer', [(i, i // 8 * 8 + move(i % 8) % 8) for i in rang...]
    sub x1 -> x0, other arithmetic: 0.66 us -> none  [local(): offset = chosen - feat * feats]
  transfers between devices with their start and end apart: 14 -> 15, of which waited for: 11 -> 6; matrix products, arithmetic and copies ran while one was open for 0% -> 0% of each run, Pallas kernels for 0% -> 9%
where the time goes in v2:
time: 56.6 us; the launch traced here: 56.4 us
  starting transfers between devices  30.7 us (54%)
  waiting for transfers between devices  12.5 us (22%)
  Pallas kernels  8.27 us (15%)
  local copies, waits for them, and re-layouts  4.57 us (8%)
    ppermute x8, starting transfers between devices, feat_step(): return lax.ppermute(v, 'feat', [(i, move(i)) for i in range(8)])  15.8 us
    ppermute x4, starting transfers between devices, along_z(): lax.ppermute(v, 'layer', [(i, i // 8 * 8 + move(i % 8) % 8) for i in rang...  10.4 us
    ppermute x8, waiting for transfers between devices, feat_step(): return lax.ppermute(v, 'feat', [(i, move(i)) for i in range(8)])  7.2 us
    ppermute x4, waiting for transfers between devices, along_z(): lax.ppermute(v, 'layer', [(i, i // 8 * 8 + move(i % 8) % 8) for i in rang...  5.28 us
    ppermute x3, starting transfers between devices, along_y(): return lax.ppermute(v, 'layer', [(i, (i + 8 * d) % 32) for i in range(32)])  4.45 us
    unnamed x4, local copies, waits for them, and re-layouts  4.45 us
    pallas_call x2, Pallas kernels, pick(): pl.pallas_call(lambda *refs: pick_kernel(flip, *refs), in_specs=[pl.Block...  4.18 us
    pallas_call x1, Pallas kernels, fetch(): pl.pallas_call(fetch_kernel, in_specs=[pl.BlockSpec(memory_space=pltpu.HB...  2.34 us
  transfers between devices with their start and end apart: 15, of which 6 were waited for; matrix products, arithmetic and copies ran while one was open for 0% of the time, Pallas kernels for 9%

profile of v2, /device:TPU:1, one launch (start us, length us, event | category | flops | bytes accessed | tf_op | source)
XLA Modules:
  0.0 56.4 jit_solution(17664008854744029827)
XLA Ops:
  0.0 2.1 %pick1.1 = bf16[128,1152]{1,0:T(8,128)(2,1)S(1)} custom-call(s32[1,128]{1,0:T(1,128)} %bitcast.7, bf16[1024,2304]{1,0:T(8,128)(2,1)} %bitcast.4), custom_call_target="tpu_custom_call" | custom-call | flops 301989888 | bytes 2359296 | tf_op jit(solution)/shard_map/pick1/pallas_call | solution.py:47
  2.1 3.3 %collective-permute-start = (bf16[128,1152]{1,0:T(8,128)(2,1)S(1)}, bf16[128,1152]{1,0:T(8,128)(2,1)S(1)}, u32[]{:S(2)}, u32[]{:S(2)}) collective-permute-start(bf16[128,1152]{1,0:T(8,128)(2,1)S(1)} %pick1.1), channel_id=1, source_target_pairs={{0,1},{1,0},{2,3},{3,2},{4,5},{5,4},{6,7},{7,6},{8,9},{9,8},{10,11... | collective-permute-start | bytes 884744 | tf_op jit(solution)/shard_map/ppermute | solution.py:123
  5.4 2.1 %pick0.1 = bf16[128,1152]{1,0:T(8,128)(2,1)S(1)} custom-call(s32[1,128]{1,0:T(1,128)} %bitcast.8, bf16[1024,2304]{1,0:T(8,128)(2,1)} %bitcast.5), custom_call_target="tpu_custom_call" | custom-call | flops 301989888 | bytes 2359296 | tf_op jit(solution)/shard_map/pick0/pallas_call | solution.py:47
  7.5 0.0 collective-permute-done
  7.5 0.1 add.113
  7.7 1.1 %collective-permute-start.1 = (bf16[32,1152]{1,0:T(8,128)(2,1)S(1)}, bf16[32,1152]{1,0:T(8,128)(2,1)S(1)}, u32[]{:S(2)}, u32[]{:S(2)}) collective-permute-start(bf16[32,1152]{1,0:T(8,128)(2,1)S(1)} %get-tuple-element.11), channel_id=1, source_target_pairs={{0,4},{1,5},{2,6},{3,7},{4,0},{5,1},{6,2},{7,3},{8,12},{9,13},{10,... | collective-permute-start | bytes 221192 | tf_op jit(solution)/shard_map/ppermute | solution.py:123
  8.8 0.9 %collective-permute-start.3 = (bf16[32,1152]{1,0:T(8,128)(2,1)S(1)}, bf16[32,1152]{1,0:T(8,128)(2,1)S(1)}, u32[]{:S(2)}, u32[]{:S(2)}) collective-permute-start(bf16[32,1152]{1,0:T(8,128)(2,1)S(1)} %get-tuple-element.12), channel_id=1, source_target_pairs={{0,6},{1,7},{2,0},{3,1},{4,2},{5,3},{6,4},{7,5},{8,14},{9,15},{10,... | collective-permute-start | bytes 221192 | tf_op jit(solution)/shard_map/ppermute | solution.py:123
  9.6 0.6 %collective-permute-start.2 = (bf16[32,1152]{1,0:T(8,128)(2,1)S(1)}, bf16[32,1152]{1,0:T(8,128)(2,1)S(1)}, u32[]{:S(2)}, u32[]{:S(2)}) collective-permute-start(bf16[32,1152]{1,0:T(8,128)(2,1)S(1)} %get-tuple-element.13), channel_id=1, source_target_pairs={{0,2},{1,3},{2,4},{3,5},{4,6},{5,7},{6,0},{7,1},{8,10},{9,11},{10,... | collective-permute-start | bytes 221192 | tf_op jit(solution)/shard_map/ppermute | solution.py:123
  10.2 2.8 %collective-permute-done.1 = bf16[32,1152]{1,0:T(8,128)(2,1)S(1)} collective-permute-done((bf16[32,1152]{1,0:T(8,128)(2,1)S(1)}, bf16[32,1152]{1,0:T(8,128)(2,1)S(1)}, u32[]{:S(2)}, u32[]{:S(2)}) %collective-permute-start.1) | collective-permute-done | bytes 73760 | tf_op jit(solution)/shard_map/ppermute | solution.py:123
  13.1 0.0 collective-permute-done.3
  13.1 1.0 %collective-permute-done.2 = bf16[32,1152]{1,0:T(8,128)(2,1)S(1)} collective-permute-done((bf16[32,1152]{1,0:T(8,128)(2,1)S(1)}, bf16[32,1152]{1,0:T(8,128)(2,1)S(1)}, u32[]{:S(2)}, u32[]{:S(2)}) %collective-permute-start.2) | collective-permute-done | bytes 73760 | tf_op jit(solution)/shard_map/ppermute | solution.py:123
  14.2 1.7 %collective-permute-start.4 = (bf16[32,1152]{1,0:T(8,128)(2,1)S(1)}, bf16[32,1152]{1,0:T(8,128)(2,1)S(1)}, u32[]{:S(2)}, u32[]{:S(2)}) collective-permute-start(bf16[32,1152]{1,0:T(8,128)(2,1)S(1)} %get-tuple-element.9), channel_id=1, source_target_pairs={{0,8},{8,0},{16,24},{24,16},{32,40},{40,32},{48,56},{56,48},{64,72... | collective-permute-start | bytes 221192 | tf_op jit(solution)/shard_map/ppermute | solution.py:129
  15.8 1.7 %collective-permute-done.4 = bf16[32,1152]{1,0:T(8,128)(2,1)S(1)} collective-permute-done((bf16[32,1152]{1,0:T(8,128)(2,1)S(1)}, bf16[32,1152]{1,0:T(8,128)(2,1)S(1)}, u32[]{:S(2)}, u32[]{:S(2)}) %collective-permute-start.4) | collective-permute-done | bytes 73760 | tf_op jit(solution)/shard_map/ppermute | solution.py:129
  17.6 5.9 %collective-permute-start.7 = (bf16[32,1152]{1,0:T(8,128)(2,1)S(1)}, bf16[32,1152]{1,0:T(8,128)(2,1)S(1)}, u32[]{:S(2)}, u32[]{:S(2)}) collective-permute-start(bf16[32,1152]{1,0:T(8,128)(2,1)S(1)} %fusion.8), channel_id=1, source_target_pairs={{0,48},{8,56},{16,0},{24,8},{32,16},{40,24},{48,32},{56,40},{64,11... | collective-permute-start | bytes 221192 | tf_op jit(solution)/shard_map/ppermute | solution.py:129
  23.5 0.0 collective-permute-start.6
  23.5 2.8 %collective-permute-start.5 = (bf16[32,1152]{1,0:T(8,128)(2,1)S(1)}, bf16[32,1152]{1,0:T(8,128)(2,1)S(1)}, u32[]{:S(2)}, u32[]{:S(2)}) collective-permute-start(bf16[32,1152]{1,0:T(8,128)(2,1)S(1)} %fusion.8), channel_id=1, source_target_pairs={{0,40},{8,32},{16,56},{24,48},{32,8},{40,0},{48,24},{56,16},{64,10... | collective-permute-start | bytes 221192 | tf_op jit(solution)/shard_map/ppermute | solution.py:129
  26.3 0.0 collective-permute-done.7
  26.3 3.5 %collective-permute-done.6 = bf16[32,1152]{1,0:T(8,128)(2,1)S(1)} collective-permute-done((bf16[32,1152]{1,0:T(8,128)(2,1)S(1)}, bf16[32,1152]{1,0:T(8,128)(2,1)S(1)}, u32[]{:S(2)}, u32[]{:S(2)}) %collective-permute-start.6) | collective-permute-done | bytes 73760 | tf_op jit(solution)/shard_map/ppermute | solution.py:129
  29.8 0.0 collective-permute-done.5
  29.8 0.1 fusion.7
  29.9 2.8 %collective-permute-start.10 = (bf16[32,1152]{1,0:T(8,128)(2,1)S(1)}, bf16[32,1152]{1,0:T(8,128)(2,1)S(1)}, u32[]{:S(2)}, u32[]{:S(2)}) collective-permute-start(bf16[32,1152]{1,0:T(8,128)(2,1)S(1)} %fusion.7), channel_id=1, source_target_pairs={{0,192},{8,200},{16,208},{24,216},{32,224},{40,232},{48,240},{56,2... | collective-permute-start | bytes 221192 | tf_op jit(solution)/shard_map/ppermute | solution.py:132
  32.7 0.0 collective-permute-start.9
  32.7 1.6 %collective-permute-start.8 = (bf16[32,1152]{1,0:T(8,128)(2,1)S(1)}, bf16[32,1152]{1,0:T(8,128)(2,1)S(1)}, u32[]{:S(2)}, u32[]{:S(2)}) collective-permute-start(bf16[32,1152]{1,0:T(8,128)(2,1)S(1)} %fusion.7), channel_id=1, source_target_pairs={{0,128},{8,136},{16,144},{24,152},{32,160},{40,168},{48,176},{56,1... | collective-permute-start | bytes 221192 | tf_op jit(solution)/shard_map/ppermute | solution.py:132
  34.4 2.3 %fetch.1.refs_1_ = bf16[2304,1024]{1,0:T(8,128)(2,1)S(1)} custom-call(bf16[2304,1024]{1,0:T(8,128)(2,1)} %bitcast.6), custom_call_target="tpu_custom_call" | custom-call | bytes 9437184 | tf_op jit(solution)/shard_map/fetch/pallas_call | solution.py:71
  36.7 0.0 copy-start
  36.7 2.1 %copy-done = bf16[2304,1024]{1,0:T(8,128)(2,1)} copy-done((bf16[2304,1024]{1,0:T(8,128)(2,1)}, bf16[2304,1024]{1,0:T(8,128)(2,1)S(1)}, u32[]{:S(2)}) %copy-start) | copy-done | bytes 4718616
  38.8 0.0 collective-permute-done.10
  38.8 0.0 collective-permute-done.9
  38.8 0.0 collective-permute-done.8
  38.8 0.1 fusion.6
  39.0 2.2 %collective-permute-start.13 = (bf16[32,1152]{1,0:T(8,128)(2,1)S(1)}, bf16[32,1152]{1,0:T(8,128)(2,1)S(1)}, u32[]{:S(2)}, u32[]{:S(2)}) collective-permute-start(bf16[32,1152]{1,0:T(8,128)(2,1)S(1)} %fusion.6), channel_id=1, source_target_pairs={{0,6},{1,7},{2,0},{3,1},{4,2},{5,3},{6,4},{7,5},{8,14},{9,15},{10,... | collective-permute-start | bytes 221192 | tf_op jit(solution)/shard_map/ppermute | solution.py:123
  41.2 0.0 collective-permute-start.12
  41.2 1.8 %collective-permute-start.11 = (bf16[32,1152]{1,0:T(8,128)(2,1)S(1)}, bf16[32,1152]{1,0:T(8,128)(2,1)S(1)}, u32[]{:S(2)}, u32[]{:S(2)}) collective-permute-start(bf16[32,1152]{1,0:T(8,128)(2,1)S(1)} %fusion.6), channel_id=1, source_target_pairs={{0,4},{1,5},{2,6},{3,7},{4,0},{5,1},{6,2},{7,3},{8,12},{9,13},{10,... | collective-permute-start | bytes 221192 | tf_op jit(solution)/shard_map/ppermute | solution.py:123
  43.0 2.9 %collective-permute-done.11 = bf16[32,1152]{1,0:T(8,128)(2,1)S(1)} collective-permute-done((bf16[32,1152]{1,0:T(8,128)(2,1)S(1)}, bf16[32,1152]{1,0:T(8,128)(2,1)S(1)}, u32[]{:S(2)}, u32[]{:S(2)}) %collective-permute-start.11) | collective-permute-done | bytes 73760 | tf_op jit(solution)/shard_map/ppermute | solution.py:123
  46.0 0.4 collective-permute-done.12
  46.4 0.0 collective-permute-done.13
  46.4 5.9 %collective-permute-start.14 = (bf16[128,1152]{1,0:T(8,128)(2,1)S(1)}, bf16[128,1152]{1,0:T(8,128)(2,1)S(1)}, u32[]{:S(2)}, u32[]{:S(2)}) collective-permute-start(bf16[128,1152]{1,0:T(8,128)(2,1)S(1)} %constant_dynamic-update-slice_fusion.refs_0_), channel_id=1, source_target_pairs={{0,1},{1,0},{2,3},{3,2},{4,5},{5,4},{6,7},{7,6},{8,9},{9,8},{10,11... | collective-permute-start | bytes 884744 | tf_op jit(solution)/shard_map/ppermute | solution.py:123
  52.3 0.0 copy-start.1
  52.3 2.3 %copy-done.1 = bf16[2304,1024]{1,0:T(8,128)(2,1)S(1)} copy-done((bf16[2304,1024]{1,0:T(8,128)(2,1)S(1)}, bf16[2304,1024]{1,0:T(8,128)(2,1)}, u32[]{:S(2)}) %copy-start.1) | copy-done | bytes 4718616
  54.7 0.5 product0.1.refs_2_
  55.2 0.0 collective-permute-done.14.refs_0_
  55.2 1.2 %product1.1 = bf16[128,1024]{1,0:T(8,128)(2,1)} custom-call(bf16[128,1152]{1,0:T(8,128)(2,1)S(1)} %collective-permute-done.14.refs_0_, bf16[2304,1024]{1,0:T(8,128)(2,1)S(1)} %copy-done.1, f32[128,1024]{1,0:T(8,128)S(1)} %product0.1.refs_2_), custom_call_target="tpu_custom_call" | custom-call | flops 301989888 | bytes 2359296 | tf_op jit(solution)/shard_map/product1/pallas_call | solution.py:101
  (8 shorter events, 0.2 us)
Async XLA Ops:
  2.1 5.4 %collective-permute-start = (bf16[128,1152]{1,0:T(8,128)(2,1)S(1)}, bf16[128,1152]{1,0:T(8,128)(2,1)S(1)}, u32[]{:S(2)}, u32[]{:S(2)}) collective-permute-start(bf16[128,1152]{1,0:T(8,128)(2,1)S(1)} %pick1.1), channel_id=1, source_target_pairs={{0,1},{1,0},{2,3},{3,2},{4,5},{5,4},{6,7},{7,6},{8,9},{9,8},{10,11... | collective-permute-start | bytes 884744 | tf_op jit(solution)/shard_map/ppermute | solution.py:123
  7.7 5.4 %collective-permute-start.1 = (bf16[32,1152]{1,0:T(8,128)(2,1)S(1)}, bf16[32,1152]{1,0:T(8,128)(2,1)S(1)}, u32[]{:S(2)}, u32[]{:S(2)}) collective-permute-start(bf16[32,1152]{1,0:T(8,128)(2,1)S(1)} %get-tuple-element.11), channel_id=1, source_target_pairs={{0,4},{1,5},{2,6},{3,7},{4,0},{5,1},{6,2},{7,3},{8,12},{9,13},{10,... | collective-permute-start | bytes 221192 | tf_op jit(solution)/shard_map/ppermute | solution.py:123
  8.8 4.3 %collective-permute-start.3 = (bf16[32,1152]{1,0:T(8,128)(2,1)S(1)}, bf16[32,1152]{1,0:T(8,128)(2,1)S(1)}, u32[]{:S(2)}, u32[]{:S(2)}) collective-permute-start(bf16[32,1152]{1,0:T(8,128)(2,1)S(1)} %get-tuple-element.12), channel_id=1, source_target_pairs={{0,6},{1,7},{2,0},{3,1},{4,2},{5,3},{6,4},{7,5},{8,14},{9,15},{10,... | collective-permute-start | bytes 221192 | tf_op jit(solution)/shard_map/ppermute | solution.py:123
  9.6 4.5 %collective-permute-start.2 = (bf16[32,1152]{1,0:T(8,128)(2,1)S(1)}, bf16[32,1152]{1,0:T(8,128)(2,1)S(1)}, u32[]{:S(2)}, u32[]{:S(2)}) collective-permute-start(bf16[32,1152]{1,0:T(8,128)(2,1)S(1)} %get-tuple-element.13), channel_id=1, source_target_pairs={{0,2},{1,3},{2,4},{3,5},{4,6},{5,7},{6,0},{7,1},{8,10},{9,11},{10,... | collective-permute-start | bytes 221192 | tf_op jit(solution)/shard_map/ppermute | solution.py:123
  14.2 3.4 %collective-permute-start.4 = (bf16[32,1152]{1,0:T(8,128)(2,1)S(1)}, bf16[32,1152]{1,0:T(8,128)(2,1)S(1)}, u32[]{:S(2)}, u32[]{:S(2)}) collective-permute-start(bf16[32,1152]{1,0:T(8,128)(2,1)S(1)} %get-tuple-element.9), channel_id=1, source_target_pairs={{0,8},{8,0},{16,24},{24,16},{32,40},{40,32},{48,56},{56,48},{64,72... | collective-permute-start | bytes 221192 | tf_op jit(solution)/shard_map/ppermute | solution.py:129
  17.6 8.7 %collective-permute-start.7 = (bf16[32,1152]{1,0:T(8,128)(2,1)S(1)}, bf16[32,1152]{1,0:T(8,128)(2,1)S(1)}, u32[]{:S(2)}, u32[]{:S(2)}) collective-permute-start(bf16[32,1152]{1,0:T(8,128)(2,1)S(1)} %fusion.8), channel_id=1, source_target_pairs={{0,48},{8,56},{16,0},{24,8},{32,16},{40,24},{48,32},{56,40},{64,11... | collective-permute-start | bytes 221192 | tf_op jit(solution)/shard_map/ppermute | solution.py:129
  23.5 6.3 %collective-permute-start.6 = (bf16[32,1152]{1,0:T(8,128)(2,1)S(1)}, bf16[32,1152]{1,0:T(8,128)(2,1)S(1)}, u32[]{:S(2)}, u32[]{:S(2)}) collective-permute-start(bf16[32,1152]{1,0:T(8,128)(2,1)S(1)} %fusion.8), channel_id=1, source_target_pairs={{0,16},{8,24},{16,32},{24,40},{32,48},{40,56},{48,0},{56,8},{64,80... | collective-permute-start | bytes 221192 | tf_op jit(solution)/shard_map/ppermute | solution.py:129
  23.5 6.3 %collective-permute-start.5 = (bf16[32,1152]{1,0:T(8,128)(2,1)S(1)}, bf16[32,1152]{1,0:T(8,128)(2,1)S(1)}, u32[]{:S(2)}, u32[]{:S(2)}) collective-permute-start(bf16[32,1152]{1,0:T(8,128)(2,1)S(1)} %fusion.8), channel_id=1, source_target_pairs={{0,40},{8,32},{16,56},{24,48},{32,8},{40,0},{48,24},{56,16},{64,10... | collective-permute-start | bytes 221192 | tf_op jit(solution)/shard_map/ppermute | solution.py:129
  29.9 8.9 %collective-permute-start.10 = (bf16[32,1152]{1,0:T(8,128)(2,1)S(1)}, bf16[32,1152]{1,0:T(8,128)(2,1)S(1)}, u32[]{:S(2)}, u32[]{:S(2)}) collective-permute-start(bf16[32,1152]{1,0:T(8,128)(2,1)S(1)} %fusion.7), channel_id=1, source_target_pairs={{0,192},{8,200},{16,208},{24,216},{32,224},{40,232},{48,240},{56,2... | collective-permute-start | bytes 221192 | tf_op jit(solution)/shard_map/ppermute | solution.py:132
  32.7 6.1 %collective-permute-start.9 = (bf16[32,1152]{1,0:T(8,128)(2,1)S(1)}, bf16[32,1152]{1,0:T(8,128)(2,1)S(1)}, u32[]{:S(2)}, u32[]{:S(2)}) collective-permute-start(bf16[32,1152]{1,0:T(8,128)(2,1)S(1)} %fusion.7), channel_id=1, source_target_pairs={{0,64},{8,72},{16,80},{24,88},{32,96},{40,104},{48,112},{56,120},{... | collective-permute-start | bytes 221192 | tf_op jit(solution)/shard_map/ppermute | solution.py:132
  32.7 6.1 %collective-permute-start.8 = (bf16[32,1152]{1,0:T(8,128)(2,1)S(1)}, bf16[32,1152]{1,0:T(8,128)(2,1)S(1)}, u32[]{:S(2)}, u32[]{:S(2)}) collective-permute-start(bf16[32,1152]{1,0:T(8,128)(2,1)S(1)} %fusion.7), channel_id=1, source_target_pairs={{0,128},{8,136},{16,144},{24,152},{32,160},{40,168},{48,176},{56,1... | collective-permute-start | bytes 221192 | tf_op jit(solution)/shard_map/ppermute | solution.py:132
  36.7 2.1 %copy-start = (bf16[2304,1024]{1,0:T(8,128)(2,1)}, bf16[2304,1024]{1,0:T(8,128)(2,1)S(1)}, u32[]{:S(2)}) copy-start(bf16[2304,1024]{1,0:T(8,128)(2,1)S(1)} %fetch.1.refs_1_) | copy-start | bytes 14155780
  39.0 7.4 %collective-permute-start.13 = (bf16[32,1152]{1,0:T(8,128)(2,1)S(1)}, bf16[32,1152]{1,0:T(8,128)(2,1)S(1)}, u32[]{:S(2)}, u32[]{:S(2)}) collective-permute-start(bf16[32,1152]{1,0:T(8,128)(2,1)S(1)} %fusion.6), channel_id=1, source_target_pairs={{0,6},{1,7},{2,0},{3,1},{4,2},{5,3},{6,4},{7,5},{8,14},{9,15},{10,... | collective-permute-start | bytes 221192 | tf_op jit(solution)/shard_map/ppermute | solution.py:123
  41.2 5.2 %collective-permute-start.12 = (bf16[32,1152]{1,0:T(8,128)(2,1)S(1)}, bf16[32,1152]{1,0:T(8,128)(2,1)S(1)}, u32[]{:S(2)}, u32[]{:S(2)}) collective-permute-start(bf16[32,1152]{1,0:T(8,128)(2,1)S(1)} %fusion.6), channel_id=1, source_target_pairs={{0,2},{1,3},{2,4},{3,5},{4,6},{5,7},{6,0},{7,1},{8,10},{9,11},{10,... | collective-permute-start | bytes 221192 | tf_op jit(solution)/shard_map/ppermute | solution.py:123
  41.2 4.8 %collective-permute-start.11 = (bf16[32,1152]{1,0:T(8,128)(2,1)S(1)}, bf16[32,1152]{1,0:T(8,128)(2,1)S(1)}, u32[]{:S(2)}, u32[]{:S(2)}) collective-permute-start(bf16[32,1152]{1,0:T(8,128)(2,1)S(1)} %fusion.6), channel_id=1, source_target_pairs={{0,4},{1,5},{2,6},{3,7},{4,0},{5,1},{6,2},{7,3},{8,12},{9,13},{10,... | collective-permute-start | bytes 221192 | tf_op jit(solution)/shard_map/ppermute | solution.py:123
  46.4 8.8 %collective-permute-start.14 = (bf16[128,1152]{1,0:T(8,128)(2,1)S(1)}, bf16[128,1152]{1,0:T(8,128)(2,1)S(1)}, u32[]{:S(2)}, u32[]{:S(2)}) collective-permute-start(bf16[128,1152]{1,0:T(8,128)(2,1)S(1)} %constant_dynamic-update-slice_fusion.refs_0_), channel_id=1, source_target_pairs={{0,1},{1,0},{2,3},{3,2},{4,5},{5,4},{6,7},{7,6},{8,9},{9,8},{10,11... | collective-permute-start | bytes 884744 | tf_op jit(solution)/shard_map/ppermute | solution.py:123
  52.3 2.3 %copy-start.1 = (bf16[2304,1024]{1,0:T(8,128)(2,1)S(1)}, bf16[2304,1024]{1,0:T(8,128)(2,1)}, u32[]{:S(2)}) copy-start(bf16[2304,1024]{1,0:T(8,128)(2,1)} %copy-done) | copy-start | bytes 14155780

commit v3 on v2

--- a/solution.py
+++ b/solution.py
@@ -61,23 +61,24 @@
     )(chosen, dec)
 
 
-def fetch_kernel(enc_ref, out_ref, sem):
+def fetch_kernel(own_ref, enc_ref, out_ref, same_ref, sem):
     copy = pltpu.make_async_copy(enc_ref, out_ref, sem)
     copy.start()
+    same_ref[...] = own_ref[...]
     copy.wait()
 
 
-def fetch(enc):
+def fetch(own, enc):
     return pl.pallas_call(
         fetch_kernel,
-        in_specs=[pl.BlockSpec(memory_space=pltpu.HBM)],
-        out_specs=pl.BlockSpec(memory_space=pltpu.VMEM),
-        out_shape=jax.ShapeDtypeStruct(enc.shape, enc.dtype),
+        in_specs=[pl.BlockSpec(memory_space=pltpu.VMEM), pl.BlockSpec(memory_space=pltpu.HBM)],
+        out_specs=[pl.BlockSpec(memory_space=pltpu.VMEM)] * 2,
+        out_shape=[pltpu.VMEM(enc.shape, enc.dtype), jax.ShapeDtypeStruct(own.shape, own.dtype)],
         scratch_shapes=[pltpu.SemaphoreType.DMA],
         compiler_params=pltpu.CompilerParams(vmem_limit_bytes=8 * MIB),
         cost_estimate=pl.CostEstimate(flops=0, bytes_accessed=4 * enc.size, transcendentals=0),
         name="fetch",
-    )(enc)
+    )(own, enc)
 
 
 def product_kernel(flip, *refs):
@@ -137,12 +138,10 @@
     def chunk(d):
         return lax.dynamic_slice_in_dim(mine, rows * ((x + d) % 4), rows, 0)
 
-    got = [along_x(chunk(d), d) for d in (2, 1, 3)]
+    got = [along_x(chunk(d), d) for d in (1, 3, 2)]
     total = chunk(0).astype(F32)
     for g in got:
         total = total + g.astype(F32)
-
-    near = fetch(enc)
 
     before = jnp.zeros_like(total)
 
@@ -155,18 +154,19 @@
 
     before, total = join([(z % 2 == 1, along_z(total.astype(BF), lambda i: i ^ 1))], before, total)
     low = total.astype(BF)
-    across = along_z(low, lambda i: i + 3 if i % 2 else i - 3)
     up = along_z(low, lambda i: i + 2)
     down = along_z(low, lambda i: i - 2)
+    across = along_z(low, lambda i: i + 3 if i % 2 else i - 3)
     before, total = join([(z >= 4, across), (z >= 2, up), (z >= 6, down)], before, total)
     low = total.astype(BF)
-    arrivals = [(y >= d, along_y(low, d)) for d in (2, 1, 3)]
+    arrivals = [(y >= d, along_y(low, d)) for d in (1, 3, 2)]
     before, total = join(arrivals, before, total)
-    prefix, near = lax.optimization_barrier((before.astype(BF), near))
+    prefix = before.astype(BF)
 
+    pieces = [along_x(prefix, d) for d in (1, 3, 2)]
+    near, prefix = fetch(prefix, enc)
     whole = jnp.zeros((k, prefix.shape[1]), BF)
-    for d in (0, 2, 1, 3):
-        piece = along_x(prefix, d) if d else prefix
+    for d, piece in zip((0, 1, 3, 2), [prefix] + pieces):
         whole = lax.dynamic_update_slice_in_dim(whole, piece, rows * ((x + 4 - d) % 4), 0)
     other = feat_step(whole, lambda i: i ^ 1)
     result = product(other, near, 1, product(whole, near, 0))

time: 56.6 us -> 55.4 us (0.979)
  local copies, waits for them, and re-layouts: 4.57 us -> 0.13 us
  waiting for transfers between devices: 12.5 us -> 15.7 us
    unnamed x4 -> x0, local copies, waits for them, and re-layouts: 4.45 us -> none
    ppermute x3, waiting for transfers between devices: 0.01 us -> 4.02 us  [along_y(): return lax.ppermute(v, 'layer', [(i, (i + 8 * d) % 32) for i in range(32)])]
    ppermute x8, starting transfers between devices: 15.8 us -> 17.6 us  [feat_step(): return lax.ppermute(v, 'feat', [(i, move(i)) for i in range(8)])]
    ppermute x4, starting transfers between devices: 10.4 us -> 8.61 us  [along_z(): lax.ppermute(v, 'layer', [(i, i // 8 * 8 + move(i % 8) % 8) for i in rang...]
    ppermute x8, waiting for transfers between devices: 7.2 us -> 5.58 us  [feat_step(): return lax.ppermute(v, 'feat', [(i, move(i)) for i in range(8)])]
    ppermute x4, waiting for transfers between devices: 5.28 us -> 6.11 us  [along_z(): lax.ppermute(v, 'layer', [(i, i // 8 * 8 + move(i % 8) % 8) for i in rang...]
  transfers between devices with their start and end apart: 15 -> 15, of which waited for: 6 -> 9; matrix products, arithmetic and copies ran while one was open for 0% -> 0% of each run, Pallas kernels for 9% -> 9%
where the time goes in v3:
time: 55.4 us; the launch traced here: 55.2 us
  starting transfers between devices  30.7 us (55%)
  waiting for transfers between devices  15.7 us (28%)
  Pallas kernels  8.26 us (15%)
    ppermute x8, starting transfers between devices, feat_step(): return lax.ppermute(v, 'feat', [(i, move(i)) for i in range(8)])  17.6 us
    ppermute x4, starting transfers between devices, along_z(): lax.ppermute(v, 'layer', [(i, i // 8 * 8 + move(i % 8) % 8) for i in rang...  8.61 us
    ppermute x4, waiting for transfers between devices, along_z(): lax.ppermute(v, 'layer', [(i, i // 8 * 8 + move(i % 8) % 8) for i in rang...  6.11 us
    ppermute x8, waiting for transfers between devices, feat_step(): return lax.ppermute(v, 'feat', [(i, move(i)) for i in range(8)])  5.58 us
    ppermute x3, starting transfers between devices, along_y(): return lax.ppermute(v, 'layer', [(i, (i + 8 * d) % 32) for i in range(32)])  4.47 us
    pallas_call x2, Pallas kernels, pick(): pl.pallas_call(lambda *refs: pick_kernel(flip, *refs), in_specs=[pl.Block...  4.18 us
    ppermute x3, waiting for transfers between devices, along_y(): return lax.ppermute(v, 'layer', [(i, (i + 8 * d) % 32) for i in range(32)])  4.02 us
    pallas_call x1, Pallas kernels, fetch(): pl.pallas_call(fetch_kernel, in_specs=[pl.BlockSpec(memory_space=pltpu.VM...  2.34 us
  transfers between devices with their start and end apart: 15, of which 9 were waited for; matrix products, arithmetic and copies ran while one was open for 0% of the time, Pallas kernels for 9%

profile of v3, /device:TPU:1, one launch (start us, length us, event | category | flops | bytes accessed | tf_op | source)
XLA Modules:
  0.0 55.2 jit_solution(15734399055443053712)
XLA Ops:
  0.0 2.1 %pick1.1 = bf16[128,1152]{1,0:T(8,128)(2,1)S(1)} custom-call(s32[1,128]{1,0:T(1,128)} %bitcast.7, bf16[1024,2304]{1,0:T(8,128)(2,1)} %bitcast.4), custom_call_target="tpu_custom_call" | custom-call | flops 301989888 | bytes 2359296 | tf_op jit(solution)/shard_map/pick1/pallas_call | solution.py:47
  2.1 3.3 %collective-permute-start = (bf16[128,1152]{1,0:T(8,128)(2,1)S(1)}, bf16[128,1152]{1,0:T(8,128)(2,1)S(1)}, u32[]{:S(2)}, u32[]{:S(2)}) collective-permute-start(bf16[128,1152]{1,0:T(8,128)(2,1)S(1)} %pick1.1), channel_id=1, source_target_pairs={{0,1},{1,0},{2,3},{3,2},{4,5},{5,4},{6,7},{7,6},{8,9},{9,8},{10,11... | collective-permute-start | bytes 884744 | tf_op jit(solution)/shard_map/ppermute | solution.py:124
  5.4 2.1 %pick0.1 = bf16[128,1152]{1,0:T(8,128)(2,1)S(1)} custom-call(s32[1,128]{1,0:T(1,128)} %bitcast.8, bf16[1024,2304]{1,0:T(8,128)(2,1)} %bitcast.5), custom_call_target="tpu_custom_call" | custom-call | flops 301989888 | bytes 2359296 | tf_op jit(solution)/shard_map/pick0/pallas_call | solution.py:47
  7.5 0.0 collective-permute-done
  7.5 0.1 add.113
  7.7 0.1 collective-permute-start.1
  7.7 1.9 %collective-permute-start.3 = (bf16[32,1152]{1,0:T(8,128)(2,1)S(1)}, bf16[32,1152]{1,0:T(8,128)(2,1)S(1)}, u32[]{:S(2)}, u32[]{:S(2)}) collective-permute-start(bf16[32,1152]{1,0:T(8,128)(2,1)S(1)} %get-tuple-element.12), channel_id=1, source_target_pairs={{0,4},{1,5},{2,6},{3,7},{4,0},{5,1},{6,2},{7,3},{8,12},{9,13},{10,... | collective-permute-start | bytes 221192 | tf_op jit(solution)/shard_map/ppermute | solution.py:124
  9.7 1.2 %collective-permute-start.2 = (bf16[32,1152]{1,0:T(8,128)(2,1)S(1)}, bf16[32,1152]{1,0:T(8,128)(2,1)S(1)}, u32[]{:S(2)}, u32[]{:S(2)}) collective-permute-start(bf16[32,1152]{1,0:T(8,128)(2,1)S(1)} %get-tuple-element.13), channel_id=1, source_target_pairs={{0,6},{1,7},{2,0},{3,1},{4,2},{5,3},{6,4},{7,5},{8,14},{9,15},{10,... | collective-permute-start | bytes 221192 | tf_op jit(solution)/shard_map/ppermute | solution.py:124
  10.8 3.6 %collective-permute-done.1 = bf16[32,1152]{1,0:T(8,128)(2,1)S(1)} collective-permute-done((bf16[32,1152]{1,0:T(8,128)(2,1)S(1)}, bf16[32,1152]{1,0:T(8,128)(2,1)S(1)}, u32[]{:S(2)}, u32[]{:S(2)}) %collective-permute-start.1) | collective-permute-done | bytes 73760 | tf_op jit(solution)/shard_map/ppermute | solution.py:124
  14.4 0.0 collective-permute-done.3
  14.4 0.2 collective-permute-done.2
  14.7 0.7 %collective-permute-start.4 = (bf16[32,1152]{1,0:T(8,128)(2,1)S(1)}, bf16[32,1152]{1,0:T(8,128)(2,1)S(1)}, u32[]{:S(2)}, u32[]{:S(2)}) collective-permute-start(bf16[32,1152]{1,0:T(8,128)(2,1)S(1)} %get-tuple-element.9), channel_id=1, source_target_pairs={{0,8},{8,0},{16,24},{24,16},{32,40},{40,32},{48,56},{56,48},{64,72... | collective-permute-start | bytes 221192 | tf_op jit(solution)/shard_map/ppermute | solution.py:130
  15.4 2.6 %collective-permute-done.4 = bf16[32,1152]{1,0:T(8,128)(2,1)S(1)} collective-permute-done((bf16[32,1152]{1,0:T(8,128)(2,1)S(1)}, bf16[32,1152]{1,0:T(8,128)(2,1)S(1)}, u32[]{:S(2)}, u32[]{:S(2)}) %collective-permute-start.4) | collective-permute-done | bytes 73760 | tf_op jit(solution)/shard_map/ppermute | solution.py:130
  18.0 5.1 %collective-permute-start.7 = (bf16[32,1152]{1,0:T(8,128)(2,1)S(1)}, bf16[32,1152]{1,0:T(8,128)(2,1)S(1)}, u32[]{:S(2)}, u32[]{:S(2)}) collective-permute-start(bf16[32,1152]{1,0:T(8,128)(2,1)S(1)} %fusion.8), channel_id=1, source_target_pairs={{0,48},{8,56},{16,0},{24,8},{32,16},{40,24},{48,32},{56,40},{64,11... | collective-permute-start | bytes 221192 | tf_op jit(solution)/shard_map/ppermute | solution.py:130
  23.1 0.0 collective-permute-start.6
  23.1 2.8 %collective-permute-start.5 = (bf16[32,1152]{1,0:T(8,128)(2,1)S(1)}, bf16[32,1152]{1,0:T(8,128)(2,1)S(1)}, u32[]{:S(2)}, u32[]{:S(2)}) collective-permute-start(bf16[32,1152]{1,0:T(8,128)(2,1)S(1)} %fusion.8), channel_id=1, source_target_pairs={{0,40},{8,32},{16,56},{24,48},{32,8},{40,0},{48,24},{56,16},{64,10... | collective-permute-start | bytes 221192 | tf_op jit(solution)/shard_map/ppermute | solution.py:130
  25.9 0.0 collective-permute-done.7
  25.9 3.5 %collective-permute-done.6 = bf16[32,1152]{1,0:T(8,128)(2,1)S(1)} collective-permute-done((bf16[32,1152]{1,0:T(8,128)(2,1)S(1)}, bf16[32,1152]{1,0:T(8,128)(2,1)S(1)}, u32[]{:S(2)}, u32[]{:S(2)}) %collective-permute-start.6) | collective-permute-done | bytes 73760 | tf_op jit(solution)/shard_map/ppermute | solution.py:130
  29.4 0.0 collective-permute-done.5
  29.4 0.1 fusion.7
  29.5 3.0 %collective-permute-start.10 = (bf16[32,1152]{1,0:T(8,128)(2,1)S(1)}, bf16[32,1152]{1,0:T(8,128)(2,1)S(1)}, u32[]{:S(2)}, u32[]{:S(2)}) collective-permute-start(bf16[32,1152]{1,0:T(8,128)(2,1)S(1)} %fusion.7), channel_id=1, source_target_pairs={{0,128},{8,136},{16,144},{24,152},{32,160},{40,168},{48,176},{56,1... | collective-permute-start | bytes 221192 | tf_op jit(solution)/shard_map/ppermute | solution.py:133
  32.5 0.8 %collective-permute-start.9 = (bf16[32,1152]{1,0:T(8,128)(2,1)S(1)}, bf16[32,1152]{1,0:T(8,128)(2,1)S(1)}, u32[]{:S(2)}, u32[]{:S(2)}) collective-permute-start(bf16[32,1152]{1,0:T(8,128)(2,1)S(1)} %fusion.7), channel_id=1, source_target_pairs={{0,192},{8,200},{16,208},{24,216},{32,224},{40,232},{48,240},{56,2... | collective-permute-start | bytes 221192 | tf_op jit(solution)/shard_map/ppermute | solution.py:133
  33.2 0.7 %collective-permute-start.8 = (bf16[32,1152]{1,0:T(8,128)(2,1)S(1)}, bf16[32,1152]{1,0:T(8,128)(2,1)S(1)}, u32[]{:S(2)}, u32[]{:S(2)}) collective-permute-start(bf16[32,1152]{1,0:T(8,128)(2,1)S(1)} %fusion.7), channel_id=1, source_target_pairs={{0,64},{8,72},{16,80},{24,88},{32,96},{40,104},{48,112},{56,120},{... | collective-permute-start | bytes 221192 | tf_op jit(solution)/shard_map/ppermute | solution.py:133
  33.9 0.3 collective-permute-done.10
  34.3 1.4 %collective-permute-done.9 = bf16[32,1152]{1,0:T(8,128)(2,1)S(1)} collective-permute-done((bf16[32,1152]{1,0:T(8,128)(2,1)S(1)}, bf16[32,1152]{1,0:T(8,128)(2,1)S(1)}, u32[]{:S(2)}, u32[]{:S(2)}) %collective-permute-start.9) | collective-permute-done | bytes 73760 | tf_op jit(solution)/shard_map/ppermute | solution.py:133
  35.7 2.3 %collective-permute-done.8 = bf16[32,1152]{1,0:T(8,128)(2,1)S(1)} collective-permute-done((bf16[32,1152]{1,0:T(8,128)(2,1)S(1)}, bf16[32,1152]{1,0:T(8,128)(2,1)S(1)}, u32[]{:S(2)}, u32[]{:S(2)}) %collective-permute-start.8) | collective-permute-done | bytes 73760 | tf_op jit(solution)/shard_map/ppermute | solution.py:133
  38.0 0.1 fusion.6.own_ref
  38.1 1.7 %collective-permute-start.13 = (bf16[32,1152]{1,0:T(8,128)(2,1)S(1)}, bf16[32,1152]{1,0:T(8,128)(2,1)S(1)}, u32[]{:S(2)}, u32[]{:S(2)}) collective-permute-start(bf16[32,1152]{1,0:T(8,128)(2,1)S(1)} %fusion.6.own_ref), channel_id=1, source_target_pairs={{0,4},{1,5},{2,6},{3,7},{4,0},{5,1},{6,2},{7,3},{8,12},{9,13},{10,... | collective-permute-start | bytes 221192 | tf_op jit(solution)/shard_map/ppermute | solution.py:124
  39.7 0.6 %collective-permute-start.12 = (bf16[32,1152]{1,0:T(8,128)(2,1)S(1)}, bf16[32,1152]{1,0:T(8,128)(2,1)S(1)}, u32[]{:S(2)}, u32[]{:S(2)}) collective-permute-start(bf16[32,1152]{1,0:T(8,128)(2,1)S(1)} %fusion.6.own_ref), channel_id=1, source_target_pairs={{0,6},{1,7},{2,0},{3,1},{4,2},{5,3},{6,4},{7,5},{8,14},{9,15},{10,... | collective-permute-start | bytes 221192 | tf_op jit(solution)/shard_map/ppermute | solution.py:124
  40.3 0.9 %collective-permute-start.11 = (bf16[32,1152]{1,0:T(8,128)(2,1)S(1)}, bf16[32,1152]{1,0:T(8,128)(2,1)S(1)}, u32[]{:S(2)}, u32[]{:S(2)}) collective-permute-start(bf16[32,1152]{1,0:T(8,128)(2,1)S(1)} %fusion.6.own_ref), channel_id=1, source_target_pairs={{0,2},{1,3},{2,4},{3,5},{4,6},{5,7},{6,0},{7,1},{8,10},{9,11},{10,... | collective-permute-start | bytes 221192 | tf_op jit(solution)/shard_map/ppermute | solution.py:124
  41.2 2.3 %fetch.1 = (bf16[2304,1024]{1,0:T(8,128)(2,1)S(1)}, bf16[32,1152]{1,0:T(8,128)(2,1)S(1)}) custom-call(bf16[32,1152]{1,0:T(8,128)(2,1)S(1)} %fusion.6.own_ref, bf16[2304,1024]{1,0:T(8,128)(2,1)} %bitcast.6), custom_call_target="tpu_custom_call" | custom-call | bytes 9437184 | tf_op jit(solution)/shard_map/fetch/pallas_call | solution.py:72
  43.6 1.1 %collective-permute-done.11 = bf16[32,1152]{1,0:T(8,128)(2,1)S(1)} collective-permute-done((bf16[32,1152]{1,0:T(8,128)(2,1)S(1)}, bf16[32,1152]{1,0:T(8,128)(2,1)S(1)}, u32[]{:S(2)}, u32[]{:S(2)}) %collective-permute-start.11) | collective-permute-done | bytes 73760 | tf_op jit(solution)/shard_map/ppermute | solution.py:124
  44.7 0.0 collective-permute-done.12
  44.8 0.0 collective-permute-done.13
  44.8 8.0 %collective-permute-start.14 = (bf16[128,1152]{1,0:T(8,128)(2,1)S(1)}, bf16[128,1152]{1,0:T(8,128)(2,1)S(1)}, u32[]{:S(2)}, u32[]{:S(2)}) collective-permute-start(bf16[128,1152]{1,0:T(8,128)(2,1)S(1)} %constant_dynamic-update-slice_fusion.refs_0_), channel_id=1, source_target_pairs={{0,1},{1,0},{2,3},{3,2},{4,5},{5,4},{6,7},{7,6},{8,9},{9,8},{10,11... | collective-permute-start | bytes 884744 | tf_op jit(solution)/shard_map/ppermute | solution.py:124
  52.8 0.5 product0.1.refs_2_
  53.3 0.7 %collective-permute-done.14.refs_0_ = bf16[128,1152]{1,0:T(8,128)(2,1)S(1)} collective-permute-done((bf16[128,1152]{1,0:T(8,128)(2,1)S(1)}, bf16[128,1152]{1,0:T(8,128)(2,1)S(1)}, u32[]{:S(2)}, u32[]{:S(2)}) %collective-permute-start.14) | collective-permute-done | bytes 294944 | tf_op jit(solution)/shard_map/ppermute | solution.py:124
  54.0 1.2 %product1.1 = bf16[128,1024]{1,0:T(8,128)(2,1)} custom-call(bf16[128,1152]{1,0:T(8,128)(2,1)S(1)} %collective-permute-done.14.refs_0_, bf16[2304,1024]{1,0:T(8,128)(2,1)S(1)} %get-tuple-element.8.refs_1_, f32[128,1024]{1,0:T(8,128)S(1)} %product0.1.refs_2_), custom_call_target="tpu_custom_call" | custom-call | flops 301989888 | bytes 2359296 | tf_op jit(solution)/shard_map/product1/pallas_call | solution.py:102
  (8 shorter events, 0.2 us)
Async XLA Ops:
  2.1 5.4 %collective-permute-start = (bf16[128,1152]{1,0:T(8,128)(2,1)S(1)}, bf16[128,1152]{1,0:T(8,128)(2,1)S(1)}, u32[]{:S(2)}, u32[]{:S(2)}) collective-permute-start(bf16[128,1152]{1,0:T(8,128)(2,1)S(1)} %pick1.1), channel_id=1, source_target_pairs={{0,1},{1,0},{2,3},{3,2},{4,5},{5,4},{6,7},{7,6},{8,9},{9,8},{10,11... | collective-permute-start | bytes 884744 | tf_op jit(solution)/shard_map/ppermute | solution.py:124
  7.7 6.7 %collective-permute-start.1 = (bf16[32,1152]{1,0:T(8,128)(2,1)S(1)}, bf16[32,1152]{1,0:T(8,128)(2,1)S(1)}, u32[]{:S(2)}, u32[]{:S(2)}) collective-permute-start(bf16[32,1152]{1,0:T(8,128)(2,1)S(1)} %get-tuple-element.11), channel_id=1, source_target_pairs={{0,2},{1,3},{2,4},{3,5},{4,6},{5,7},{6,0},{7,1},{8,10},{9,11},{10,... | collective-permute-start | bytes 221192 | tf_op jit(solution)/shard_map/ppermute | solution.py:124
  7.7 6.7 %collective-permute-start.3 = (bf16[32,1152]{1,0:T(8,128)(2,1)S(1)}, bf16[32,1152]{1,0:T(8,128)(2,1)S(1)}, u32[]{:S(2)}, u32[]{:S(2)}) collective-permute-start(bf16[32,1152]{1,0:T(8,128)(2,1)S(1)} %get-tuple-element.12), channel_id=1, source_target_pairs={{0,4},{1,5},{2,6},{3,7},{4,0},{5,1},{6,2},{7,3},{8,12},{9,13},{10,... | collective-permute-start | bytes 221192 | tf_op jit(solution)/shard_map/ppermute | solution.py:124
  9.7 4.9 %collective-permute-start.2 = (bf16[32,1152]{1,0:T(8,128)(2,1)S(1)}, bf16[32,1152]{1,0:T(8,128)(2,1)S(1)}, u32[]{:S(2)}, u32[]{:S(2)}) collective-permute-start(bf16[32,1152]{1,0:T(8,128)(2,1)S(1)} %get-tuple-element.13), channel_id=1, source_target_pairs={{0,6},{1,7},{2,0},{3,1},{4,2},{5,3},{6,4},{7,5},{8,14},{9,15},{10,... | collective-permute-start | bytes 221192 | tf_op jit(solution)/shard_map/ppermute | solution.py:124
  14.7 3.3 %collective-permute-start.4 = (bf16[32,1152]{1,0:T(8,128)(2,1)S(1)}, bf16[32,1152]{1,0:T(8,128)(2,1)S(1)}, u32[]{:S(2)}, u32[]{:S(2)}) collective-permute-start(bf16[32,1152]{1,0:T(8,128)(2,1)S(1)} %get-tuple-element.9), channel_id=1, source_target_pairs={{0,8},{8,0},{16,24},{24,16},{32,40},{40,32},{48,56},{56,48},{64,72... | collective-permute-start | bytes 221192 | tf_op jit(solution)/shard_map/ppermute | solution.py:130
  18.0 7.9 %collective-permute-start.7 = (bf16[32,1152]{1,0:T(8,128)(2,1)S(1)}, bf16[32,1152]{1,0:T(8,128)(2,1)S(1)}, u32[]{:S(2)}, u32[]{:S(2)}) collective-permute-start(bf16[32,1152]{1,0:T(8,128)(2,1)S(1)} %fusion.8), channel_id=1, source_target_pairs={{0,48},{8,56},{16,0},{24,8},{32,16},{40,24},{48,32},{56,40},{64,11... | collective-permute-start | bytes 221192 | tf_op jit(solution)/shard_map/ppermute | solution.py:130
  23.1 6.3 %collective-permute-start.6 = (bf16[32,1152]{1,0:T(8,128)(2,1)S(1)}, bf16[32,1152]{1,0:T(8,128)(2,1)S(1)}, u32[]{:S(2)}, u32[]{:S(2)}) collective-permute-start(bf16[32,1152]{1,0:T(8,128)(2,1)S(1)} %fusion.8), channel_id=1, source_target_pairs={{0,16},{8,24},{16,32},{24,40},{32,48},{40,56},{48,0},{56,8},{64,80... | collective-permute-start | bytes 221192 | tf_op jit(solution)/shard_map/ppermute | solution.py:130
  23.1 6.3 %collective-permute-start.5 = (bf16[32,1152]{1,0:T(8,128)(2,1)S(1)}, bf16[32,1152]{1,0:T(8,128)(2,1)S(1)}, u32[]{:S(2)}, u32[]{:S(2)}) collective-permute-start(bf16[32,1152]{1,0:T(8,128)(2,1)S(1)} %fusion.8), channel_id=1, source_target_pairs={{0,40},{8,32},{16,56},{24,48},{32,8},{40,0},{48,24},{56,16},{64,10... | collective-permute-start | bytes 221192 | tf_op jit(solution)/shard_map/ppermute | solution.py:130
  29.5 4.8 %collective-permute-start.10 = (bf16[32,1152]{1,0:T(8,128)(2,1)S(1)}, bf16[32,1152]{1,0:T(8,128)(2,1)S(1)}, u32[]{:S(2)}, u32[]{:S(2)}) collective-permute-start(bf16[32,1152]{1,0:T(8,128)(2,1)S(1)} %fusion.7), channel_id=1, source_target_pairs={{0,128},{8,136},{16,144},{24,152},{32,160},{40,168},{48,176},{56,1... | collective-permute-start | bytes 221192 | tf_op jit(solution)/shard_map/ppermute | solution.py:133
  32.5 3.2 %collective-permute-start.9 = (bf16[32,1152]{1,0:T(8,128)(2,1)S(1)}, bf16[32,1152]{1,0:T(8,128)(2,1)S(1)}, u32[]{:S(2)}, u32[]{:S(2)}) collective-permute-start(bf16[32,1152]{1,0:T(8,128)(2,1)S(1)} %fusion.7), channel_id=1, source_target_pairs={{0,192},{8,200},{16,208},{24,216},{32,224},{40,232},{48,240},{56,2... | collective-permute-start | bytes 221192 | tf_op jit(solution)/shard_map/ppermute | solution.py:133
  33.2 4.7 %collective-permute-start.8 = (bf16[32,1152]{1,0:T(8,128)(2,1)S(1)}, bf16[32,1152]{1,0:T(8,128)(2,1)S(1)}, u32[]{:S(2)}, u32[]{:S(2)}) collective-permute-start(bf16[32,1152]{1,0:T(8,128)(2,1)S(1)} %fusion.7), channel_id=1, source_target_pairs={{0,64},{8,72},{16,80},{24,88},{32,96},{40,104},{48,112},{56,120},{... | collective-permute-start | bytes 221192 | tf_op jit(solution)/shard_map/ppermute | solution.py:133
  38.1 6.7 %collective-permute-start.13 = (bf16[32,1152]{1,0:T(8,128)(2,1)S(1)}, bf16[32,1152]{1,0:T(8,128)(2,1)S(1)}, u32[]{:S(2)}, u32[]{:S(2)}) collective-permute-start(bf16[32,1152]{1,0:T(8,128)(2,1)S(1)} %fusion.6.own_ref), channel_id=1, source_target_pairs={{0,4},{1,5},{2,6},{3,7},{4,0},{5,1},{6,2},{7,3},{8,12},{9,13},{10,... | collective-permute-start | bytes 221192 | tf_op jit(solution)/shard_map/ppermute | solution.py:124
  39.7 5.0 %collective-permute-start.12 = (bf16[32,1152]{1,0:T(8,128)(2,1)S(1)}, bf16[32,1152]{1,0:T(8,128)(2,1)S(1)}, u32[]{:S(2)}, u32[]{:S(2)}) collective-permute-start(bf16[32,1152]{1,0:T(8,128)(2,1)S(1)} %fusion.6.own_ref), channel_id=1, source_target_pairs={{0,6},{1,7},{2,0},{3,1},{4,2},{5,3},{6,4},{7,5},{8,14},{9,15},{10,... | collective-permute-start | bytes 221192 | tf_op jit(solution)/shard_map/ppermute | solution.py:124
  40.3 4.4 %collective-permute-start.11 = (bf16[32,1152]{1,0:T(8,128)(2,1)S(1)}, bf16[32,1152]{1,0:T(8,128)(2,1)S(1)}, u32[]{:S(2)}, u32[]{:S(2)}) collective-permute-start(bf16[32,1152]{1,0:T(8,128)(2,1)S(1)} %fusion.6.own_ref), channel_id=1, source_target_pairs={{0,2},{1,3},{2,4},{3,5},{4,6},{5,7},{6,0},{7,1},{8,10},{9,11},{10,... | collective-permute-start | bytes 221192 | tf_op jit(solution)/shard_map/ppermute | solution.py:124
  44.8 9.2 %collective-permute-start.14 = (bf16[128,1152]{1,0:T(8,128)(2,1)S(1)}, bf16[128,1152]{1,0:T(8,128)(2,1)S(1)}, u32[]{:S(2)}, u32[]{:S(2)}) collective-permute-start(bf16[128,1152]{1,0:T(8,128)(2,1)S(1)} %constant_dynamic-update-slice_fusion.refs_0_), channel_id=1, source_target_pairs={{0,1},{1,0},{2,3},{3,2},{4,5},{5,4},{6,7},{7,6},{8,9},{9,8},{10,11... | collective-permute-start | bytes 884744 | tf_op jit(solution)/shard_map/ppermute | solution.py:124

commit v4 on v3

v4 whole, which is shorter than its diff:
```python
import jax
import jax.numpy as jnp
from jax import lax
from jax.experimental import pallas as pl
from jax.experimental.pallas import tpu as pltpu
from jax.sharding import PartitionSpec as P

BF = jnp.bfloat16
F32 = jnp.float32
I32 = jnp.int32
MIB = 2**20
PARTS = 6
FEATS = 8
LAYERS = 32


def iota(shape, axis):
    return lax.broadcasted_iota(I32, shape, axis)


def ranks_of(chosen):
    k = chosen.shape[1]
    along = jnp.broadcast_to(chosen, (k, k))
    down = along.T
    row, lane = iota((k, k), 0), iota((k, k), 1)
    b_first = (along < down) | ((along == down) & (lane < row))
    a_first = (down < along) | ((along == down) & (row < lane))
    rank_down = jnp.sum(b_first.astype(F32), axis=1, keepdims=True)
    rank_along = jnp.sum(a_first.astype(F32), axis=0, keepdims=True)
    return rank_down, rank_along


def slots_onehot(chosen, rank_along, first, n, base, hot_ref):
    k = chosen.shape[1]
    feats = hot_ref.shape[1]
    slot = (first + iota((n, k), 0)).astype(F32)
    here = jnp.broadcast_to(rank_along, (n, k)) == slot
    value = jnp.where(here, jnp.broadcast_to(chosen.astype(F32) + 1.0, (n, k)), 0.0)
    feature = jnp.sum(value, axis=1, keepdims=True) - 1.0 - base.astype(F32)
    feature = jnp.broadcast_to(feature, (n, k))
    lane = iota((n, k), 1).astype(F32)
    for j in range(feats // k):
        hot_ref[:, j * k : (j + 1) * k] = (feature == lane + float(j * k)).astype(F32).astype(BF)


def pick_kernel(near, chosen_ref, dec_ref, *refs):
    outs, (hot_ref, buf_ref, list_ref, sems) = refs[:-4], refs[-4:]
    n, feats = hot_ref.shape
    k = list_ref.shape[1]
    width = buf_ref.shape[1]
    wide = width // PARTS
    share = k // FEATS
    feat = lax.axis_index("feat")
    listed = pltpu.make_async_copy(chosen_ref, list_ref, sems.at[PARTS])
    listed.start()
    copies = []
    for p in range(PARTS):
        cols = pl.ds(p * wide, wide)
        copies.append(pltpu.make_async_copy(dec_ref.at[:, cols], buf_ref.at[:, cols], sems.at[p]))
        copies[p].start()
    listed.wait()
    chosen = list_ref[...]
    rank_down, rank_along = ranks_of(chosen)
    first = share * (feat - 1) if near else 0
    slots_onehot(chosen, rank_along, first, n, feat * feats, hot_ref)
    if near:
        p = iota((k, k), 1)
        half = k // 2
        other, rest = lax.div(p, half), lax.rem(p, half)
        owner = 2 * lax.div(rest, share) + lax.rem(feat + other, 2)
        slot = share * owner + lax.rem(rest, share)
        order = jnp.broadcast_to(rank_down, (k, k)) == slot.astype(F32)
        outs[3][...] = order.astype(F32).astype(BF)
        edge = iota((FEATS, k), 0)
        held = jnp.sum((jnp.broadcast_to(chosen, (FEATS, k)) < edge * feats).astype(F32), axis=1, keepdims=True)
        far = jnp.abs(held - (edge[:, :1] * share).astype(F32)) > share
        outs[4][...] = jnp.broadcast_to(jnp.max(far.astype(F32), axis=0, keepdims=True), outs[4].shape)
    for p in range(PARTS):
        cols = slice(p * wide, (p + 1) * wide)
        copies[p].wait()
        part = jnp.dot(hot_ref[...], buf_ref[:, cols], preferred_element_type=F32).astype(BF)
        if near:
            for i in range(3):
                outs[i][:, cols] = part[i * share : (i + 1) * share]
        else:
            outs[0][:, cols] = part


def pick(chosen, dec, near):
    feats, width = dec.shape
    k = chosen.shape[1]
    share = k // FEATS
    n = 3 * share if near else k
    if near:
        shapes = [(share, width)] * 3 + [(k, k), (8, 128), (share, width)]
        shapes = [jax.ShapeDtypeStruct(shape, F32 if shape[0] == 8 else BF) for shape in shapes]
        spaces = [pltpu.VMEM] * 5 + [pltpu.HBM]
    else:
        shapes, spaces = [jax.ShapeDtypeStruct((k, width), BF)], [pltpu.VMEM]
    return pl.pallas_call(
        lambda *refs: pick_kernel(near, *refs),
        in_specs=[pl.BlockSpec(memory_space=pltpu.HBM)] * 2,
        out_specs=[pl.BlockSpec(memory_space=space) for space in spaces],
        out_shape=shapes,
        scratch_shapes=[
            pltpu.VMEM((n, feats), BF),
            pltpu.VMEM((feats, width), BF),
            pltpu.VMEM((1, k), I32),
            pltpu.SemaphoreType.DMA((PARTS + 1,)),
        ],
        compiler_params=pltpu.CompilerParams(vmem_limit_bytes=12 * MIB),
        cost_estimate=pl.CostEstimate(flops=2 * n * feats * width, bytes_accessed=2 * feats * width, transcendentals=0),
        name="pick_near" if near else "pick_all",
    )(chosen, dec)


def settle_kernel(own_ref, up_ref, down_ref, far_ref, room_ref, out_ref, sem):
    far = far_ref[0, 0] > 0.0

    @pl.when(far)
    def _():
        copy = pltpu.make_async_copy(room_ref, out_ref, sem)
        copy.start()
        copy.wait()

    @pl.when(jnp.logical_not(far))
    def _():
        out_ref[...] = own_ref[...] + up_ref[...] + down_ref[...]


def settle(own, up, down, far, room):
    return pl.pallas_call(
        settle_kernel,
        in_specs=[pl.BlockSpec(memory_space=pltpu.VMEM)] * 4 + [pl.BlockSpec(memory_space=pltpu.HBM)],
        out_specs=pl.BlockSpec(memory_space=pltpu.VMEM),
        out_shape=jax.ShapeDtypeStruct(own.shape, own.dtype),
        scratch_shapes=[pltpu.SemaphoreType.DMA],
        compiler_params=pltpu.CompilerParams(vmem_limit_bytes=2 * MIB),
        cost_estimate=pl.CostEstimate(flops=2 * own.size, bytes_accessed=8 * own.size, transcendentals=0),
        name="settle",
    )(own, up, down, far, room)


def fetch_kernel(own_ref, enc_ref, out_ref, same_ref, sem):
    copy = pltpu.make_async_copy(enc_ref, out_ref, sem)
    copy.start()
    same_ref[...] = own_ref[...]
    copy.wait()


def fetch(own, enc):
    return pl.pallas_call(
        fetch_kernel,
        in_specs=[pl.BlockSpec(memory_space=pltpu.VMEM), pl.BlockSpec(memory_space=pltpu.HBM)],
        out_specs=[pl.BlockSpec(memory_space=pltpu.VMEM)] * 2,
        out_shape=[pltpu.VMEM(enc.shape, enc.dtype), jax.ShapeDtypeStruct(own.shape, own.dtype)],
        scratch_shapes=[pltpu.SemaphoreType.DMA],
        compiler_params=pltpu.CompilerParams(vmem_limit_bytes=8 * MIB),
        cost_estimate=pl.CostEstimate(flops=0, bytes_accessed=4 * enc.size, transcendentals=0),
        name="fetch",
    )(own, enc)


def product_kernel(last, left_ref, enc_ref, *refs):
    half = left_ref.shape[0]
    if last:
        first_ref, order_ref, out_ref, rows_ref = refs
        rows_ref[:half, :] = first_ref[...]
    else:
        out_ref = rows_ref = refs[0]
    at = half if last else 0
    tile = 256
    for j in range(out_ref.shape[1] // tile):
        cols = slice(j * tile, (j + 1) * tile)
        part = jnp.dot(left_ref[...], enc_ref[:, cols], preferred_element_type=F32)
        rows_ref[at : at + half, cols] = part.astype(BF)
    if last:
        for j in range(out_ref.shape[1] // tile):
            cols = slice(j * tile, (j + 1) * tile)
            part = jnp.dot(order_ref[...], rows_ref[:, cols], preferred_element_type=F32)
            out_ref[:, cols] = part.astype(BF)


def product(left, enc, *more):
    half, width = left.shape
    n = enc.shape[1]
    last = bool(more)
    return pl.pallas_call(
        lambda *refs: product_kernel(last, *refs),
        in_specs=[pl.BlockSpec(memory_space=pltpu.VMEM)] * (2 + len(more)),
        out_specs=pl.BlockSpec(memory_space=pltpu.VMEM),
        out_shape=jax.ShapeDtypeStruct((2 * half if last else half, n), BF),
        scratch_shapes=[pltpu.VMEM((2 * half, n), BF)] if last else [],
        compiler_params=pltpu.CompilerParams(vmem_limit_bytes=16 * MIB),
        cost_estimate=pl.CostEstimate(flops=2 * half * n * width, bytes_accessed=2 * width * n, transcendentals=0),
        name="product_last" if last else "product_own",
    )(left, enc, *more)


def local(encoder, decoder, chosen):
    enc = pltpu.with_memory_space_constraint(encoder[0], pltpu.HBM)
    dec = pltpu.with_memory_space_constraint(decoder[0], pltpu.HBM)
    k, feats = chosen.shape[0], dec.shape[0]
    share = k // FEATS
    listed = pltpu.with_memory_space_constraint(chosen.reshape(1, k), pltpu.HBM)
    feat, layer = lax.axis_index("feat"), lax.axis_index("layer")
    x = feat // 2
    y, z = layer // 8, layer % 8

    def feat_step(v, move):
        return lax.ppermute(v, "feat", [(i, move(i) % FEATS) for i in range(FEATS)])

    def along_x(v, d):
        return feat_step(v, lambda i: i + 2 * d)

    def along_z(v, move):
        return lax.ppermute(v, "layer", [(i, i // 8 * 8 + move(i % 8) % 8) for i in range(LAYERS)])

    def along_y(v, d):
        return lax.ppermute(v, "layer", [(i, (i + 8 * d) % LAYERS) for i in range(LAYERS)])

    below, own, above, order, far, room = pick(listed, dec, True)
    up = feat_step(above, lambda i: i + 1)
    down = feat_step(below, lambda i: i - 1)

    def general(state):
        (rows,) = pick(listed, dec, False)

        def chunk(d):
            return lax.dynamic_slice_in_dim(rows, share * ((feat + d) % FEATS), share, 0)

        total = chunk(0)
        for d in range(1, FEATS):
            total = total + feat_step(chunk(d), lambda i: i + d)
        return jnp.zeros_like(state[0]), total

    edges = jnp.arange(1, FEATS)
    held = jnp.sum((chosen[:, None] < edges[None, :] * feats).astype(I32), axis=0)
    spread = jnp.any(jnp.abs(held - edges * share) > share)
    room = lax.while_loop(lambda state: state[0], general, (spread, room))[1]
    total = settle(own, up, down, far, room).astype(F32)

    before = jnp.zeros_like(total)

    def join(arrivals, before, total):
        for lower, v in arrivals:
            v = v.astype(F32)
            before = before + jnp.where(lower, v, 0.0)
            total = total + v
        return before, total

    before, total = join([(z % 2 == 1, along_z(total.astype(BF), lambda i: i ^ 1))], before, total)
    low = total.astype(BF)
    up = along_z(low, lambda i: i + 2)
    down = along_z(low, lambda i: i - 2)
    across = along_z(low, lambda i: i + 3 if i % 2 else i - 3)
    before, total = join([(z >= 4, across), (z >= 2, up), (z >= 6, down)], before, total)
    low = total.astype(BF)
    arrivals = [(y >= d, along_y(low, d)) for d in (1, 3, 2)]
    before, total = join(arrivals, before, total)
    prefix = before.astype(BF)

    pieces = [along_x(prefix, d) for d in (1, 3, 2)]
    near, prefix = fetch(prefix, enc)
    whole = jnp.zeros((k // 2, prefix.shape[1]), BF)
    for d, piece in zip((0, 1, 3, 2), [prefix] + pieces):
        whole = lax.dynamic_update_slice_in_dim(whole, piece, share * ((x + 4 - d) % 4), 0)
    other = feat_step(whole, lambda i: i ^ 1)
    return product(other, near, product(whole, near), order)[None]


def solution(mesh):
    placed = (P("layer", None, "feat"), P("layer", "feat", None), P())
    return jax.shard_map(
        local, mesh=mesh, in_specs=placed, out_specs=P("layer", None, "feat"), check_vma=False
    )
```

time: 55.4 us -> 51.9 us (0.937)
  waiting for transfers between devices: 15.7 us -> 11.6 us
  other arithmetic: 0.3 us -> 1.74 us
  starting transfers between devices: 30.7 us -> 29.7 us
  loops' own time: 0 us -> 0.7 us
    ppermute x11 -> x9, starting transfers between devices: 22.1 us -> 17.5 us  [the longest x6 13 us: feat_step(): return lax.ppermute(v, 'feat', [(i, move(i) % FEATS) for i in range(FEATS)])]
    ppermute x4, starting transfers between devices: 8.61 us -> 12.2 us  [along_z(): lax.ppermute(v, 'layer', [(i, i // 8 * 8 + move(i % 8) % 8) for i in rang...]
    ppermute x11 -> x9, waiting for transfers between devices: 9.6 us -> 7.35 us  [the longest x6 3.98 us: feat_step(): return lax.ppermute(v, 'feat', [(i, move(i) % FEATS) for i in range(FEATS)])]
    ppermute x4, waiting for transfers between devices: 6.11 us -> 4.2 us  [along_z(): lax.ppermute(v, 'layer', [(i, i // 8 * 8 + move(i % 8) % 8) for i in rang...]
    reduce_sum x0 -> x1, other arithmetic: none -> 0.84 us  [local(): jnp.sum((chosen[:, None] < edges[None, :] * feats).astype(I32), axis=0)]
    reduce_or x0 -> x1, other arithmetic: none -> 0.72 us  [local(): spread = jnp.any(jnp.abs(held - edges * share) > share)]
    another operation x0 -> x1, loops' own time: none -> 0.7 us  [local(): room = lax.while_loop(lambda state: state[0], general, (spread, room))[1]]
  transfers between devices with their start and end apart: 15 -> 13, of which waited for: 9 -> 9; matrix products, arithmetic and copies ran while one was open for 0% -> 0% of each run, Pallas kernels for 9% -> 6%
where the time goes in v4:
time: 51.9 us; the launch traced here: 51.8 us
  starting transfers between devices  29.7 us (57%)
  waiting for transfers between devices  11.6 us (22%)
  Pallas kernels  7.94 us (15%)
  other arithmetic  1.74 us (3%)
  loops' own time  0.7 us (1%)
    ppermute x6, starting transfers between devices, feat_step(): return lax.ppermute(v, 'feat', [(i, move(i) % FEATS) for i in range(FEATS)])  13 us
    ppermute x4, starting transfers between devices, along_z(): lax.ppermute(v, 'layer', [(i, i // 8 * 8 + move(i % 8) % 8) for i in rang...  12.2 us
    ppermute x3, starting transfers between devices, along_y(): lax.ppermute(v, 'layer', [(i, (i + 8 * d) % LAYERS) for i in range(LAYERS)])  4.46 us
    ppermute x4, waiting for transfers between devices, along_z(): lax.ppermute(v, 'layer', [(i, i // 8 * 8 + move(i % 8) % 8) for i in rang...  4.2 us
    ppermute x6, waiting for transfers between devices, feat_step(): return lax.ppermute(v, 'feat', [(i, move(i) % FEATS) for i in range(FEATS)])  3.98 us
    ppermute x3, waiting for transfers between devices, along_y(): lax.ppermute(v, 'layer', [(i, (i + 8 * d) % LAYERS) for i in range(LAYERS)])  3.38 us
    pallas_call x1, Pallas kernels, pick(): pl.pallas_call(lambda *refs: pick_kernel(near, *refs), in_specs=[pl.Block...  2.8 us
    pallas_call x2, Pallas kernels, product(): pl.pallas_call(lambda *refs: product_kernel(last, *refs), in_specs=[pl.Bl...  2.73 us
  transfers between devices with their start and end apart: 13, of which 9 were waited for; matrix products, arithmetic and copies ran while one was open for 0% of the time, Pallas kernels for 6%

profile of v4, /device:TPU:1, one launch (start us, length us, event | category | flops | bytes accessed | tf_op | source)
XLA Modules:
  0.0 51.8 jit_solution(11782336677739156427)
XLA Ops:
  0.0 0.8 %convert_reduce_fusion = s32[7]{0:T(128)S(1)} fusion(s32[128]{0:T(128)} %param.7, s32[7]{0:T(128)S(1)} %fusion.9), kind=kLoop, calls=%fused_computation.25 | loop fusion | flops 2681 | bytes 568 | tf_op jit(solution)/shard_map/reduce_sum | solution.py:238
  0.8 0.7 %compare_reduce_fusion = pred[]{:T(512)} fusion(s32[7]{0:T(128)S(1)} %convert_reduce_fusion), kind=kLoop, calls=%fused_computation.26 | loop fusion | flops 41 | bytes 29 | tf_op jit(solution)/shard_map/reduce_or | solution.py:239
  1.6 2.8 %pick_near.1 = (bf16[16,2304]{1,0:T(8,128)(2,1)S(1)}, bf16[16,2304]{1,0:T(8,128)(2,1)S(1)}, bf16[16,2304]{1,0:T(8,128)(2,1)S(1)}, bf16[128,128]{1,0:T(8,128)(2,1...) custom-call(s32[1,128]{1,0:T(1,128)} %bitcast.7, bf16[1024,2304]{1,0:T(8,128)(2,1)} %bitcast.4), custom_call_target="tpu_custom_call" | custom-call | flops 226492416 | bytes 4718592 | tf_op jit(solution)/shard_map/pick_near/pallas_call | solution.py:100
  4.4 0.7 %while.9 = (pred[]{:T(512)}, bf16[16,2304]{1,0:T(8,128)(2,1)}, s32[1,128]{1,0:T(1,128)}, bf16[1024,2304]{1,0:T(8,128)(2,1)}, s32[]{:T(128)}) while((pred[]{:T(512)}, bf16[16,2304]{1,0:T(8,128)(2,1)}, s32[1,128]{1,0:T(1,128)}, bf16[1024,2304]{1,0:T(8,128)(2,1)}, s32[]{:T(128)}) %tuple.23), condition=%region_3.4_spmd, body=%region_2.3_spmd | while | flops 604569600 | bytes 8480398 | solution.py:240
  5.1 2.6 %collective-permute-start.7 = (bf16[16,2304]{1,0:T(8,128)(2,1)S(1)}, bf16[16,2304]{1,0:T(8,128)(2,1)S(1)}, u32[]{:S(2)}, u32[]{:S(2)}) collective-permute-start(bf16[16,2304]{1,0:T(8,128)(2,1)S(1)} %get-tuple-element.39), channel_id=1, source_target_pairs={{0,1},{1,2},{2,3},{3,4},{4,5},{5,6},{6,7},{7,0},{8,9},{9,10},{10,1... | collective-permute-start | bytes 221192 | tf_op jit(solution)/shard_map/ppermute | solution.py:211
  7.7 0.7 %collective-permute-start.8 = (bf16[16,2304]{1,0:T(8,128)(2,1)S(1)}, bf16[16,2304]{1,0:T(8,128)(2,1)S(1)}, u32[]{:S(2)}, u32[]{:S(2)}) collective-permute-start(bf16[16,2304]{1,0:T(8,128)(2,1)S(1)} %get-tuple-element.40), channel_id=1, source_target_pairs={{0,7},{1,0},{2,1},{3,2},{4,3},{5,4},{6,5},{7,6},{8,15},{9,8},{10,9... | collective-permute-start | bytes 221192 | tf_op jit(solution)/shard_map/ppermute | solution.py:211
  8.3 0.7 %collective-permute-done.7.up_ref = bf16[16,2304]{1,0:T(8,128)(2,1)S(1)} collective-permute-done((bf16[16,2304]{1,0:T(8,128)(2,1)S(1)}, bf16[16,2304]{1,0:T(8,128)(2,1)S(1)}, u32[]{:S(2)}, u32[]{:S(2)}) %collective-permute-start.7) | collective-permute-done | bytes 73760 | tf_op jit(solution)/shard_map/ppermute | solution.py:211
  9.1 2.4 %collective-permute-done.8.down_ref = bf16[16,2304]{1,0:T(8,128)(2,1)S(1)} collective-permute-done((bf16[16,2304]{1,0:T(8,128)(2,1)S(1)}, bf16[16,2304]{1,0:T(8,128)(2,1)S(1)}, u32[]{:S(2)}, u32[]{:S(2)}) %collective-permute-start.8) | collective-permute-done | bytes 73760 | tf_op jit(solution)/shard_map/ppermute | solution.py:211
  11.5 0.1 settle.1
  11.5 1.7 %collective-permute-start.9 = (bf16[16,2304]{1,0:T(8,128)(2,1)S(1)}, bf16[16,2304]{1,0:T(8,128)(2,1)S(1)}, u32[]{:S(2)}, u32[]{:S(2)}) collective-permute-start(bf16[16,2304]{1,0:T(8,128)(2,1)S(1)} %settle.1), channel_id=1, source_target_pairs={{0,8},{8,0},{16,24},{24,16},{32,40},{40,32},{48,56},{56,48},{64,72... | collective-permute-start | bytes 221192 | tf_op jit(solution)/shard_map/ppermute | solution.py:217
  13.3 1.7 %collective-permute-done.9 = bf16[16,2304]{1,0:T(8,128)(2,1)S(1)} collective-permute-done((bf16[16,2304]{1,0:T(8,128)(2,1)S(1)}, bf16[16,2304]{1,0:T(8,128)(2,1)S(1)}, u32[]{:S(2)}, u32[]{:S(2)}) %collective-permute-start.9) | collective-permute-done | bytes 73760 | tf_op jit(solution)/shard_map/ppermute | solution.py:217
  15.0 6.9 %collective-permute-start.10 = (bf16[16,2304]{1,0:T(8,128)(2,1)S(1)}, bf16[16,2304]{1,0:T(8,128)(2,1)S(1)}, u32[]{:S(2)}, u32[]{:S(2)}) collective-permute-start(bf16[16,2304]{1,0:T(8,128)(2,1)S(1)} %fusion.8), channel_id=1, source_target_pairs={{0,40},{8,32},{16,56},{24,48},{32,8},{40,0},{48,24},{56,16},{64,10... | collective-permute-start | bytes 221192 | tf_op jit(solution)/shard_map/ppermute | solution.py:217
  21.9 1.2 %collective-permute-start.11 = (bf16[16,2304]{1,0:T(8,128)(2,1)S(1)}, bf16[16,2304]{1,0:T(8,128)(2,1)S(1)}, u32[]{:S(2)}, u32[]{:S(2)}) collective-permute-start(bf16[16,2304]{1,0:T(8,128)(2,1)S(1)} %fusion.8), channel_id=1, source_target_pairs={{0,16},{8,24},{16,32},{24,40},{32,48},{40,56},{48,0},{56,8},{64,80... | collective-permute-start | bytes 221192 | tf_op jit(solution)/shard_map/ppermute | solution.py:217
  23.1 2.4 %collective-permute-start.12 = (bf16[16,2304]{1,0:T(8,128)(2,1)S(1)}, bf16[16,2304]{1,0:T(8,128)(2,1)S(1)}, u32[]{:S(2)}, u32[]{:S(2)}) collective-permute-start(bf16[16,2304]{1,0:T(8,128)(2,1)S(1)} %fusion.8), channel_id=1, source_target_pairs={{0,48},{8,56},{16,0},{24,8},{32,16},{40,24},{48,32},{56,40},{64,11... | collective-permute-start | bytes 221192 | tf_op jit(solution)/shard_map/ppermute | solution.py:217
  25.5 0.0 collective-permute-done.10
  25.5 2.0 %collective-permute-done.11 = bf16[16,2304]{1,0:T(8,128)(2,1)S(1)} collective-permute-done((bf16[16,2304]{1,0:T(8,128)(2,1)S(1)}, bf16[16,2304]{1,0:T(8,128)(2,1)S(1)}, u32[]{:S(2)}, u32[]{:S(2)}) %collective-permute-start.11) | collective-permute-done | bytes 73760 | tf_op jit(solution)/shard_map/ppermute | solution.py:217
  27.5 0.4 collective-permute-done.12
  28.0 0.1 fusion.7
  28.0 1.4 %collective-permute-start.13 = (bf16[16,2304]{1,0:T(8,128)(2,1)S(1)}, bf16[16,2304]{1,0:T(8,128)(2,1)S(1)}, u32[]{:S(2)}, u32[]{:S(2)}) collective-permute-start(bf16[16,2304]{1,0:T(8,128)(2,1)S(1)} %fusion.7), channel_id=1, source_target_pairs={{0,64},{8,72},{16,80},{24,88},{32,96},{40,104},{48,112},{56,120},{... | collective-permute-start | bytes 221192 | tf_op jit(solution)/shard_map/ppermute | solution.py:220
  29.4 1.5 %collective-permute-start.14 = (bf16[16,2304]{1,0:T(8,128)(2,1)S(1)}, bf16[16,2304]{1,0:T(8,128)(2,1)S(1)}, u32[]{:S(2)}, u32[]{:S(2)}) collective-permute-start(bf16[16,2304]{1,0:T(8,128)(2,1)S(1)} %fusion.7), channel_id=1, source_target_pairs={{0,192},{8,200},{16,208},{24,216},{32,224},{40,232},{48,240},{56,2... | collective-permute-start | bytes 221192 | tf_op jit(solution)/shard_map/ppermute | solution.py:220
  30.9 1.6 %collective-permute-start.15 = (bf16[16,2304]{1,0:T(8,128)(2,1)S(1)}, bf16[16,2304]{1,0:T(8,128)(2,1)S(1)}, u32[]{:S(2)}, u32[]{:S(2)}) collective-permute-start(bf16[16,2304]{1,0:T(8,128)(2,1)S(1)} %fusion.7), channel_id=1, source_target_pairs={{0,128},{8,136},{16,144},{24,152},{32,160},{40,168},{48,176},{56,1... | collective-permute-start | bytes 221192 | tf_op jit(solution)/shard_map/ppermute | solution.py:220
  32.5 0.1 collective-permute-done.13
  32.6 0.0 collective-permute-done.14
  32.6 3.3 %collective-permute-done.15 = bf16[16,2304]{1,0:T(8,128)(2,1)S(1)} collective-permute-done((bf16[16,2304]{1,0:T(8,128)(2,1)S(1)}, bf16[16,2304]{1,0:T(8,128)(2,1)S(1)}, u32[]{:S(2)}, u32[]{:S(2)}) %collective-permute-start.15) | collective-permute-done | bytes 73760 | tf_op jit(solution)/shard_map/ppermute | solution.py:220
  35.9 0.1 fusion.6.own_ref
  36.0 2.7 %collective-permute-start.16 = (bf16[16,2304]{1,0:T(8,128)(2,1)S(1)}, bf16[16,2304]{1,0:T(8,128)(2,1)S(1)}, u32[]{:S(2)}, u32[]{:S(2)}) collective-permute-start(bf16[16,2304]{1,0:T(8,128)(2,1)S(1)} %fusion.6.own_ref), channel_id=1, source_target_pairs={{0,2},{1,3},{2,4},{3,5},{4,6},{5,7},{6,0},{7,1},{8,10},{9,11},{10,... | collective-permute-start | bytes 221192 | tf_op jit(solution)/shard_map/ppermute | solution.py:211
  38.7 0.2 collective-permute-start.17
  38.9 1.7 %collective-permute-start.18 = (bf16[16,2304]{1,0:T(8,128)(2,1)S(1)}, bf16[16,2304]{1,0:T(8,128)(2,1)S(1)}, u32[]{:S(2)}, u32[]{:S(2)}) collective-permute-start(bf16[16,2304]{1,0:T(8,128)(2,1)S(1)} %fusion.6.own_ref), channel_id=1, source_target_pairs={{0,4},{1,5},{2,6},{3,7},{4,0},{5,1},{6,2},{7,3},{8,12},{9,13},{10,... | collective-permute-start | bytes 221192 | tf_op jit(solution)/shard_map/ppermute | solution.py:211
  40.6 2.3 %fetch.1 = (bf16[2304,1024]{1,0:T(8,128)(2,1)S(1)}, bf16[16,2304]{1,0:T(8,128)(2,1)S(1)}) custom-call(bf16[16,2304]{1,0:T(8,128)(2,1)S(1)} %fusion.6.own_ref, bf16[2304,1024]{1,0:T(8,128)(2,1)} %bitcast.6), custom_call_target="tpu_custom_call" | custom-call | bytes 9437184 | tf_op jit(solution)/shard_map/fetch/pallas_call | solution.py:152
  43.0 0.0 collective-permute-done.16
  43.0 0.0 collective-permute-done.17
  43.0 0.6 %collective-permute-done.18 = bf16[16,2304]{1,0:T(8,128)(2,1)S(1)} collective-permute-done((bf16[16,2304]{1,0:T(8,128)(2,1)S(1)}, bf16[16,2304]{1,0:T(8,128)(2,1)S(1)}, u32[]{:S(2)}, u32[]{:S(2)}) %collective-permute-start.18) | collective-permute-done | bytes 73760 | tf_op jit(solution)/shard_map/ppermute | solution.py:211
  43.6 5.2 %collective-permute-start.19 = (bf16[64,2304]{1,0:T(8,128)(2,1)S(1)}, bf16[64,2304]{1,0:T(8,128)(2,1)S(1)}, u32[]{:S(2)}, u32[]{:S(2)}) collective-permute-start(bf16[64,2304]{1,0:T(8,128)(2,1)S(1)} %constant_dynamic-update-slice_fusion.refs_0_), channel_id=1, source_target_pairs={{0,1},{1,0},{2,3},{3,2},{4,5},{5,4},{6,7},{7,6},{8,9},{9,8},{10,11... | collective-permute-start | bytes 884744 | tf_op jit(solution)/shard_map/ppermute | solution.py:211
  48.8 0.9 %product_own.1.refs_2_ = bf16[64,1024]{1,0:T(8,128)(2,1)S(1)} custom-call(bf16[64,2304]{1,0:T(8,128)(2,1)S(1)} %constant_dynamic-update-slice_fusion.refs_0_, bf16[2304,1024]{1,0:T(8,128)(2,1)S(1)} %get-tuple-element.45.refs_1_), custom_call_target="tpu_custom_call" | custom-call | flops 301989888 | bytes 4718592 | tf_op jit(solution)/shard_map/product_own/pallas_call | solution.py:188
  49.7 0.3 collective-permute-done.19.refs_0_
  50.0 1.8 %product_last.1 = bf16[128,1024]{1,0:T(8,128)(2,1)} custom-call(bf16[64,2304]{1,0:T(8,128)(2,1)S(1)} %collective-permute-done.19.refs_0_, bf16[2304,1024]{1,0:T(8,128)(2,1)S(1)} %get-tuple-element.45.refs_1_, bf16[64,1024]{1,0:T(8,128)(2,1)S(1)} %product_own.1.refs_2_, bf16[128,128]{1,0:T(8,128)(2,1)S(1)} %get-tuple-element.46.refs_3_), custom_call_target="tpu_custom_call" | custom-call | flops 301989888 | bytes 4718592 | tf_op jit(solution)/shard_map/product_last/pallas_call | solution.py:188
  (7 shorter events, 0.1 us)
Async XLA Ops:
  5.1 4.0 %collective-permute-start.7 = (bf16[16,2304]{1,0:T(8,128)(2,1)S(1)}, bf16[16,2304]{1,0:T(8,128)(2,1)S(1)}, u32[]{:S(2)}, u32[]{:S(2)}) collective-permute-start(bf16[16,2304]{1,0:T(8,128)(2,1)S(1)} %get-tuple-element.39), channel_id=1, source_target_pairs={{0,1},{1,2},{2,3},{3,4},{4,5},{5,6},{6,7},{7,0},{8,9},{9,10},{10,1... | collective-permute-start | bytes 221192 | tf_op jit(solution)/shard_map/ppermute | solution.py:211
  7.7 3.8 %collective-permute-start.8 = (bf16[16,2304]{1,0:T(8,128)(2,1)S(1)}, bf16[16,2304]{1,0:T(8,128)(2,1)S(1)}, u32[]{:S(2)}, u32[]{:S(2)}) collective-permute-start(bf16[16,2304]{1,0:T(8,128)(2,1)S(1)} %get-tuple-element.40), channel_id=1, source_target_pairs={{0,7},{1,0},{2,1},{3,2},{4,3},{5,4},{6,5},{7,6},{8,15},{9,8},{10,9... | collective-permute-start | bytes 221192 | tf_op jit(solution)/shard_map/ppermute | solution.py:211
  11.5 3.5 %collective-permute-start.9 = (bf16[16,2304]{1,0:T(8,128)(2,1)S(1)}, bf16[16,2304]{1,0:T(8,128)(2,1)S(1)}, u32[]{:S(2)}, u32[]{:S(2)}) collective-permute-start(bf16[16,2304]{1,0:T(8,128)(2,1)S(1)} %settle.1), channel_id=1, source_target_pairs={{0,8},{8,0},{16,24},{24,16},{32,40},{40,32},{48,56},{56,48},{64,72... | collective-permute-start | bytes 221192 | tf_op jit(solution)/shard_map/ppermute | solution.py:217
  15.0 10.5 %collective-permute-start.10 = (bf16[16,2304]{1,0:T(8,128)(2,1)S(1)}, bf16[16,2304]{1,0:T(8,128)(2,1)S(1)}, u32[]{:S(2)}, u32[]{:S(2)}) collective-permute-start(bf16[16,2304]{1,0:T(8,128)(2,1)S(1)} %fusion.8), channel_id=1, source_target_pairs={{0,40},{8,32},{16,56},{24,48},{32,8},{40,0},{48,24},{56,16},{64,10... | collective-permute-start | bytes 221192 | tf_op jit(solution)/shard_map/ppermute | solution.py:217
  21.9 5.6 %collective-permute-start.11 = (bf16[16,2304]{1,0:T(8,128)(2,1)S(1)}, bf16[16,2304]{1,0:T(8,128)(2,1)S(1)}, u32[]{:S(2)}, u32[]{:S(2)}) collective-permute-start(bf16[16,2304]{1,0:T(8,128)(2,1)S(1)} %fusion.8), channel_id=1, source_target_pairs={{0,16},{8,24},{16,32},{24,40},{32,48},{40,56},{48,0},{56,8},{64,80... | collective-permute-start | bytes 221192 | tf_op jit(solution)/shard_map/ppermute | solution.py:217
  23.1 4.8 %collective-permute-start.12 = (bf16[16,2304]{1,0:T(8,128)(2,1)S(1)}, bf16[16,2304]{1,0:T(8,128)(2,1)S(1)}, u32[]{:S(2)}, u32[]{:S(2)}) collective-permute-start(bf16[16,2304]{1,0:T(8,128)(2,1)S(1)} %fusion.8), channel_id=1, source_target_pairs={{0,48},{8,56},{16,0},{24,8},{32,16},{40,24},{48,32},{56,40},{64,11... | collective-permute-start | bytes 221192 | tf_op jit(solution)/shard_map/ppermute | solution.py:217
  28.0 4.6 %collective-permute-start.13 = (bf16[16,2304]{1,0:T(8,128)(2,1)S(1)}, bf16[16,2304]{1,0:T(8,128)(2,1)S(1)}, u32[]{:S(2)}, u32[]{:S(2)}) collective-permute-start(bf16[16,2304]{1,0:T(8,128)(2,1)S(1)} %fusion.7), channel_id=1, source_target_pairs={{0,64},{8,72},{16,80},{24,88},{32,96},{40,104},{48,112},{56,120},{... | collective-permute-start | bytes 221192 | tf_op jit(solution)/shard_map/ppermute | solution.py:220
  29.4 3.2 %collective-permute-start.14 = (bf16[16,2304]{1,0:T(8,128)(2,1)S(1)}, bf16[16,2304]{1,0:T(8,128)(2,1)S(1)}, u32[]{:S(2)}, u32[]{:S(2)}) collective-permute-start(bf16[16,2304]{1,0:T(8,128)(2,1)S(1)} %fusion.7), channel_id=1, source_target_pairs={{0,192},{8,200},{16,208},{24,216},{32,224},{40,232},{48,240},{56,2... | collective-permute-start | bytes 221192 | tf_op jit(solution)/shard_map/ppermute | solution.py:220
  30.9 4.9 %collective-permute-start.15 = (bf16[16,2304]{1,0:T(8,128)(2,1)S(1)}, bf16[16,2304]{1,0:T(8,128)(2,1)S(1)}, u32[]{:S(2)}, u32[]{:S(2)}) collective-permute-start(bf16[16,2304]{1,0:T(8,128)(2,1)S(1)} %fusion.7), channel_id=1, source_target_pairs={{0,128},{8,136},{16,144},{24,152},{32,160},{40,168},{48,176},{56,1... | collective-permute-start | bytes 221192 | tf_op jit(solution)/shard_map/ppermute | solution.py:220
  36.0 7.0 %collective-permute-start.16 = (bf16[16,2304]{1,0:T(8,128)(2,1)S(1)}, bf16[16,2304]{1,0:T(8,128)(2,1)S(1)}, u32[]{:S(2)}, u32[]{:S(2)}) collective-permute-start(bf16[16,2304]{1,0:T(8,128)(2,1)S(1)} %fusion.6.own_ref), channel_id=1, source_target_pairs={{0,2},{1,3},{2,4},{3,5},{4,6},{5,7},{6,0},{7,1},{8,10},{9,11},{10,... | collective-permute-start | bytes 221192 | tf_op jit(solution)/shard_map/ppermute | solution.py:211
  38.7 4.3 %collective-permute-start.17 = (bf16[16,2304]{1,0:T(8,128)(2,1)S(1)}, bf16[16,2304]{1,0:T(8,128)(2,1)S(1)}, u32[]{:S(2)}, u32[]{:S(2)}) collective-permute-start(bf16[16,2304]{1,0:T(8,128)(2,1)S(1)} %fusion.6.own_ref), channel_id=1, source_target_pairs={{0,6},{1,7},{2,0},{3,1},{4,2},{5,3},{6,4},{7,5},{8,14},{9,15},{10,... | collective-permute-start | bytes 221192 | tf_op jit(solution)/shard_map/ppermute | solution.py:211
  38.9 4.7 %collective-permute-start.18 = (bf16[16,2304]{1,0:T(8,128)(2,1)S(1)}, bf16[16,2304]{1,0:T(8,128)(2,1)S(1)}, u32[]{:S(2)}, u32[]{:S(2)}) collective-permute-start(bf16[16,2304]{1,0:T(8,128)(2,1)S(1)} %fusion.6.own_ref), channel_id=1, source_target_pairs={{0,4},{1,5},{2,6},{3,7},{4,0},{5,1},{6,2},{7,3},{8,12},{9,13},{10,... | collective-permute-start | bytes 221192 | tf_op jit(solution)/shard_map/ppermute | solution.py:211
  43.6 6.4 %collective-permute-start.19 = (bf16[64,2304]{1,0:T(8,128)(2,1)S(1)}, bf16[64,2304]{1,0:T(8,128)(2,1)S(1)}, u32[]{:S(2)}, u32[]{:S(2)}) collective-permute-start(bf16[64,2304]{1,0:T(8,128)(2,1)S(1)} %constant_dynamic-update-slice_fusion.refs_0_), channel_id=1, source_target_pairs={{0,1},{1,0},{2,3},{3,2},{4,5},{5,4},{6,7},{7,6},{8,9},{9,8},{10,11... | collective-permute-start | bytes 884744 | tf_op jit(solution)/shard_map/ppermute | solution.py:211

commit v5 on v4

--- a/solution.py
+++ b/solution.py
@@ -94,6 +94,7 @@
     if near:
         shapes = [(share, width)] * 3 + [(k, k), (8, 128), (share, width)]
         shapes = [jax.ShapeDtypeStruct(shape, F32 if shape[0] == 8 else BF) for shape in shapes]
+        shapes[-1] = pltpu.HBM((share, width), BF)
         spaces = [pltpu.VMEM] * 5 + [pltpu.HBM]
     else:
         shapes, spaces = [jax.ShapeDtypeStruct((k, width), BF)], [pltpu.VMEM]
@@ -112,6 +113,18 @@
         cost_estimate=pl.CostEstimate(flops=2 * n * feats * width, bytes_accessed=2 * feats * width, transcendentals=0),
         name="pick_near" if near else "pick_all",
     )(chosen, dec)
+
+
+def after(up, down, room):
+    return pl.pallas_call(
+        lambda up_ref, down_ref, room_ref, out_ref: None,
+        in_specs=[pl.BlockSpec(memory_space=pltpu.VMEM)] * 2 + [pl.BlockSpec(memory_space=pltpu.HBM)],
+        out_specs=pl.BlockSpec(memory_space=pltpu.HBM),
+        out_shape=pltpu.HBM(room.shape, room.dtype),
+        input_output_aliases={2: 0},
+        compiler_params=pltpu.CompilerParams(vmem_limit_bytes=MIB),
+        name="after",
+    )(up, down, pltpu.with_memory_space_constraint(room, pltpu.HBM))
 
 
 def settle_kernel(own_ref, up_ref, down_ref, far_ref, room_ref, out_ref, sem):
@@ -236,8 +249,8 @@
 
     edges = jnp.arange(1, FEATS)
     held = jnp.sum((chosen[:, None] < edges[None, :] * feats).astype(I32), axis=0)
-    spread = jnp.any(jnp.abs(held - edges * share) > share)
-    room = lax.while_loop(lambda state: state[0], general, (spread, room))[1]
+    close = jnp.all(jnp.abs(held - edges * share) <= share)
+    room = lax.while_loop(lambda state: state[0], general, (jnp.logical_not(close), after(up, down, room)))[1]
     total = settle(own, up, down, far, room).astype(F32)
 
     before = jnp.zeros_like(total)

time: 51.9 us -> 49.7 us (0.958)
  waiting for transfers between devices: 11.6 us -> 10.5 us
  other arithmetic: 1.74 us -> 1.04 us
  loops' own time: 0.7 us -> 0.01 us
  between operations: 0.11 us -> 0.75 us
    ppermute x6, waiting for transfers between devices: 3.98 us -> 2.88 us  [feat_step(): return lax.ppermute(v, 'feat', [(i, move(i) % FEATS) for i in range(FEATS)])]
    reduce_or x1 -> x0, other arithmetic: 0.72 us -> none  [local(): spread = jnp.any(jnp.abs(held - edges * share) > share)]
    another operation x1, loops' own time: 0.7 us -> 0.01 us  [local(): lax.while_loop(lambda state: state[0], general, (jnp.logical_not(close),...]
    reduce_and x0 -> x1, other arithmetic: none -> 0.68 us  [local(): close = jnp.all(jnp.abs(held - edges * share) <= share)]
    reduce_sum x1, other arithmetic: 0.84 us -> 0.18 us  [local(): jnp.sum((chosen[:, None] < edges[None, :] * feats).astype(I32), axis=0)]
  transfers between devices with their start and end apart: 13 -> 13, of which waited for: 9 -> 8; matrix products, arithmetic and copies ran while one was open for 0% -> 2% of each run, Pallas kernels for 6% -> 7%
where the time goes in v5:
time: 49.7 us; the launch traced here: 49.6 us
  starting transfers between devices  29.3 us (59%)
  waiting for transfers between devices  10.5 us (21%)
  Pallas kernels  7.95 us (16%)
  other arithmetic  1.04 us (2%)
  between operations  0.75 us (2%)
    ppermute x6, starting transfers between devices, feat_step(): return lax.ppermute(v, 'feat', [(i, move(i) % FEATS) for i in range(FEATS)])  12.6 us
    ppermute x4, starting transfers between devices, along_z(): lax.ppermute(v, 'layer', [(i, i // 8 * 8 + move(i % 8) % 8) for i in rang...  12.2 us
    ppermute x3, starting transfers between devices, along_y(): lax.ppermute(v, 'layer', [(i, (i + 8 * d) % LAYERS) for i in range(LAYERS)])  4.46 us
    ppermute x4, waiting for transfers between devices, along_z(): lax.ppermute(v, 'layer', [(i, i // 8 * 8 + move(i % 8) % 8) for i in rang...  4.2 us
    ppermute x3, waiting for transfers between devices, along_y(): lax.ppermute(v, 'layer', [(i, (i + 8 * d) % LAYERS) for i in range(LAYERS)])  3.38 us
    ppermute x6, waiting for transfers between devices, feat_step(): return lax.ppermute(v, 'feat', [(i, move(i) % FEATS) for i in range(FEATS)])  2.88 us
    pallas_call x1, Pallas kernels, pick(): pl.pallas_call(lambda *refs: pick_kernel(near, *refs), in_specs=[pl.Block...  2.81 us
    pallas_call x2, Pallas kernels, product(): pl.pallas_call(lambda *refs: product_kernel(last, *refs), in_specs=[pl.Bl...  2.73 us
  transfers between devices with their start and end apart: 13, of which 8 were waited for; matrix products, arithmetic and copies ran while one was open for 2% of the time, Pallas kernels for 7%

profile of v5, /device:TPU:1, one launch (start us, length us, event | category | flops | bytes accessed | tf_op | source)
XLA Modules:
  0.0 49.6 jit_solution(14269095821774871004)
XLA Ops:
  0.0 0.0 copy-start
  0.0 2.8 %pick_near.1 = (bf16[16,2304]{1,0:T(8,128)(2,1)S(1)}, bf16[16,2304]{1,0:T(8,128)(2,1)S(1)}, bf16[16,2304]{1,0:T(8,128)(2,1)S(1)}, bf16[128,128]{1,0:T(8,128)(2,1...) custom-call(s32[1,128]{1,0:T(1,128)} %bitcast.7, bf16[1024,2304]{1,0:T(8,128)(2,1)} %bitcast.4), custom_call_target="tpu_custom_call" | custom-call | flops 226492416 | bytes 4718592 | tf_op jit(solution)/shard_map/pick_near/pallas_call | solution.py:101
  2.8 2.6 %collective-permute-start.7 = (bf16[16,2304]{1,0:T(8,128)(2,1)S(1)}, bf16[16,2304]{1,0:T(8,128)(2,1)S(1)}, u32[]{:S(2)}, u32[]{:S(2)}) collective-permute-start(bf16[16,2304]{1,0:T(8,128)(2,1)S(1)} %get-tuple-element.39), channel_id=1, source_target_pairs={{0,1},{1,2},{2,3},{3,4},{4,5},{5,6},{6,7},{7,0},{8,9},{9,10},{10,1... | collective-permute-start | bytes 221192 | tf_op jit(solution)/shard_map/ppermute | solution.py:224
  5.4 0.7 %collective-permute-start.8 = (bf16[16,2304]{1,0:T(8,128)(2,1)S(1)}, bf16[16,2304]{1,0:T(8,128)(2,1)S(1)}, u32[]{:S(2)}, u32[]{:S(2)}) collective-permute-start(bf16[16,2304]{1,0:T(8,128)(2,1)S(1)} %get-tuple-element.40), channel_id=1, source_target_pairs={{0,7},{1,0},{2,1},{3,2},{4,3},{5,4},{6,5},{7,6},{8,15},{9,8},{10,9... | collective-permute-start | bytes 221192 | tf_op jit(solution)/shard_map/ppermute | solution.py:224
  6.1 0.0 copy-done
  6.1 0.2 convert_reduce_fusion
  6.3 0.7 %compare_reduce_fusion = pred[]{:T(512)} fusion(s32[7]{0:T(128)S(1)} %convert_reduce_fusion), kind=kLoop, calls=%fused_computation.26 | loop fusion | flops 41 | bytes 29 | tf_op jit(solution)/shard_map/reduce_and | solution.py:252
  7.6 0.0 collective-permute-done.7.up_ref
  7.6 1.6 %collective-permute-done.8.down_ref = bf16[16,2304]{1,0:T(8,128)(2,1)S(1)} collective-permute-done((bf16[16,2304]{1,0:T(8,128)(2,1)S(1)}, bf16[16,2304]{1,0:T(8,128)(2,1)S(1)}, u32[]{:S(2)}, u32[]{:S(2)}) %collective-permute-start.8) | collective-permute-done | bytes 73760 | tf_op jit(solution)/shard_map/ppermute | solution.py:224
  9.2 0.1 settle.1
  9.3 1.7 %collective-permute-start.9 = (bf16[16,2304]{1,0:T(8,128)(2,1)S(1)}, bf16[16,2304]{1,0:T(8,128)(2,1)S(1)}, u32[]{:S(2)}, u32[]{:S(2)}) collective-permute-start(bf16[16,2304]{1,0:T(8,128)(2,1)S(1)} %settle.1), channel_id=1, source_target_pairs={{0,8},{8,0},{16,24},{24,16},{32,40},{40,32},{48,56},{56,48},{64,72... | collective-permute-start | bytes 221192 | tf_op jit(solution)/shard_map/ppermute | solution.py:230
  11.0 1.7 %collective-permute-done.9 = bf16[16,2304]{1,0:T(8,128)(2,1)S(1)} collective-permute-done((bf16[16,2304]{1,0:T(8,128)(2,1)S(1)}, bf16[16,2304]{1,0:T(8,128)(2,1)S(1)}, u32[]{:S(2)}, u32[]{:S(2)}) %collective-permute-start.9) | collective-permute-done | bytes 73760 | tf_op jit(solution)/shard_map/ppermute | solution.py:230
  12.8 6.9 %collective-permute-start.10 = (bf16[16,2304]{1,0:T(8,128)(2,1)S(1)}, bf16[16,2304]{1,0:T(8,128)(2,1)S(1)}, u32[]{:S(2)}, u32[]{:S(2)}) collective-permute-start(bf16[16,2304]{1,0:T(8,128)(2,1)S(1)} %fusion.8), channel_id=1, source_target_pairs={{0,40},{8,32},{16,56},{24,48},{32,8},{40,0},{48,24},{56,16},{64,10... | collective-permute-start | bytes 221192 | tf_op jit(solution)/shard_map/ppermute | solution.py:230
  19.7 1.2 %collective-permute-start.11 = (bf16[16,2304]{1,0:T(8,128)(2,1)S(1)}, bf16[16,2304]{1,0:T(8,128)(2,1)S(1)}, u32[]{:S(2)}, u32[]{:S(2)}) collective-permute-start(bf16[16,2304]{1,0:T(8,128)(2,1)S(1)} %fusion.8), channel_id=1, source_target_pairs={{0,16},{8,24},{16,32},{24,40},{32,48},{40,56},{48,0},{56,8},{64,80... | collective-permute-start | bytes 221192 | tf_op jit(solution)/shard_map/ppermute | solution.py:230
  20.9 2.4 %collective-permute-start.12 = (bf16[16,2304]{1,0:T(8,128)(2,1)S(1)}, bf16[16,2304]{1,0:T(8,128)(2,1)S(1)}, u32[]{:S(2)}, u32[]{:S(2)}) collective-permute-start(bf16[16,2304]{1,0:T(8,128)(2,1)S(1)} %fusion.8), channel_id=1, source_target_pairs={{0,48},{8,56},{16,0},{24,8},{32,16},{40,24},{48,32},{56,40},{64,11... | collective-permute-start | bytes 221192 | tf_op jit(solution)/shard_map/ppermute | solution.py:230
  23.3 0.0 collective-permute-done.10
  23.3 2.0 %collective-permute-done.11 = bf16[16,2304]{1,0:T(8,128)(2,1)S(1)} collective-permute-done((bf16[16,2304]{1,0:T(8,128)(2,1)S(1)}, bf16[16,2304]{1,0:T(8,128)(2,1)S(1)}, u32[]{:S(2)}, u32[]{:S(2)}) %collective-permute-start.11) | collective-permute-done | bytes 73760 | tf_op jit(solution)/shard_map/ppermute | solution.py:230
  25.3 0.4 collective-permute-done.12
  25.7 0.1 fusion.7
  25.8 1.4 %collective-permute-start.13 = (bf16[16,2304]{1,0:T(8,128)(2,1)S(1)}, bf16[16,2304]{1,0:T(8,128)(2,1)S(1)}, u32[]{:S(2)}, u32[]{:S(2)}) collective-permute-start(bf16[16,2304]{1,0:T(8,128)(2,1)S(1)} %fusion.7), channel_id=1, source_target_pairs={{0,64},{8,72},{16,80},{24,88},{32,96},{40,104},{48,112},{56,120},{... | collective-permute-start | bytes 221192 | tf_op jit(solution)/shard_map/ppermute | solution.py:233
  27.1 1.5 %collective-permute-start.14 = (bf16[16,2304]{1,0:T(8,128)(2,1)S(1)}, bf16[16,2304]{1,0:T(8,128)(2,1)S(1)}, u32[]{:S(2)}, u32[]{:S(2)}) collective-permute-start(bf16[16,2304]{1,0:T(8,128)(2,1)S(1)} %fusion.7), channel_id=1, source_target_pairs={{0,192},{8,200},{16,208},{24,216},{32,224},{40,232},{48,240},{56,2... | collective-permute-start | bytes 221192 | tf_op jit(solution)/shard_map/ppermute | solution.py:233
  28.7 1.6 %collective-permute-start.15 = (bf16[16,2304]{1,0:T(8,128)(2,1)S(1)}, bf16[16,2304]{1,0:T(8,128)(2,1)S(1)}, u32[]{:S(2)}, u32[]{:S(2)}) collective-permute-start(bf16[16,2304]{1,0:T(8,128)(2,1)S(1)} %fusion.7), channel_id=1, source_target_pairs={{0,128},{8,136},{16,144},{24,152},{32,160},{40,168},{48,176},{56,1... | collective-permute-start | bytes 221192 | tf_op jit(solution)/shard_map/ppermute | solution.py:233
  30.2 0.1 collective-permute-done.13
  30.3 0.0 collective-permute-done.14
  30.4 3.3 %collective-permute-done.15 = bf16[16,2304]{1,0:T(8,128)(2,1)S(1)} collective-permute-done((bf16[16,2304]{1,0:T(8,128)(2,1)S(1)}, bf16[16,2304]{1,0:T(8,128)(2,1)S(1)}, u32[]{:S(2)}, u32[]{:S(2)}) %collective-permute-start.15) | collective-permute-done | bytes 73760 | tf_op jit(solution)/shard_map/ppermute | solution.py:233
  33.6 0.1 fusion.6.own_ref
  33.7 1.6 %collective-permute-start.16 = (bf16[16,2304]{1,0:T(8,128)(2,1)S(1)}, bf16[16,2304]{1,0:T(8,128)(2,1)S(1)}, u32[]{:S(2)}, u32[]{:S(2)}) collective-permute-start(bf16[16,2304]{1,0:T(8,128)(2,1)S(1)} %fusion.6.own_ref), channel_id=1, source_target_pairs={{0,2},{1,3},{2,4},{3,5},{4,6},{5,7},{6,0},{7,1},{8,10},{9,11},{10,... | collective-permute-start | bytes 221192 | tf_op jit(solution)/shard_map/ppermute | solution.py:224
  35.3 1.3 %collective-permute-start.17 = (bf16[16,2304]{1,0:T(8,128)(2,1)S(1)}, bf16[16,2304]{1,0:T(8,128)(2,1)S(1)}, u32[]{:S(2)}, u32[]{:S(2)}) collective-permute-start(bf16[16,2304]{1,0:T(8,128)(2,1)S(1)} %fusion.6.own_ref), channel_id=1, source_target_pairs={{0,6},{1,7},{2,0},{3,1},{4,2},{5,3},{6,4},{7,5},{8,14},{9,15},{10,... | collective-permute-start | bytes 221192 | tf_op jit(solution)/shard_map/ppermute | solution.py:224
  36.7 1.2 %collective-permute-start.18 = (bf16[16,2304]{1,0:T(8,128)(2,1)S(1)}, bf16[16,2304]{1,0:T(8,128)(2,1)S(1)}, u32[]{:S(2)}, u32[]{:S(2)}) collective-permute-start(bf16[16,2304]{1,0:T(8,128)(2,1)S(1)} %fusion.6.own_ref), channel_id=1, source_target_pairs={{0,4},{1,5},{2,6},{3,7},{4,0},{5,1},{6,2},{7,3},{8,12},{9,13},{10,... | collective-permute-start | bytes 221192 | tf_op jit(solution)/shard_map/ppermute | solution.py:224
  37.9 2.3 %fetch.1 = (bf16[2304,1024]{1,0:T(8,128)(2,1)S(1)}, bf16[16,2304]{1,0:T(8,128)(2,1)S(1)}) custom-call(bf16[16,2304]{1,0:T(8,128)(2,1)S(1)} %fusion.6.own_ref, bf16[2304,1024]{1,0:T(8,128)(2,1)} %bitcast.6), custom_call_target="tpu_custom_call" | custom-call | bytes 9437184 | tf_op jit(solution)/shard_map/fetch/pallas_call | solution.py:165
  40.3 0.0 collective-permute-done.16
  40.3 0.0 collective-permute-done.17
  40.4 1.0 %collective-permute-done.18 = bf16[16,2304]{1,0:T(8,128)(2,1)S(1)} collective-permute-done((bf16[16,2304]{1,0:T(8,128)(2,1)S(1)}, bf16[16,2304]{1,0:T(8,128)(2,1)S(1)}, u32[]{:S(2)}, u32[]{:S(2)}) %collective-permute-start.18) | collective-permute-done | bytes 73760 | tf_op jit(solution)/shard_map/ppermute | solution.py:224
  41.4 5.2 %collective-permute-start.19 = (bf16[64,2304]{1,0:T(8,128)(2,1)S(1)}, bf16[64,2304]{1,0:T(8,128)(2,1)S(1)}, u32[]{:S(2)}, u32[]{:S(2)}) collective-permute-start(bf16[64,2304]{1,0:T(8,128)(2,1)S(1)} %constant_dynamic-update-slice_fusion.refs_0_), channel_id=1, source_target_pairs={{0,1},{1,0},{2,3},{3,2},{4,5},{5,4},{6,7},{7,6},{8,9},{9,8},{10,11... | collective-permute-start | bytes 884744 | tf_op jit(solution)/shard_map/ppermute | solution.py:224
  46.6 0.9 %product_own.1.refs_2_ = bf16[64,1024]{1,0:T(8,128)(2,1)S(1)} custom-call(bf16[64,2304]{1,0:T(8,128)(2,1)S(1)} %constant_dynamic-update-slice_fusion.refs_0_, bf16[2304,1024]{1,0:T(8,128)(2,1)S(1)} %get-tuple-element.45.refs_1_), custom_call_target="tpu_custom_call" | custom-call | flops 301989888 | bytes 4718592 | tf_op jit(solution)/shard_map/product_own/pallas_call | solution.py:201
  47.5 0.3 collective-permute-done.19.refs_0_
  47.8 1.8 %product_last.1 = bf16[128,1024]{1,0:T(8,128)(2,1)} custom-call(bf16[64,2304]{1,0:T(8,128)(2,1)S(1)} %collective-permute-done.19.refs_0_, bf16[2304,1024]{1,0:T(8,128)(2,1)S(1)} %get-tuple-element.45.refs_1_, bf16[64,1024]{1,0:T(8,128)(2,1)S(1)} %product_own.1.refs_2_, bf16[128,128]{1,0:T(8,128)(2,1)S(1)} %get-tuple-element.46.refs_3_), custom_call_target="tpu_custom_call" | custom-call | flops 301989888 | bytes 4718592 | tf_op jit(solution)/shard_map/product_last/pallas_call | solution.py:201
  (9 shorter events, 0.1 us)
Async XLA Ops:
  0.0 6.1 %copy-start = (s32[128]{0:T(128)S(1)}, s32[128]{0:T(128)}, u32[]{:S(2)}) copy-start(s32[128]{0:T(128)} %param.7) | copy-start | bytes 1540
  2.8 4.8 %collective-permute-start.7 = (bf16[16,2304]{1,0:T(8,128)(2,1)S(1)}, bf16[16,2304]{1,0:T(8,128)(2,1)S(1)}, u32[]{:S(2)}, u32[]{:S(2)}) collective-permute-start(bf16[16,2304]{1,0:T(8,128)(2,1)S(1)} %get-tuple-element.39), channel_id=1, source_target_pairs={{0,1},{1,2},{2,3},{3,4},{4,5},{5,6},{6,7},{7,0},{8,9},{9,10},{10,1... | collective-permute-start | bytes 221192 | tf_op jit(solution)/shard_map/ppermute | solution.py:224
  5.4 3.8 %collective-permute-start.8 = (bf16[16,2304]{1,0:T(8,128)(2,1)S(1)}, bf16[16,2304]{1,0:T(8,128)(2,1)S(1)}, u32[]{:S(2)}, u32[]{:S(2)}) collective-permute-start(bf16[16,2304]{1,0:T(8,128)(2,1)S(1)} %get-tuple-element.40), channel_id=1, source_target_pairs={{0,7},{1,0},{2,1},{3,2},{4,3},{5,4},{6,5},{7,6},{8,15},{9,8},{10,9... | collective-permute-start | bytes 221192 | tf_op jit(solution)/shard_map/ppermute | solution.py:224
  9.3 3.5 %collective-permute-start.9 = (bf16[16,2304]{1,0:T(8,128)(2,1)S(1)}, bf16[16,2304]{1,0:T(8,128)(2,1)S(1)}, u32[]{:S(2)}, u32[]{:S(2)}) collective-permute-start(bf16[16,2304]{1,0:T(8,128)(2,1)S(1)} %settle.1), channel_id=1, source_target_pairs={{0,8},{8,0},{16,24},{24,16},{32,40},{40,32},{48,56},{56,48},{64,72... | collective-permute-start | bytes 221192 | tf_op jit(solution)/shard_map/ppermute | solution.py:230
  12.8 10.5 %collective-permute-start.10 = (bf16[16,2304]{1,0:T(8,128)(2,1)S(1)}, bf16[16,2304]{1,0:T(8,128)(2,1)S(1)}, u32[]{:S(2)}, u32[]{:S(2)}) collective-permute-start(bf16[16,2304]{1,0:T(8,128)(2,1)S(1)} %fusion.8), channel_id=1, source_target_pairs={{0,40},{8,32},{16,56},{24,48},{32,8},{40,0},{48,24},{56,16},{64,10... | collective-permute-start | bytes 221192 | tf_op jit(solution)/shard_map/ppermute | solution.py:230
  19.7 5.6 %collective-permute-start.11 = (bf16[16,2304]{1,0:T(8,128)(2,1)S(1)}, bf16[16,2304]{1,0:T(8,128)(2,1)S(1)}, u32[]{:S(2)}, u32[]{:S(2)}) collective-permute-start(bf16[16,2304]{1,0:T(8,128)(2,1)S(1)} %fusion.8), channel_id=1, source_target_pairs={{0,16},{8,24},{16,32},{24,40},{32,48},{40,56},{48,0},{56,8},{64,80... | collective-permute-start | bytes 221192 | tf_op jit(solution)/shard_map/ppermute | solution.py:230
  20.9 4.8 %collective-permute-start.12 = (bf16[16,2304]{1,0:T(8,128)(2,1)S(1)}, bf16[16,2304]{1,0:T(8,128)(2,1)S(1)}, u32[]{:S(2)}, u32[]{:S(2)}) collective-permute-start(bf16[16,2304]{1,0:T(8,128)(2,1)S(1)} %fusion.8), channel_id=1, source_target_pairs={{0,48},{8,56},{16,0},{24,8},{32,16},{40,24},{48,32},{56,40},{64,11... | collective-permute-start | bytes 221192 | tf_op jit(solution)/shard_map/ppermute | solution.py:230
  25.8 4.6 %collective-permute-start.13 = (bf16[16,2304]{1,0:T(8,128)(2,1)S(1)}, bf16[16,2304]{1,0:T(8,128)(2,1)S(1)}, u32[]{:S(2)}, u32[]{:S(2)}) collective-permute-start(bf16[16,2304]{1,0:T(8,128)(2,1)S(1)} %fusion.7), channel_id=1, source_target_pairs={{0,64},{8,72},{16,80},{24,88},{32,96},{40,104},{48,112},{56,120},{... | collective-permute-start | bytes 221192 | tf_op jit(solution)/shard_map/ppermute | solution.py:233
  27.1 3.2 %collective-permute-start.14 = (bf16[16,2304]{1,0:T(8,128)(2,1)S(1)}, bf16[16,2304]{1,0:T(8,128)(2,1)S(1)}, u32[]{:S(2)}, u32[]{:S(2)}) collective-permute-start(bf16[16,2304]{1,0:T(8,128)(2,1)S(1)} %fusion.7), channel_id=1, source_target_pairs={{0,192},{8,200},{16,208},{24,216},{32,224},{40,232},{48,240},{56,2... | collective-permute-start | bytes 221192 | tf_op jit(solution)/shard_map/ppermute | solution.py:233
  28.7 4.9 %collective-permute-start.15 = (bf16[16,2304]{1,0:T(8,128)(2,1)S(1)}, bf16[16,2304]{1,0:T(8,128)(2,1)S(1)}, u32[]{:S(2)}, u32[]{:S(2)}) collective-permute-start(bf16[16,2304]{1,0:T(8,128)(2,1)S(1)} %fusion.7), channel_id=1, source_target_pairs={{0,128},{8,136},{16,144},{24,152},{32,160},{40,168},{48,176},{56,1... | collective-permute-start | bytes 221192 | tf_op jit(solution)/shard_map/ppermute | solution.py:233
  33.7 6.6 %collective-permute-start.16 = (bf16[16,2304]{1,0:T(8,128)(2,1)S(1)}, bf16[16,2304]{1,0:T(8,128)(2,1)S(1)}, u32[]{:S(2)}, u32[]{:S(2)}) collective-permute-start(bf16[16,2304]{1,0:T(8,128)(2,1)S(1)} %fusion.6.own_ref), channel_id=1, source_target_pairs={{0,2},{1,3},{2,4},{3,5},{4,6},{5,7},{6,0},{7,1},{8,10},{9,11},{10,... | collective-permute-start | bytes 221192 | tf_op jit(solution)/shard_map/ppermute | solution.py:224
  35.3 5.0 %collective-permute-start.17 = (bf16[16,2304]{1,0:T(8,128)(2,1)S(1)}, bf16[16,2304]{1,0:T(8,128)(2,1)S(1)}, u32[]{:S(2)}, u32[]{:S(2)}) collective-permute-start(bf16[16,2304]{1,0:T(8,128)(2,1)S(1)} %fusion.6.own_ref), channel_id=1, source_target_pairs={{0,6},{1,7},{2,0},{3,1},{4,2},{5,3},{6,4},{7,5},{8,14},{9,15},{10,... | collective-permute-start | bytes 221192 | tf_op jit(solution)/shard_map/ppermute | solution.py:224
  36.7 4.7 %collective-permute-start.18 = (bf16[16,2304]{1,0:T(8,128)(2,1)S(1)}, bf16[16,2304]{1,0:T(8,128)(2,1)S(1)}, u32[]{:S(2)}, u32[]{:S(2)}) collective-permute-start(bf16[16,2304]{1,0:T(8,128)(2,1)S(1)} %fusion.6.own_ref), channel_id=1, source_target_pairs={{0,4},{1,5},{2,6},{3,7},{4,0},{5,1},{6,2},{7,3},{8,12},{9,13},{10,... | collective-permute-start | bytes 221192 | tf_op jit(solution)/shard_map/ppermute | solution.py:224
  41.4 6.4 %collective-permute-start.19 = (bf16[64,2304]{1,0:T(8,128)(2,1)S(1)}, bf16[64,2304]{1,0:T(8,128)(2,1)S(1)}, u32[]{:S(2)}, u32[]{:S(2)}) collective-permute-start(bf16[64,2304]{1,0:T(8,128)(2,1)S(1)} %constant_dynamic-update-slice_fusion.refs_0_), channel_id=1, source_target_pairs={{0,1},{1,0},{2,3},{3,2},{4,5},{5,4},{6,7},{7,6},{8,9},{9,8},{10,11... | collective-permute-start | bytes 884744 | tf_op jit(solution)/shard_map/ppermute | solution.py:224

commit v6 on v5

--- a/solution.py
+++ b/solution.py
@@ -217,20 +217,17 @@
     share = k // FEATS
     listed = pltpu.with_memory_space_constraint(chosen.reshape(1, k), pltpu.HBM)
     feat, layer = lax.axis_index("feat"), lax.axis_index("layer")
-    x = feat // 2
+    x, core = feat // 2, feat % 2
     y, z = layer // 8, layer % 8
 
     def feat_step(v, move):
         return lax.ppermute(v, "feat", [(i, move(i) % FEATS) for i in range(FEATS)])
 
     def along_x(v, d):
-        return feat_step(v, lambda i: i + 2 * d)
-
-    def along_z(v, move):
-        return lax.ppermute(v, "layer", [(i, i // 8 * 8 + move(i % 8) % 8) for i in range(LAYERS)])
-
-    def along_y(v, d):
-        return lax.ppermute(v, "layer", [(i, (i + 8 * d) % LAYERS) for i in range(LAYERS)])
+        return feat_step(v, lambda i: i ^ (2 * d))
+
+    def along_z(v, d):
+        return lax.ppermute(v, "layer", [(i, i ^ d) for i in range(LAYERS)])
 
     below, own, above, order, far, room = pick(listed, dec, True)
     up = feat_step(above, lambda i: i + 1)
@@ -262,22 +259,41 @@
             total = total + v
         return before, total
 
-    before, total = join([(z % 2 == 1, along_z(total.astype(BF), lambda i: i ^ 1))], before, total)
     low = total.astype(BF)
-    up = along_z(low, lambda i: i + 2)
-    down = along_z(low, lambda i: i - 2)
-    across = along_z(low, lambda i: i + 3 if i % 2 else i - 3)
-    before, total = join([(z >= 4, across), (z >= 2, up), (z >= 6, down)], before, total)
-    low = total.astype(BF)
-    arrivals = [(y >= d, along_y(low, d)) for d in (1, 3, 2)]
+    arrivals = [((z ^ d) < z, along_z(low, d)) for d in (1,)]
     before, total = join(arrivals, before, total)
-    prefix = before.astype(BF)
-
-    pieces = [along_x(prefix, d) for d in (1, 3, 2)]
+    def crossed(v, dy, dz, first):
+        pairs = []
+        for layer in range(LAYERS):
+            for f in range(FEATS):
+                to = layer ^ dz if (f % 2 == 1) == first else layer ^ (8 * dy)
+                pairs.append((layer * FEATS + f, to * FEATS + f))
+        return lax.ppermute(v, ("layer", "feat"), pairs)
+
+    ways = tuple(zip((2, 3, 1), (5, 7, 2)))
+    pair = total
+    low = pair.astype(BF)
+    for dy, dz in ways:
+        v = crossed(low, dy, dz, True).astype(F32)
+        lower = jnp.where(core == 1, (z ^ dz) < z, (y ^ dy) < y)
+        if dy == 2:
+            masked = jnp.where(lower, v, 0.0)
+        else:
+            masked = masked + jnp.where(lower, v, 0.0)
+        total = total + v
+    before = before + masked
+    prefix = before
+    for dy, dz in ways:
+        out = jnp.where(core == 1, total, masked + jnp.where(z < (z ^ dz), pair, 0.0))
+        v = crossed(out.astype(BF), dy, dz, False).astype(F32)
+        prefix = prefix + jnp.where((core == 0) | ((y ^ dy) < y), v, 0.0)
+    prefix = prefix.astype(BF)
+
+    pieces = [along_x(prefix, d) for d in (3, 2, 1)]
     near, prefix = fetch(prefix, enc)
     whole = jnp.zeros((k // 2, prefix.shape[1]), BF)
-    for d, piece in zip((0, 1, 3, 2), [prefix] + pieces):
-        whole = lax.dynamic_update_slice_in_dim(whole, piece, share * ((x + 4 - d) % 4), 0)
+    for d, piece in zip((0,) + (3, 2, 1), [prefix] + pieces):
+        whole = lax.dynamic_update_slice_in_dim(whole, piece, share * (x ^ d), 0)
     other = feat_step(whole, lambda i: i ^ 1)
     return product(other, near, product(whole, near), order)[None]
 

time: 49.7 us -> 46.2 us (0.930)
  starting transfers between devices: 29.3 us -> 24.5 us
  waiting for transfers between devices: 10.5 us -> 11.5 us
    ppermute x7, starting transfers between devices: 16.7 us -> 13.7 us  [the longest x6 12 us: crossed(): return lax.ppermute(v, ('layer', 'feat'), pairs)]
    ppermute x6, starting transfers between devices: 12.6 us -> 10.9 us  [feat_step(): return lax.ppermute(v, 'feat', [(i, move(i) % FEATS) for i in range(FEATS)])]
    ppermute x7, waiting for transfers between devices: 7.58 us -> 8.69 us  [the longest x6 6.95 us: crossed(): return lax.ppermute(v, ('layer', 'feat'), pairs)]
where the time goes in v6:
time: 46.2 us; the launch traced here: 46 us
  starting transfers between devices  24.5 us (53%)
  waiting for transfers between devices  11.5 us (25%)
  Pallas kernels  7.95 us (17%)
  other arithmetic  1.14 us (2%)
  between operations  0.75 us (2%)
    ppermute x6, starting transfers between devices, crossed(): return lax.ppermute(v, ('layer', 'feat'), pairs)  12 us
    ppermute x6, starting transfers between devices, feat_step(): return lax.ppermute(v, 'feat', [(i, move(i) % FEATS) for i in range(FEATS)])  10.9 us
    ppermute x6, waiting for transfers between devices, crossed(): return lax.ppermute(v, ('layer', 'feat'), pairs)  6.95 us
    ppermute x6, waiting for transfers between devices, feat_step(): return lax.ppermute(v, 'feat', [(i, move(i) % FEATS) for i in range(FEATS)])  2.84 us
    pallas_call x1, Pallas kernels, pick(): pl.pallas_call(lambda *refs: pick_kernel(near, *refs), in_specs=[pl.Block...  2.81 us
    pallas_call x2, Pallas kernels, product(): pl.pallas_call(lambda *refs: product_kernel(last, *refs), in_specs=[pl.Bl...  2.73 us
    pallas_call x1, Pallas kernels, fetch(): pl.pallas_call(fetch_kernel, in_specs=[pl.BlockSpec(memory_space=pltpu.VM...  2.34 us
    ppermute x1, waiting for transfers between devices, along_z(): return lax.ppermute(v, 'layer', [(i, i ^ d) for i in range(LAYERS)])  1.74 us
  transfers between devices with their start and end apart: 13, of which 8 were waited for; matrix products, arithmetic and copies ran while one was open for 2% of the time, Pallas kernels for 7%

profile of v6, /device:TPU:1, one launch (start us, length us, event | category | flops | bytes accessed | tf_op | source)
XLA Modules:
  0.0 46.0 jit_solution(17877909207798025798)
XLA Ops:
  0.0 0.0 copy-start
  0.0 2.8 %pick_near.1 = (bf16[16,2304]{1,0:T(8,128)(2,1)S(1)}, bf16[16,2304]{1,0:T(8,128)(2,1)S(1)}, bf16[16,2304]{1,0:T(8,128)(2,1)S(1)}, bf16[128,128]{1,0:T(8,128)(2,1...) custom-call(s32[1,128]{1,0:T(1,128)} %bitcast.7, bf16[1024,2304]{1,0:T(8,128)(2,1)} %bitcast.4), custom_call_target="tpu_custom_call" | custom-call | flops 226492416 | bytes 4718592 | tf_op jit(solution)/shard_map/pick_near/pallas_call | solution.py:101
  2.8 2.6 %collective-permute-start.7 = (bf16[16,2304]{1,0:T(8,128)(2,1)S(1)}, bf16[16,2304]{1,0:T(8,128)(2,1)S(1)}, u32[]{:S(2)}, u32[]{:S(2)}) collective-permute-start(bf16[16,2304]{1,0:T(8,128)(2,1)S(1)} %get-tuple-element.39), channel_id=1, source_target_pairs={{0,1},{1,2},{2,3},{3,4},{4,5},{5,6},{6,7},{7,0},{8,9},{9,10},{10,1... | collective-permute-start | bytes 221192 | tf_op jit(solution)/shard_map/ppermute | solution.py:224
  5.4 0.7 %collective-permute-start.8 = (bf16[16,2304]{1,0:T(8,128)(2,1)S(1)}, bf16[16,2304]{1,0:T(8,128)(2,1)S(1)}, u32[]{:S(2)}, u32[]{:S(2)}) collective-permute-start(bf16[16,2304]{1,0:T(8,128)(2,1)S(1)} %get-tuple-element.40), channel_id=1, source_target_pairs={{0,7},{1,0},{2,1},{3,2},{4,3},{5,4},{6,5},{7,6},{8,15},{9,8},{10,9... | collective-permute-start | bytes 221192 | tf_op jit(solution)/shard_map/ppermute | solution.py:224
  6.1 0.0 copy-done
  6.1 0.2 convert_reduce_fusion
  6.3 0.7 %compare_reduce_fusion = pred[]{:T(512)} fusion(s32[7]{0:T(128)S(1)} %convert_reduce_fusion), kind=kLoop, calls=%fused_computation.28 | loop fusion | flops 41 | bytes 29 | tf_op jit(solution)/shard_map/reduce_and | solution.py:249
  7.6 0.0 collective-permute-done.7.up_ref
  7.6 1.6 %collective-permute-done.8.down_ref = bf16[16,2304]{1,0:T(8,128)(2,1)S(1)} collective-permute-done((bf16[16,2304]{1,0:T(8,128)(2,1)S(1)}, bf16[16,2304]{1,0:T(8,128)(2,1)S(1)}, u32[]{:S(2)}, u32[]{:S(2)}) %collective-permute-start.8) | collective-permute-done | bytes 73760 | tf_op jit(solution)/shard_map/ppermute | solution.py:224
  9.2 0.1 settle.1
  9.3 1.7 %collective-permute-start.9 = (bf16[16,2304]{1,0:T(8,128)(2,1)S(1)}, bf16[16,2304]{1,0:T(8,128)(2,1)S(1)}, u32[]{:S(2)}, u32[]{:S(2)}) collective-permute-start(bf16[16,2304]{1,0:T(8,128)(2,1)S(1)} %settle.1), channel_id=1, source_target_pairs={{0,8},{8,0},{16,24},{24,16},{32,40},{40,32},{48,56},{56,48},{64,72... | collective-permute-start | bytes 221192 | tf_op jit(solution)/shard_map/ppermute | solution.py:230
  11.0 1.7 %collective-permute-done.9 = bf16[16,2304]{1,0:T(8,128)(2,1)S(1)} collective-permute-done((bf16[16,2304]{1,0:T(8,128)(2,1)S(1)}, bf16[16,2304]{1,0:T(8,128)(2,1)S(1)}, u32[]{:S(2)}, u32[]{:S(2)}) %collective-permute-start.9) | collective-permute-done | bytes 73760 | tf_op jit(solution)/shard_map/ppermute | solution.py:230
  12.8 6.9 %collective-permute-start.10 = (bf16[16,2304]{1,0:T(8,128)(2,1)S(1)}, bf16[16,2304]{1,0:T(8,128)(2,1)S(1)}, u32[]{:S(2)}, u32[]{:S(2)}) collective-permute-start(bf16[16,2304]{1,0:T(8,128)(2,1)S(1)} %fusion.7), channel_id=1, source_target_pairs={{0,128},{1,41},{2,130},{3,43},{4,132},{5,45},{6,134},{7,47},{8,136... | collective-permute-start | bytes 221192 | tf_op jit(solution)/shard_map/ppermute | solution.py:271
  19.7 0.0 collective-permute-start.11
  19.7 1.3 %collective-permute-start.12 = (bf16[16,2304]{1,0:T(8,128)(2,1)S(1)}, bf16[16,2304]{1,0:T(8,128)(2,1)S(1)}, u32[]{:S(2)}, u32[]{:S(2)}) collective-permute-start(bf16[16,2304]{1,0:T(8,128)(2,1)S(1)} %fusion.7), channel_id=1, source_target_pairs={{0,64},{1,17},{2,66},{3,19},{4,68},{5,21},{6,70},{7,23},{8,72},{9,... | collective-permute-start | bytes 221192 | tf_op jit(solution)/shard_map/ppermute | solution.py:271
  21.0 0.5 %collective-permute-done.10 = bf16[16,2304]{1,0:T(8,128)(2,1)S(1)} collective-permute-done((bf16[16,2304]{1,0:T(8,128)(2,1)S(1)}, bf16[16,2304]{1,0:T(8,128)(2,1)S(1)}, u32[]{:S(2)}, u32[]{:S(2)}) %collective-permute-start.10) | collective-permute-done | bytes 73760 | tf_op jit(solution)/shard_map/ppermute | solution.py:271
  21.5 2.6 %collective-permute-done.11 = bf16[16,2304]{1,0:T(8,128)(2,1)S(1)} collective-permute-done((bf16[16,2304]{1,0:T(8,128)(2,1)S(1)}, bf16[16,2304]{1,0:T(8,128)(2,1)S(1)}, u32[]{:S(2)}, u32[]{:S(2)}) %collective-permute-start.11) | collective-permute-done | bytes 73760 | tf_op jit(solution)/shard_map/ppermute | solution.py:271
  24.1 0.0 collective-permute-done.12
  24.1 0.1 select_convert_fusion.2
  24.2 3.0 %collective-permute-start.13 = (bf16[16,2304]{1,0:T(8,128)(2,1)S(1)}, bf16[16,2304]{1,0:T(8,128)(2,1)S(1)}, u32[]{:S(2)}, u32[]{:S(2)}) collective-permute-start(bf16[16,2304]{1,0:T(8,128)(2,1)S(1)} %get-tuple-element.64), channel_id=1, source_target_pairs={{0,40},{1,129},{2,42},{3,131},{4,44},{5,133},{6,46},{7,135},{8,32}... | collective-permute-start | bytes 221192 | tf_op jit(solution)/shard_map/ppermute | solution.py:271
  27.2 0.8 %collective-permute-start.14 = (bf16[16,2304]{1,0:T(8,128)(2,1)S(1)}, bf16[16,2304]{1,0:T(8,128)(2,1)S(1)}, u32[]{:S(2)}, u32[]{:S(2)}) collective-permute-start(bf16[16,2304]{1,0:T(8,128)(2,1)S(1)} %get-tuple-element.65), channel_id=1, source_target_pairs={{0,56},{1,193},{2,58},{3,195},{4,60},{5,197},{6,62},{7,199},{8,48}... | collective-permute-start | bytes 221192 | tf_op jit(solution)/shard_map/ppermute | solution.py:271
  28.0 0.0 collective-permute-start.15
  28.0 1.0 %collective-permute-done.13 = bf16[16,2304]{1,0:T(8,128)(2,1)S(1)} collective-permute-done((bf16[16,2304]{1,0:T(8,128)(2,1)S(1)}, bf16[16,2304]{1,0:T(8,128)(2,1)S(1)}, u32[]{:S(2)}, u32[]{:S(2)}) %collective-permute-start.13) | collective-permute-done | bytes 73760 | tf_op jit(solution)/shard_map/ppermute | solution.py:271
  29.0 2.8 %collective-permute-done.14 = bf16[16,2304]{1,0:T(8,128)(2,1)S(1)} collective-permute-done((bf16[16,2304]{1,0:T(8,128)(2,1)S(1)}, bf16[16,2304]{1,0:T(8,128)(2,1)S(1)}, u32[]{:S(2)}, u32[]{:S(2)}) %collective-permute-start.14) | collective-permute-done | bytes 73760 | tf_op jit(solution)/shard_map/ppermute | solution.py:271
  31.8 0.0 collective-permute-done.15
  31.8 0.1 fusion.4.own_ref
  31.9 2.0 %collective-permute-start.16 = (bf16[16,2304]{1,0:T(8,128)(2,1)S(1)}, bf16[16,2304]{1,0:T(8,128)(2,1)S(1)}, u32[]{:S(2)}, u32[]{:S(2)}) collective-permute-start(bf16[16,2304]{1,0:T(8,128)(2,1)S(1)} %fusion.4.own_ref), channel_id=1, source_target_pairs={{0,6},{1,7},{2,4},{3,5},{4,2},{5,3},{6,0},{7,1},{8,14},{9,15},{10,... | collective-permute-start | bytes 221192 | tf_op jit(solution)/shard_map/ppermute | solution.py:224
  34.0 0.5 %collective-permute-start.17 = (bf16[16,2304]{1,0:T(8,128)(2,1)S(1)}, bf16[16,2304]{1,0:T(8,128)(2,1)S(1)}, u32[]{:S(2)}, u32[]{:S(2)}) collective-permute-start(bf16[16,2304]{1,0:T(8,128)(2,1)S(1)} %fusion.4.own_ref), channel_id=1, source_target_pairs={{0,4},{1,5},{2,6},{3,7},{4,0},{5,1},{6,2},{7,3},{8,12},{9,13},{10,... | collective-permute-start | bytes 221192 | tf_op jit(solution)/shard_map/ppermute | solution.py:224
  34.5 0.8 %collective-permute-start.18 = (bf16[16,2304]{1,0:T(8,128)(2,1)S(1)}, bf16[16,2304]{1,0:T(8,128)(2,1)S(1)}, u32[]{:S(2)}, u32[]{:S(2)}) collective-permute-start(bf16[16,2304]{1,0:T(8,128)(2,1)S(1)} %fusion.4.own_ref), channel_id=1, source_target_pairs={{0,2},{1,3},{2,0},{3,1},{4,6},{5,7},{6,4},{7,5},{8,10},{9,11},{10,... | collective-permute-start | bytes 221192 | tf_op jit(solution)/shard_map/ppermute | solution.py:224
  35.3 2.3 %fetch.1 = (bf16[2304,1024]{1,0:T(8,128)(2,1)S(1)}, bf16[16,2304]{1,0:T(8,128)(2,1)S(1)}) custom-call(bf16[16,2304]{1,0:T(8,128)(2,1)S(1)} %fusion.4.own_ref, bf16[2304,1024]{1,0:T(8,128)(2,1)} %bitcast.6), custom_call_target="tpu_custom_call" | custom-call | bytes 9437184 | tf_op jit(solution)/shard_map/fetch/pallas_call | solution.py:165
  37.7 0.0 collective-permute-done.16
  37.7 1.0 %collective-permute-done.17 = bf16[16,2304]{1,0:T(8,128)(2,1)S(1)} collective-permute-done((bf16[16,2304]{1,0:T(8,128)(2,1)S(1)}, bf16[16,2304]{1,0:T(8,128)(2,1)S(1)}, u32[]{:S(2)}, u32[]{:S(2)}) %collective-permute-start.17) | collective-permute-done | bytes 73760 | tf_op jit(solution)/shard_map/ppermute | solution.py:224
  38.7 0.0 collective-permute-done.18
  38.7 4.2 %collective-permute-start.19 = (bf16[64,2304]{1,0:T(8,128)(2,1)S(1)}, bf16[64,2304]{1,0:T(8,128)(2,1)S(1)}, u32[]{:S(2)}, u32[]{:S(2)}) collective-permute-start(bf16[64,2304]{1,0:T(8,128)(2,1)S(1)} %constant_dynamic-update-slice_fusion.refs_0_), channel_id=1, source_target_pairs={{0,1},{1,0},{2,3},{3,2},{4,5},{5,4},{6,7},{7,6},{8,9},{9,8},{10,11... | collective-permute-start | bytes 884744 | tf_op jit(solution)/shard_map/ppermute | solution.py:224
  43.0 0.9 %product_own.1.refs_2_ = bf16[64,1024]{1,0:T(8,128)(2,1)S(1)} custom-call(bf16[64,2304]{1,0:T(8,128)(2,1)S(1)} %constant_dynamic-update-slice_fusion.refs_0_, bf16[2304,1024]{1,0:T(8,128)(2,1)S(1)} %get-tuple-element.45.refs_1_), custom_call_target="tpu_custom_call" | custom-call | flops 301989888 | bytes 4718592 | tf_op jit(solution)/shard_map/product_own/pallas_call | solution.py:201
  43.9 0.3 collective-permute-done.19.refs_0_
  44.2 1.8 %product_last.1 = bf16[128,1024]{1,0:T(8,128)(2,1)} custom-call(bf16[64,2304]{1,0:T(8,128)(2,1)S(1)} %collective-permute-done.19.refs_0_, bf16[2304,1024]{1,0:T(8,128)(2,1)S(1)} %get-tuple-element.45.refs_1_, bf16[64,1024]{1,0:T(8,128)(2,1)S(1)} %product_own.1.refs_2_, bf16[128,128]{1,0:T(8,128)(2,1)S(1)} %get-tuple-element.46.refs_3_), custom_call_target="tpu_custom_call" | custom-call | flops 301989888 | bytes 4718592 | tf_op jit(solution)/shard_map/product_last/pallas_call | solution.py:201
  (9 shorter events, 0.1 us)
Async XLA Ops:
  0.0 6.1 %copy-start = (s32[128]{0:T(128)S(1)}, s32[128]{0:T(128)}, u32[]{:S(2)}) copy-start(s32[128]{0:T(128)} %param.7) | copy-start | bytes 1540
  2.8 4.8 %collective-permute-start.7 = (bf16[16,2304]{1,0:T(8,128)(2,1)S(1)}, bf16[16,2304]{1,0:T(8,128)(2,1)S(1)}, u32[]{:S(2)}, u32[]{:S(2)}) collective-permute-start(bf16[16,2304]{1,0:T(8,128)(2,1)S(1)} %get-tuple-element.39), channel_id=1, source_target_pairs={{0,1},{1,2},{2,3},{3,4},{4,5},{5,6},{6,7},{7,0},{8,9},{9,10},{10,1... | collective-permute-start | bytes 221192 | tf_op jit(solution)/shard_map/ppermute | solution.py:224
  5.4 3.8 %collective-permute-start.8 = (bf16[16,2304]{1,0:T(8,128)(2,1)S(1)}, bf16[16,2304]{1,0:T(8,128)(2,1)S(1)}, u32[]{:S(2)}, u32[]{:S(2)}) collective-permute-start(bf16[16,2304]{1,0:T(8,128)(2,1)S(1)} %get-tuple-element.40), channel_id=1, source_target_pairs={{0,7},{1,0},{2,1},{3,2},{4,3},{5,4},{6,5},{7,6},{8,15},{9,8},{10,9... | collective-permute-start | bytes 221192 | tf_op jit(solution)/shard_map/ppermute | solution.py:224
  9.3 3.5 %collective-permute-start.9 = (bf16[16,2304]{1,0:T(8,128)(2,1)S(1)}, bf16[16,2304]{1,0:T(8,128)(2,1)S(1)}, u32[]{:S(2)}, u32[]{:S(2)}) collective-permute-start(bf16[16,2304]{1,0:T(8,128)(2,1)S(1)} %settle.1), channel_id=1, source_target_pairs={{0,8},{8,0},{16,24},{24,16},{32,40},{40,32},{48,56},{56,48},{64,72... | collective-permute-start | bytes 221192 | tf_op jit(solution)/shard_map/ppermute | solution.py:230
  12.8 8.7 %collective-permute-start.10 = (bf16[16,2304]{1,0:T(8,128)(2,1)S(1)}, bf16[16,2304]{1,0:T(8,128)(2,1)S(1)}, u32[]{:S(2)}, u32[]{:S(2)}) collective-permute-start(bf16[16,2304]{1,0:T(8,128)(2,1)S(1)} %fusion.7), channel_id=1, source_target_pairs={{0,128},{1,41},{2,130},{3,43},{4,132},{5,45},{6,134},{7,47},{8,136... | collective-permute-start | bytes 221192 | tf_op jit(solution)/shard_map/ppermute | solution.py:271
  19.7 4.4 %collective-permute-start.11 = (bf16[16,2304]{1,0:T(8,128)(2,1)S(1)}, bf16[16,2304]{1,0:T(8,128)(2,1)S(1)}, u32[]{:S(2)}, u32[]{:S(2)}) collective-permute-start(bf16[16,2304]{1,0:T(8,128)(2,1)S(1)} %fusion.7), channel_id=1, source_target_pairs={{0,192},{1,57},{2,194},{3,59},{4,196},{5,61},{6,198},{7,63},{8,200... | collective-permute-start | bytes 221192 | tf_op jit(solution)/shard_map/ppermute | solution.py:271
  19.7 4.4 %collective-permute-start.12 = (bf16[16,2304]{1,0:T(8,128)(2,1)S(1)}, bf16[16,2304]{1,0:T(8,128)(2,1)S(1)}, u32[]{:S(2)}, u32[]{:S(2)}) collective-permute-start(bf16[16,2304]{1,0:T(8,128)(2,1)S(1)} %fusion.7), channel_id=1, source_target_pairs={{0,64},{1,17},{2,66},{3,19},{4,68},{5,21},{6,70},{7,23},{8,72},{9,... | collective-permute-start | bytes 221192 | tf_op jit(solution)/shard_map/ppermute | solution.py:271
  24.2 4.8 %collective-permute-start.13 = (bf16[16,2304]{1,0:T(8,128)(2,1)S(1)}, bf16[16,2304]{1,0:T(8,128)(2,1)S(1)}, u32[]{:S(2)}, u32[]{:S(2)}) collective-permute-start(bf16[16,2304]{1,0:T(8,128)(2,1)S(1)} %get-tuple-element.64), channel_id=1, source_target_pairs={{0,40},{1,129},{2,42},{3,131},{4,44},{5,133},{6,46},{7,135},{8,32}... | collective-permute-start | bytes 221192 | tf_op jit(solution)/shard_map/ppermute | solution.py:271
  27.2 4.6 %collective-permute-start.14 = (bf16[16,2304]{1,0:T(8,128)(2,1)S(1)}, bf16[16,2304]{1,0:T(8,128)(2,1)S(1)}, u32[]{:S(2)}, u32[]{:S(2)}) collective-permute-start(bf16[16,2304]{1,0:T(8,128)(2,1)S(1)} %get-tuple-element.65), channel_id=1, source_target_pairs={{0,56},{1,193},{2,58},{3,195},{4,60},{5,197},{6,62},{7,199},{8,48}... | collective-permute-start | bytes 221192 | tf_op jit(solution)/shard_map/ppermute | solution.py:271
  28.0 3.8 %collective-permute-start.15 = (bf16[16,2304]{1,0:T(8,128)(2,1)S(1)}, bf16[16,2304]{1,0:T(8,128)(2,1)S(1)}, u32[]{:S(2)}, u32[]{:S(2)}) collective-permute-start(bf16[16,2304]{1,0:T(8,128)(2,1)S(1)} %get-tuple-element.66), channel_id=1, source_target_pairs={{0,16},{1,65},{2,18},{3,67},{4,20},{5,69},{6,22},{7,71},{8,24},{9,... | collective-permute-start | bytes 221192 | tf_op jit(solution)/shard_map/ppermute | solution.py:271
  31.9 5.7 %collective-permute-start.16 = (bf16[16,2304]{1,0:T(8,128)(2,1)S(1)}, bf16[16,2304]{1,0:T(8,128)(2,1)S(1)}, u32[]{:S(2)}, u32[]{:S(2)}) collective-permute-start(bf16[16,2304]{1,0:T(8,128)(2,1)S(1)} %fusion.4.own_ref), channel_id=1, source_target_pairs={{0,6},{1,7},{2,4},{3,5},{4,2},{5,3},{6,0},{7,1},{8,14},{9,15},{10,... | collective-permute-start | bytes 221192 | tf_op jit(solution)/shard_map/ppermute | solution.py:224
  34.0 4.7 %collective-permute-start.17 = (bf16[16,2304]{1,0:T(8,128)(2,1)S(1)}, bf16[16,2304]{1,0:T(8,128)(2,1)S(1)}, u32[]{:S(2)}, u32[]{:S(2)}) collective-permute-start(bf16[16,2304]{1,0:T(8,128)(2,1)S(1)} %fusion.4.own_ref), channel_id=1, source_target_pairs={{0,4},{1,5},{2,6},{3,7},{4,0},{5,1},{6,2},{7,3},{8,12},{9,13},{10,... | collective-permute-start | bytes 221192 | tf_op jit(solution)/shard_map/ppermute | solution.py:224
  34.5 4.2 %collective-permute-start.18 = (bf16[16,2304]{1,0:T(8,128)(2,1)S(1)}, bf16[16,2304]{1,0:T(8,128)(2,1)S(1)}, u32[]{:S(2)}, u32[]{:S(2)}) collective-permute-start(bf16[16,2304]{1,0:T(8,128)(2,1)S(1)} %fusion.4.own_ref), channel_id=1, source_target_pairs={{0,2},{1,3},{2,0},{3,1},{4,6},{5,7},{6,4},{7,5},{8,10},{9,11},{10,... | collective-permute-start | bytes 221192 | tf_op jit(solution)/shard_map/ppermute | solution.py:224
  38.7 5.4 %collective-permute-start.19 = (bf16[64,2304]{1,0:T(8,128)(2,1)S(1)}, bf16[64,2304]{1,0:T(8,128)(2,1)S(1)}, u32[]{:S(2)}, u32[]{:S(2)}) collective-permute-start(bf16[64,2304]{1,0:T(8,128)(2,1)S(1)} %constant_dynamic-update-slice_fusion.refs_0_), channel_id=1, source_target_pairs={{0,1},{1,0},{2,3},{3,2},{4,5},{5,4},{6,7},{7,6},{8,9},{9,8},{10,11... | collective-permute-start | bytes 884744 | tf_op jit(solution)/shard_map/ppermute | solution.py:224

commit v7 on v6

--- a/solution.py
+++ b/solution.py
@@ -270,7 +270,7 @@
                 pairs.append((layer * FEATS + f, to * FEATS + f))
         return lax.ppermute(v, ("layer", "feat"), pairs)
 
-    ways = tuple(zip((2, 3, 1), (5, 7, 2)))
+    ways = ((2, 5), (3, 7), (1, 2))
     pair = total
     low = pair.astype(BF)
     for dy, dz in ways:
@@ -283,7 +283,7 @@
         total = total + v
     before = before + masked
     prefix = before
-    for dy, dz in ways:
+    for dy, dz in ((3, 5), (2, 7), (1, 2)):
         out = jnp.where(core == 1, total, masked + jnp.where(z < (z ^ dz), pair, 0.0))
         v = crossed(out.astype(BF), dy, dz, False).astype(F32)
         prefix = prefix + jnp.where((core == 0) | ((y ^ dy) < y), v, 0.0)

time: 46.2 us -> 46.2 us (level)
  no operation moved by 1% of the time
where the time goes in v7:
time: 46.2 us; the launch traced here: 46 us
  starting transfers between devices  24.2 us (52%)
  waiting for transfers between devices  11.9 us (26%)
  Pallas kernels  7.95 us (17%)
  other arithmetic  1.14 us (2%)
  between operations  0.75 us (2%)
    ppermute x6, starting transfers between devices, crossed(): return lax.ppermute(v, ('layer', 'feat'), pairs)  11.7 us
    ppermute x6, starting transfers between devices, feat_step(): return lax.ppermute(v, 'feat', [(i, move(i) % FEATS) for i in range(FEATS)])  10.7 us
    ppermute x6, waiting for transfers between devices, crossed(): return lax.ppermute(v, ('layer', 'feat'), pairs)  7.23 us
    ppermute x6, waiting for transfers between devices, feat_step(): return lax.ppermute(v, 'feat', [(i, move(i) % FEATS) for i in range(FEATS)])  2.96 us
    pallas_call x1, Pallas kernels, pick(): pl.pallas_call(lambda *refs: pick_kernel(near, *refs), in_specs=[pl.Block...  2.81 us
    pallas_call x2, Pallas kernels, product(): pl.pallas_call(lambda *refs: product_kernel(last, *refs), in_specs=[pl.Bl...  2.73 us
    pallas_call x1, Pallas kernels, fetch(): pl.pallas_call(fetch_kernel, in_specs=[pl.BlockSpec(memory_space=pltpu.VM...  2.34 us
    ppermute x1, waiting for transfers between devices, along_z(): return lax.ppermute(v, 'layer', [(i, i ^ d) for i in range(LAYERS)])  1.74 us
  transfers between devices with their start and end apart: 13, of which 8 were waited for; matrix products, arithmetic and copies ran while one was open for 2% of the time, Pallas kernels for 7%

profile of v7, /device:TPU:1, one launch (start us, length us, event | category | flops | bytes accessed | tf_op | source)
XLA Modules:
  0.0 46.0 jit_solution(11977227933201141534)
XLA Ops:
  0.0 0.0 copy-start
  0.0 2.8 %pick_near.1 = (bf16[16,2304]{1,0:T(8,128)(2,1)S(1)}, bf16[16,2304]{1,0:T(8,128)(2,1)S(1)}, bf16[16,2304]{1,0:T(8,128)(2,1)S(1)}, bf16[128,128]{1,0:T(8,128)(2,1...) custom-call(s32[1,128]{1,0:T(1,128)} %bitcast.7, bf16[1024,2304]{1,0:T(8,128)(2,1)} %bitcast.4), custom_call_target="tpu_custom_call" | custom-call | flops 226492416 | bytes 4718592 | tf_op jit(solution)/shard_map/pick_near/pallas_call | solution.py:101
  2.8 2.6 %collective-permute-start.7 = (bf16[16,2304]{1,0:T(8,128)(2,1)S(1)}, bf16[16,2304]{1,0:T(8,128)(2,1)S(1)}, u32[]{:S(2)}, u32[]{:S(2)}) collective-permute-start(bf16[16,2304]{1,0:T(8,128)(2,1)S(1)} %get-tuple-element.39), channel_id=1, source_target_pairs={{0,1},{1,2},{2,3},{3,4},{4,5},{5,6},{6,7},{7,0},{8,9},{9,10},{10,1... | collective-permute-start | bytes 221192 | tf_op jit(solution)/shard_map/ppermute | solution.py:224
  5.4 0.7 %collective-permute-start.8 = (bf16[16,2304]{1,0:T(8,128)(2,1)S(1)}, bf16[16,2304]{1,0:T(8,128)(2,1)S(1)}, u32[]{:S(2)}, u32[]{:S(2)}) collective-permute-start(bf16[16,2304]{1,0:T(8,128)(2,1)S(1)} %get-tuple-element.40), channel_id=1, source_target_pairs={{0,7},{1,0},{2,1},{3,2},{4,3},{5,4},{6,5},{7,6},{8,15},{9,8},{10,9... | collective-permute-start | bytes 221192 | tf_op jit(solution)/shard_map/ppermute | solution.py:224
  6.1 0.0 copy-done
  6.1 0.2 convert_reduce_fusion
  6.3 0.7 %compare_reduce_fusion = pred[]{:T(512)} fusion(s32[7]{0:T(128)S(1)} %convert_reduce_fusion), kind=kLoop, calls=%fused_computation.28 | loop fusion | flops 41 | bytes 29 | tf_op jit(solution)/shard_map/reduce_and | solution.py:249
  7.6 0.0 collective-permute-done.7.up_ref
  7.6 1.6 %collective-permute-done.8.down_ref = bf16[16,2304]{1,0:T(8,128)(2,1)S(1)} collective-permute-done((bf16[16,2304]{1,0:T(8,128)(2,1)S(1)}, bf16[16,2304]{1,0:T(8,128)(2,1)S(1)}, u32[]{:S(2)}, u32[]{:S(2)}) %collective-permute-start.8) | collective-permute-done | bytes 73760 | tf_op jit(solution)/shard_map/ppermute | solution.py:224
  9.2 0.1 settle.1
  9.3 1.7 %collective-permute-start.9 = (bf16[16,2304]{1,0:T(8,128)(2,1)S(1)}, bf16[16,2304]{1,0:T(8,128)(2,1)S(1)}, u32[]{:S(2)}, u32[]{:S(2)}) collective-permute-start(bf16[16,2304]{1,0:T(8,128)(2,1)S(1)} %settle.1), channel_id=1, source_target_pairs={{0,8},{8,0},{16,24},{24,16},{32,40},{40,32},{48,56},{56,48},{64,72... | collective-permute-start | bytes 221192 | tf_op jit(solution)/shard_map/ppermute | solution.py:230
  11.0 1.7 %collective-permute-done.9 = bf16[16,2304]{1,0:T(8,128)(2,1)S(1)} collective-permute-done((bf16[16,2304]{1,0:T(8,128)(2,1)S(1)}, bf16[16,2304]{1,0:T(8,128)(2,1)S(1)}, u32[]{:S(2)}, u32[]{:S(2)}) %collective-permute-start.9) | collective-permute-done | bytes 73760 | tf_op jit(solution)/shard_map/ppermute | solution.py:230
  12.8 6.9 %collective-permute-start.10 = (bf16[16,2304]{1,0:T(8,128)(2,1)S(1)}, bf16[16,2304]{1,0:T(8,128)(2,1)S(1)}, u32[]{:S(2)}, u32[]{:S(2)}) collective-permute-start(bf16[16,2304]{1,0:T(8,128)(2,1)S(1)} %fusion.7), channel_id=1, source_target_pairs={{0,128},{1,41},{2,130},{3,43},{4,132},{5,45},{6,134},{7,47},{8,136... | collective-permute-start | bytes 221192 | tf_op jit(solution)/shard_map/ppermute | solution.py:271
  19.7 0.0 collective-permute-start.11
  19.7 1.3 %collective-permute-start.12 = (bf16[16,2304]{1,0:T(8,128)(2,1)S(1)}, bf16[16,2304]{1,0:T(8,128)(2,1)S(1)}, u32[]{:S(2)}, u32[]{:S(2)}) collective-permute-start(bf16[16,2304]{1,0:T(8,128)(2,1)S(1)} %fusion.7), channel_id=1, source_target_pairs={{0,64},{1,17},{2,66},{3,19},{4,68},{5,21},{6,70},{7,23},{8,72},{9,... | collective-permute-start | bytes 221192 | tf_op jit(solution)/shard_map/ppermute | solution.py:271
  21.0 0.5 %collective-permute-done.10 = bf16[16,2304]{1,0:T(8,128)(2,1)S(1)} collective-permute-done((bf16[16,2304]{1,0:T(8,128)(2,1)S(1)}, bf16[16,2304]{1,0:T(8,128)(2,1)S(1)}, u32[]{:S(2)}, u32[]{:S(2)}) %collective-permute-start.10) | collective-permute-done | bytes 73760 | tf_op jit(solution)/shard_map/ppermute | solution.py:271
  21.5 2.6 %collective-permute-done.11 = bf16[16,2304]{1,0:T(8,128)(2,1)S(1)} collective-permute-done((bf16[16,2304]{1,0:T(8,128)(2,1)S(1)}, bf16[16,2304]{1,0:T(8,128)(2,1)S(1)}, u32[]{:S(2)}, u32[]{:S(2)}) %collective-permute-start.11) | collective-permute-done | bytes 73760 | tf_op jit(solution)/shard_map/ppermute | solution.py:271
  24.1 0.0 collective-permute-done.12
  24.1 0.1 select_convert_fusion.2
  24.2 2.8 %collective-permute-start.13 = (bf16[16,2304]{1,0:T(8,128)(2,1)S(1)}, bf16[16,2304]{1,0:T(8,128)(2,1)S(1)}, u32[]{:S(2)}, u32[]{:S(2)}) collective-permute-start(bf16[16,2304]{1,0:T(8,128)(2,1)S(1)} %get-tuple-element.64), channel_id=1, source_target_pairs={{0,40},{1,193},{2,42},{3,195},{4,44},{5,197},{6,46},{7,199},{8,32}... | collective-permute-start | bytes 221192 | tf_op jit(solution)/shard_map/ppermute | solution.py:271
  27.0 0.3 collective-permute-start.14
  27.4 0.3 collective-permute-start.15
  27.7 1.4 %collective-permute-done.13 = bf16[16,2304]{1,0:T(8,128)(2,1)S(1)} collective-permute-done((bf16[16,2304]{1,0:T(8,128)(2,1)S(1)}, bf16[16,2304]{1,0:T(8,128)(2,1)S(1)}, u32[]{:S(2)}, u32[]{:S(2)}) %collective-permute-start.13) | collective-permute-done | bytes 73760 | tf_op jit(solution)/shard_map/ppermute | solution.py:271
  29.1 2.7 %collective-permute-done.14 = bf16[16,2304]{1,0:T(8,128)(2,1)S(1)} collective-permute-done((bf16[16,2304]{1,0:T(8,128)(2,1)S(1)}, bf16[16,2304]{1,0:T(8,128)(2,1)S(1)}, u32[]{:S(2)}, u32[]{:S(2)}) %collective-permute-start.14) | collective-permute-done | bytes 73760 | tf_op jit(solution)/shard_map/ppermute | solution.py:271
  31.8 0.0 collective-permute-done.15
  31.8 0.1 fusion.4.own_ref
  31.9 2.2 %collective-permute-start.16 = (bf16[16,2304]{1,0:T(8,128)(2,1)S(1)}, bf16[16,2304]{1,0:T(8,128)(2,1)S(1)}, u32[]{:S(2)}, u32[]{:S(2)}) collective-permute-start(bf16[16,2304]{1,0:T(8,128)(2,1)S(1)} %fusion.4.own_ref), channel_id=1, source_target_pairs={{0,6},{1,7},{2,4},{3,5},{4,2},{5,3},{6,0},{7,1},{8,14},{9,15},{10,... | collective-permute-start | bytes 221192 | tf_op jit(solution)/shard_map/ppermute | solution.py:224
  34.1 0.5 %collective-permute-start.17 = (bf16[16,2304]{1,0:T(8,128)(2,1)S(1)}, bf16[16,2304]{1,0:T(8,128)(2,1)S(1)}, u32[]{:S(2)}, u32[]{:S(2)}) collective-permute-start(bf16[16,2304]{1,0:T(8,128)(2,1)S(1)} %fusion.4.own_ref), channel_id=1, source_target_pairs={{0,4},{1,5},{2,6},{3,7},{4,0},{5,1},{6,2},{7,3},{8,12},{9,13},{10,... | collective-permute-start | bytes 221192 | tf_op jit(solution)/shard_map/ppermute | solution.py:224
  34.6 0.7 %collective-permute-start.18 = (bf16[16,2304]{1,0:T(8,128)(2,1)S(1)}, bf16[16,2304]{1,0:T(8,128)(2,1)S(1)}, u32[]{:S(2)}, u32[]{:S(2)}) collective-permute-start(bf16[16,2304]{1,0:T(8,128)(2,1)S(1)} %fusion.4.own_ref), channel_id=1, source_target_pairs={{0,2},{1,3},{2,0},{3,1},{4,6},{5,7},{6,4},{7,5},{8,10},{9,11},{10,... | collective-permute-start | bytes 221192 | tf_op jit(solution)/shard_map/ppermute | solution.py:224
  35.3 2.3 %fetch.1 = (bf16[2304,1024]{1,0:T(8,128)(2,1)S(1)}, bf16[16,2304]{1,0:T(8,128)(2,1)S(1)}) custom-call(bf16[16,2304]{1,0:T(8,128)(2,1)S(1)} %fusion.4.own_ref, bf16[2304,1024]{1,0:T(8,128)(2,1)} %bitcast.6), custom_call_target="tpu_custom_call" | custom-call | bytes 9437184 | tf_op jit(solution)/shard_map/fetch/pallas_call | solution.py:165
  37.7 0.0 collective-permute-done.16
  37.7 1.1 %collective-permute-done.17 = bf16[16,2304]{1,0:T(8,128)(2,1)S(1)} collective-permute-done((bf16[16,2304]{1,0:T(8,128)(2,1)S(1)}, bf16[16,2304]{1,0:T(8,128)(2,1)S(1)}, u32[]{:S(2)}, u32[]{:S(2)}) %collective-permute-start.17) | collective-permute-done | bytes 73760 | tf_op jit(solution)/shard_map/ppermute | solution.py:224
  38.8 0.0 collective-permute-done.18
  38.9 4.1 %collective-permute-start.19 = (bf16[64,2304]{1,0:T(8,128)(2,1)S(1)}, bf16[64,2304]{1,0:T(8,128)(2,1)S(1)}, u32[]{:S(2)}, u32[]{:S(2)}) collective-permute-start(bf16[64,2304]{1,0:T(8,128)(2,1)S(1)} %constant_dynamic-update-slice_fusion.refs_0_), channel_id=1, source_target_pairs={{0,1},{1,0},{2,3},{3,2},{4,5},{5,4},{6,7},{7,6},{8,9},{9,8},{10,11... | collective-permute-start | bytes 884744 | tf_op jit(solution)/shard_map/ppermute | solution.py:224
  43.0 0.9 %product_own.1.refs_2_ = bf16[64,1024]{1,0:T(8,128)(2,1)S(1)} custom-call(bf16[64,2304]{1,0:T(8,128)(2,1)S(1)} %constant_dynamic-update-slice_fusion.refs_0_, bf16[2304,1024]{1,0:T(8,128)(2,1)S(1)} %get-tuple-element.45.refs_1_), custom_call_target="tpu_custom_call" | custom-call | flops 301989888 | bytes 4718592 | tf_op jit(solution)/shard_map/product_own/pallas_call | solution.py:201
  43.9 0.3 collective-permute-done.19.refs_0_
  44.2 1.8 %product_last.1 = bf16[128,1024]{1,0:T(8,128)(2,1)} custom-call(bf16[64,2304]{1,0:T(8,128)(2,1)S(1)} %collective-permute-done.19.refs_0_, bf16[2304,1024]{1,0:T(8,128)(2,1)S(1)} %get-tuple-element.45.refs_1_, bf16[64,1024]{1,0:T(8,128)(2,1)S(1)} %product_own.1.refs_2_, bf16[128,128]{1,0:T(8,128)(2,1)S(1)} %get-tuple-element.46.refs_3_), custom_call_target="tpu_custom_call" | custom-call | flops 301989888 | bytes 4718592 | tf_op jit(solution)/shard_map/product_last/pallas_call | solution.py:201
  (9 shorter events, 0.1 us)
Async XLA Ops:
  0.0 6.1 %copy-start = (s32[128]{0:T(128)S(1)}, s32[128]{0:T(128)}, u32[]{:S(2)}) copy-start(s32[128]{0:T(128)} %param.7) | copy-start | bytes 1540
  2.8 4.8 %collective-permute-start.7 = (bf16[16,2304]{1,0:T(8,128)(2,1)S(1)}, bf16[16,2304]{1,0:T(8,128)(2,1)S(1)}, u32[]{:S(2)}, u32[]{:S(2)}) collective-permute-start(bf16[16,2304]{1,0:T(8,128)(2,1)S(1)} %get-tuple-element.39), channel_id=1, source_target_pairs={{0,1},{1,2},{2,3},{3,4},{4,5},{5,6},{6,7},{7,0},{8,9},{9,10},{10,1... | collective-permute-start | bytes 221192 | tf_op jit(solution)/shard_map/ppermute | solution.py:224
  5.4 3.8 %collective-permute-start.8 = (bf16[16,2304]{1,0:T(8,128)(2,1)S(1)}, bf16[16,2304]{1,0:T(8,128)(2,1)S(1)}, u32[]{:S(2)}, u32[]{:S(2)}) collective-permute-start(bf16[16,2304]{1,0:T(8,128)(2,1)S(1)} %get-tuple-element.40), channel_id=1, source_target_pairs={{0,7},{1,0},{2,1},{3,2},{4,3},{5,4},{6,5},{7,6},{8,15},{9,8},{10,9... | collective-permute-start | bytes 221192 | tf_op jit(solution)/shard_map/ppermute | solution.py:224
  9.3 3.5 %collective-permute-start.9 = (bf16[16,2304]{1,0:T(8,128)(2,1)S(1)}, bf16[16,2304]{1,0:T(8,128)(2,1)S(1)}, u32[]{:S(2)}, u32[]{:S(2)}) collective-permute-start(bf16[16,2304]{1,0:T(8,128)(2,1)S(1)} %settle.1), channel_id=1, source_target_pairs={{0,8},{8,0},{16,24},{24,16},{32,40},{40,32},{48,56},{56,48},{64,72... | collective-permute-start | bytes 221192 | tf_op jit(solution)/shard_map/ppermute | solution.py:230
  12.8 8.7 %collective-permute-start.10 = (bf16[16,2304]{1,0:T(8,128)(2,1)S(1)}, bf16[16,2304]{1,0:T(8,128)(2,1)S(1)}, u32[]{:S(2)}, u32[]{:S(2)}) collective-permute-start(bf16[16,2304]{1,0:T(8,128)(2,1)S(1)} %fusion.7), channel_id=1, source_target_pairs={{0,128},{1,41},{2,130},{3,43},{4,132},{5,45},{6,134},{7,47},{8,136... | collective-permute-start | bytes 221192 | tf_op jit(solution)/shard_map/ppermute | solution.py:271
  19.7 4.4 %collective-permute-start.11 = (bf16[16,2304]{1,0:T(8,128)(2,1)S(1)}, bf16[16,2304]{1,0:T(8,128)(2,1)S(1)}, u32[]{:S(2)}, u32[]{:S(2)}) collective-permute-start(bf16[16,2304]{1,0:T(8,128)(2,1)S(1)} %fusion.7), channel_id=1, source_target_pairs={{0,192},{1,57},{2,194},{3,59},{4,196},{5,61},{6,198},{7,63},{8,200... | collective-permute-start | bytes 221192 | tf_op jit(solution)/shard_map/ppermute | solution.py:271
  19.7 4.4 %collective-permute-start.12 = (bf16[16,2304]{1,0:T(8,128)(2,1)S(1)}, bf16[16,2304]{1,0:T(8,128)(2,1)S(1)}, u32[]{:S(2)}, u32[]{:S(2)}) collective-permute-start(bf16[16,2304]{1,0:T(8,128)(2,1)S(1)} %fusion.7), channel_id=1, source_target_pairs={{0,64},{1,17},{2,66},{3,19},{4,68},{5,21},{6,70},{7,23},{8,72},{9,... | collective-permute-start | bytes 221192 | tf_op jit(solution)/shard_map/ppermute | solution.py:271
  24.2 4.9 %collective-permute-start.13 = (bf16[16,2304]{1,0:T(8,128)(2,1)S(1)}, bf16[16,2304]{1,0:T(8,128)(2,1)S(1)}, u32[]{:S(2)}, u32[]{:S(2)}) collective-permute-start(bf16[16,2304]{1,0:T(8,128)(2,1)S(1)} %get-tuple-element.64), channel_id=1, source_target_pairs={{0,40},{1,193},{2,42},{3,195},{4,44},{5,197},{6,46},{7,199},{8,32}... | collective-permute-start | bytes 221192 | tf_op jit(solution)/shard_map/ppermute | solution.py:271
  27.0 4.8 %collective-permute-start.14 = (bf16[16,2304]{1,0:T(8,128)(2,1)S(1)}, bf16[16,2304]{1,0:T(8,128)(2,1)S(1)}, u32[]{:S(2)}, u32[]{:S(2)}) collective-permute-start(bf16[16,2304]{1,0:T(8,128)(2,1)S(1)} %get-tuple-element.65), channel_id=1, source_target_pairs={{0,56},{1,129},{2,58},{3,131},{4,60},{5,133},{6,62},{7,135},{8,48}... | collective-permute-start | bytes 221192 | tf_op jit(solution)/shard_map/ppermute | solution.py:271
  27.4 4.4 %collective-permute-start.15 = (bf16[16,2304]{1,0:T(8,128)(2,1)S(1)}, bf16[16,2304]{1,0:T(8,128)(2,1)S(1)}, u32[]{:S(2)}, u32[]{:S(2)}) collective-permute-start(bf16[16,2304]{1,0:T(8,128)(2,1)S(1)} %get-tuple-element.66), channel_id=1, source_target_pairs={{0,16},{1,65},{2,18},{3,67},{4,20},{5,69},{6,22},{7,71},{8,24},{9,... | collective-permute-start | bytes 221192 | tf_op jit(solution)/shard_map/ppermute | solution.py:271
  31.9 5.7 %collective-permute-start.16 = (bf16[16,2304]{1,0:T(8,128)(2,1)S(1)}, bf16[16,2304]{1,0:T(8,128)(2,1)S(1)}, u32[]{:S(2)}, u32[]{:S(2)}) collective-permute-start(bf16[16,2304]{1,0:T(8,128)(2,1)S(1)} %fusion.4.own_ref), channel_id=1, source_target_pairs={{0,6},{1,7},{2,4},{3,5},{4,2},{5,3},{6,0},{7,1},{8,14},{9,15},{10,... | collective-permute-start | bytes 221192 | tf_op jit(solution)/shard_map/ppermute | solution.py:224
  34.1 4.7 %collective-permute-start.17 = (bf16[16,2304]{1,0:T(8,128)(2,1)S(1)}, bf16[16,2304]{1,0:T(8,128)(2,1)S(1)}, u32[]{:S(2)}, u32[]{:S(2)}) collective-permute-start(bf16[16,2304]{1,0:T(8,128)(2,1)S(1)} %fusion.4.own_ref), channel_id=1, source_target_pairs={{0,4},{1,5},{2,6},{3,7},{4,0},{5,1},{6,2},{7,3},{8,12},{9,13},{10,... | collective-permute-start | bytes 221192 | tf_op jit(solution)/shard_map/ppermute | solution.py:224
  34.6 4.2 %collective-permute-start.18 = (bf16[16,2304]{1,0:T(8,128)(2,1)S(1)}, bf16[16,2304]{1,0:T(8,128)(2,1)S(1)}, u32[]{:S(2)}, u32[]{:S(2)}) collective-permute-start(bf16[16,2304]{1,0:T(8,128)(2,1)S(1)} %fusion.4.own_ref), channel_id=1, source_target_pairs={{0,2},{1,3},{2,0},{3,1},{4,6},{5,7},{6,4},{7,5},{8,10},{9,11},{10,... | collective-permute-start | bytes 221192 | tf_op jit(solution)/shard_map/ppermute | solution.py:224
  38.9 5.3 %collective-permute-start.19 = (bf16[64,2304]{1,0:T(8,128)(2,1)S(1)}, bf16[64,2304]{1,0:T(8,128)(2,1)S(1)}, u32[]{:S(2)}, u32[]{:S(2)}) collective-permute-start(bf16[64,2304]{1,0:T(8,128)(2,1)S(1)} %constant_dynamic-update-slice_fusion.refs_0_), channel_id=1, source_target_pairs={{0,1},{1,0},{2,3},{3,2},{4,5},{5,4},{6,7},{7,6},{8,9},{9,8},{10,11... | collective-permute-start | bytes 884744 | tf_op jit(solution)/shard_map/ppermute | solution.py:224

commit v8 on v7

--- a/solution.py
+++ b/solution.py
@@ -270,7 +270,7 @@
                 pairs.append((layer * FEATS + f, to * FEATS + f))
         return lax.ppermute(v, ("layer", "feat"), pairs)
 
-    ways = ((2, 5), (3, 7), (1, 2))
+    ways = ((2, 5), (3, 2), (1, 7))
     pair = total
     low = pair.astype(BF)
     for dy, dz in ways:

time: 46.2 us -> 46.2 us (level)
  starting transfers between devices: 24.2 us -> 22.8 us
  waiting for transfers between devices: 11.9 us -> 13.2 us
    ppermute x6, starting transfers between devices: 10.7 us -> 9.52 us  [feat_step(): return lax.ppermute(v, 'feat', [(i, move(i) % FEATS) for i in range(FEATS)])]
    ppermute x6, waiting for transfers between devices: 7.23 us -> 8.44 us  [crossed(): return lax.ppermute(v, ('layer', 'feat'), pairs)]
  transfers between devices with their start and end apart: 13 -> 13, of which waited for: 8 -> 9; matrix products, arithmetic and copies ran while one was open for 2% -> 2% of each run, Pallas kernels for 7% -> 7%
where the time goes in v8:
time: 46.2 us; the launch traced here: 46 us
  starting transfers between devices  22.8 us (49%)
  waiting for transfers between devices  13.2 us (29%)
  Pallas kernels  7.95 us (17%)
  other arithmetic  1.14 us (2%)
  between operations  0.75 us (2%)
    ppermute x6, starting transfers between devices, crossed(): return lax.ppermute(v, ('layer', 'feat'), pairs)  11.6 us
    ppermute x6, starting transfers between devices, feat_step(): return lax.ppermute(v, 'feat', [(i, move(i) % FEATS) for i in range(FEATS)])  9.52 us
    ppermute x6, waiting for transfers between devices, crossed(): return lax.ppermute(v, ('layer', 'feat'), pairs)  8.44 us
    ppermute x6, waiting for transfers between devices, feat_step(): return lax.ppermute(v, 'feat', [(i, move(i) % FEATS) for i in range(FEATS)])  3.05 us
    pallas_call x1, Pallas kernels, pick(): pl.pallas_call(lambda *refs: pick_kernel(near, *refs), in_specs=[pl.Block...  2.81 us
    pallas_call x2, Pallas kernels, product(): pl.pallas_call(lambda *refs: product_kernel(last, *refs), in_specs=[pl.Bl...  2.73 us
    pallas_call x1, Pallas kernels, fetch(): pl.pallas_call(fetch_kernel, in_specs=[pl.BlockSpec(memory_space=pltpu.VM...  2.34 us
    ppermute x1, waiting for transfers between devices, along_z(): return lax.ppermute(v, 'layer', [(i, i ^ d) for i in range(LAYERS)])  1.74 us
  transfers between devices with their start and end apart: 13, of which 9 were waited for; matrix products, arithmetic and copies ran while one was open for 2% of the time, Pallas kernels for 7%

profile of v8, /device:TPU:1, one launch (start us, length us, event | category | flops | bytes accessed | tf_op | source)
XLA Modules:
  0.0 46.0 jit_solution(13388326833267722954)
XLA Ops:
  0.0 0.0 copy-start
  0.0 2.8 %pick_near.1 = (bf16[16,2304]{1,0:T(8,128)(2,1)S(1)}, bf16[16,2304]{1,0:T(8,128)(2,1)S(1)}, bf16[16,2304]{1,0:T(8,128)(2,1)S(1)}, bf16[128,128]{1,0:T(8,128)(2,1...) custom-call(s32[1,128]{1,0:T(1,128)} %bitcast.7, bf16[1024,2304]{1,0:T(8,128)(2,1)} %bitcast.4), custom_call_target="tpu_custom_call" | custom-call | flops 226492416 | bytes 4718592 | tf_op jit(solution)/shard_map/pick_near/pallas_call | solution.py:101
  2.8 2.6 %collective-permute-start.7 = (bf16[16,2304]{1,0:T(8,128)(2,1)S(1)}, bf16[16,2304]{1,0:T(8,128)(2,1)S(1)}, u32[]{:S(2)}, u32[]{:S(2)}) collective-permute-start(bf16[16,2304]{1,0:T(8,128)(2,1)S(1)} %get-tuple-element.39), channel_id=1, source_target_pairs={{0,1},{1,2},{2,3},{3,4},{4,5},{5,6},{6,7},{7,0},{8,9},{9,10},{10,1... | collective-permute-start | bytes 221192 | tf_op jit(solution)/shard_map/ppermute | solution.py:224
  5.4 0.7 %collective-permute-start.8 = (bf16[16,2304]{1,0:T(8,128)(2,1)S(1)}, bf16[16,2304]{1,0:T(8,128)(2,1)S(1)}, u32[]{:S(2)}, u32[]{:S(2)}) collective-permute-start(bf16[16,2304]{1,0:T(8,128)(2,1)S(1)} %get-tuple-element.40), channel_id=1, source_target_pairs={{0,7},{1,0},{2,1},{3,2},{4,3},{5,4},{6,5},{7,6},{8,15},{9,8},{10,9... | collective-permute-start | bytes 221192 | tf_op jit(solution)/shard_map/ppermute | solution.py:224
  6.1 0.0 copy-done
  6.1 0.2 convert_reduce_fusion
  6.3 0.7 %compare_reduce_fusion = pred[]{:T(512)} fusion(s32[7]{0:T(128)S(1)} %convert_reduce_fusion), kind=kLoop, calls=%fused_computation.28 | loop fusion | flops 41 | bytes 29 | tf_op jit(solution)/shard_map/reduce_and | solution.py:249
  7.6 0.0 collective-permute-done.7.up_ref
  7.6 1.6 %collective-permute-done.8.down_ref = bf16[16,2304]{1,0:T(8,128)(2,1)S(1)} collective-permute-done((bf16[16,2304]{1,0:T(8,128)(2,1)S(1)}, bf16[16,2304]{1,0:T(8,128)(2,1)S(1)}, u32[]{:S(2)}, u32[]{:S(2)}) %collective-permute-start.8) | collective-permute-done | bytes 73760 | tf_op jit(solution)/shard_map/ppermute | solution.py:224
  9.2 0.1 settle.1
  9.3 1.7 %collective-permute-start.9 = (bf16[16,2304]{1,0:T(8,128)(2,1)S(1)}, bf16[16,2304]{1,0:T(8,128)(2,1)S(1)}, u32[]{:S(2)}, u32[]{:S(2)}) collective-permute-start(bf16[16,2304]{1,0:T(8,128)(2,1)S(1)} %settle.1), channel_id=1, source_target_pairs={{0,8},{8,0},{16,24},{24,16},{32,40},{40,32},{48,56},{56,48},{64,72... | collective-permute-start | bytes 221192 | tf_op jit(solution)/shard_map/ppermute | solution.py:230
  11.0 1.7 %collective-permute-done.9 = bf16[16,2304]{1,0:T(8,128)(2,1)S(1)} collective-permute-done((bf16[16,2304]{1,0:T(8,128)(2,1)S(1)}, bf16[16,2304]{1,0:T(8,128)(2,1)S(1)}, u32[]{:S(2)}, u32[]{:S(2)}) %collective-permute-start.9) | collective-permute-done | bytes 73760 | tf_op jit(solution)/shard_map/ppermute | solution.py:230
  12.8 6.9 %collective-permute-start.10 = (bf16[16,2304]{1,0:T(8,128)(2,1)S(1)}, bf16[16,2304]{1,0:T(8,128)(2,1)S(1)}, u32[]{:S(2)}, u32[]{:S(2)}) collective-permute-start(bf16[16,2304]{1,0:T(8,128)(2,1)S(1)} %fusion.7), channel_id=1, source_target_pairs={{0,128},{1,41},{2,130},{3,43},{4,132},{5,45},{6,134},{7,47},{8,136... | collective-permute-start | bytes 221192 | tf_op jit(solution)/shard_map/ppermute | solution.py:271
  19.7 1.2 %collective-permute-start.11 = (bf16[16,2304]{1,0:T(8,128)(2,1)S(1)}, bf16[16,2304]{1,0:T(8,128)(2,1)S(1)}, u32[]{:S(2)}, u32[]{:S(2)}) collective-permute-start(bf16[16,2304]{1,0:T(8,128)(2,1)S(1)} %fusion.7), channel_id=1, source_target_pairs={{0,192},{1,17},{2,194},{3,19},{4,196},{5,21},{6,198},{7,23},{8,200... | collective-permute-start | bytes 221192 | tf_op jit(solution)/shard_map/ppermute | solution.py:271
  20.9 0.0 collective-permute-start.12
  20.9 0.6 %collective-permute-done.10 = bf16[16,2304]{1,0:T(8,128)(2,1)S(1)} collective-permute-done((bf16[16,2304]{1,0:T(8,128)(2,1)S(1)}, bf16[16,2304]{1,0:T(8,128)(2,1)S(1)}, u32[]{:S(2)}, u32[]{:S(2)}) %collective-permute-start.10) | collective-permute-done | bytes 73760 | tf_op jit(solution)/shard_map/ppermute | solution.py:271
  21.5 3.1 %collective-permute-done.11 = bf16[16,2304]{1,0:T(8,128)(2,1)S(1)} collective-permute-done((bf16[16,2304]{1,0:T(8,128)(2,1)S(1)}, bf16[16,2304]{1,0:T(8,128)(2,1)S(1)}, u32[]{:S(2)}, u32[]{:S(2)}) %collective-permute-start.11) | collective-permute-done | bytes 73760 | tf_op jit(solution)/shard_map/ppermute | solution.py:271
  24.6 0.7 %collective-permute-done.12 = bf16[16,2304]{1,0:T(8,128)(2,1)S(1)} collective-permute-done((bf16[16,2304]{1,0:T(8,128)(2,1)S(1)}, bf16[16,2304]{1,0:T(8,128)(2,1)S(1)}, u32[]{:S(2)}, u32[]{:S(2)}) %collective-permute-start.12) | collective-permute-done | bytes 73760 | tf_op jit(solution)/shard_map/ppermute | solution.py:271
  25.3 0.1 select_convert_fusion.2
  25.4 2.8 %collective-permute-start.13 = (bf16[16,2304]{1,0:T(8,128)(2,1)S(1)}, bf16[16,2304]{1,0:T(8,128)(2,1)S(1)}, u32[]{:S(2)}, u32[]{:S(2)}) collective-permute-start(bf16[16,2304]{1,0:T(8,128)(2,1)S(1)} %get-tuple-element.64), channel_id=1, source_target_pairs={{0,40},{1,193},{2,42},{3,195},{4,44},{5,197},{6,46},{7,199},{8,32}... | collective-permute-start | bytes 221192 | tf_op jit(solution)/shard_map/ppermute | solution.py:271
  28.2 0.3 collective-permute-start.14
  28.6 0.3 collective-permute-start.15
  28.9 1.4 %collective-permute-done.13 = bf16[16,2304]{1,0:T(8,128)(2,1)S(1)} collective-permute-done((bf16[16,2304]{1,0:T(8,128)(2,1)S(1)}, bf16[16,2304]{1,0:T(8,128)(2,1)S(1)}, u32[]{:S(2)}, u32[]{:S(2)}) %collective-permute-start.13) | collective-permute-done | bytes 73760 | tf_op jit(solution)/shard_map/ppermute | solution.py:271
  30.3 2.6 %collective-permute-done.14 = bf16[16,2304]{1,0:T(8,128)(2,1)S(1)} collective-permute-done((bf16[16,2304]{1,0:T(8,128)(2,1)S(1)}, bf16[16,2304]{1,0:T(8,128)(2,1)S(1)}, u32[]{:S(2)}, u32[]{:S(2)}) %collective-permute-start.14) | collective-permute-done | bytes 73760 | tf_op jit(solution)/shard_map/ppermute | solution.py:271
  32.9 0.0 collective-permute-done.15
  32.9 0.1 fusion.4.own_ref
  33.1 2.2 %collective-permute-start.16 = (bf16[16,2304]{1,0:T(8,128)(2,1)S(1)}, bf16[16,2304]{1,0:T(8,128)(2,1)S(1)}, u32[]{:S(2)}, u32[]{:S(2)}) collective-permute-start(bf16[16,2304]{1,0:T(8,128)(2,1)S(1)} %fusion.4.own_ref), channel_id=1, source_target_pairs={{0,6},{1,7},{2,4},{3,5},{4,2},{5,3},{6,0},{7,1},{8,14},{9,15},{10,... | collective-permute-start | bytes 221192 | tf_op jit(solution)/shard_map/ppermute | solution.py:224
  35.3 0.5 %collective-permute-start.17 = (bf16[16,2304]{1,0:T(8,128)(2,1)S(1)}, bf16[16,2304]{1,0:T(8,128)(2,1)S(1)}, u32[]{:S(2)}, u32[]{:S(2)}) collective-permute-start(bf16[16,2304]{1,0:T(8,128)(2,1)S(1)} %fusion.4.own_ref), channel_id=1, source_target_pairs={{0,4},{1,5},{2,6},{3,7},{4,0},{5,1},{6,2},{7,3},{8,12},{9,13},{10,... | collective-permute-start | bytes 221192 | tf_op jit(solution)/shard_map/ppermute | solution.py:224
  35.8 0.6 %collective-permute-start.18 = (bf16[16,2304]{1,0:T(8,128)(2,1)S(1)}, bf16[16,2304]{1,0:T(8,128)(2,1)S(1)}, u32[]{:S(2)}, u32[]{:S(2)}) collective-permute-start(bf16[16,2304]{1,0:T(8,128)(2,1)S(1)} %fusion.4.own_ref), channel_id=1, source_target_pairs={{0,2},{1,3},{2,0},{3,1},{4,6},{5,7},{6,4},{7,5},{8,10},{9,11},{10,... | collective-permute-start | bytes 221192 | tf_op jit(solution)/shard_map/ppermute | solution.py:224
  36.4 2.3 %fetch.1 = (bf16[2304,1024]{1,0:T(8,128)(2,1)S(1)}, bf16[16,2304]{1,0:T(8,128)(2,1)S(1)}) custom-call(bf16[16,2304]{1,0:T(8,128)(2,1)S(1)} %fusion.4.own_ref, bf16[2304,1024]{1,0:T(8,128)(2,1)} %bitcast.6), custom_call_target="tpu_custom_call" | custom-call | bytes 9437184 | tf_op jit(solution)/shard_map/fetch/pallas_call | solution.py:165
  38.8 0.0 collective-permute-done.16
  38.8 1.2 %collective-permute-done.17 = bf16[16,2304]{1,0:T(8,128)(2,1)S(1)} collective-permute-done((bf16[16,2304]{1,0:T(8,128)(2,1)S(1)}, bf16[16,2304]{1,0:T(8,128)(2,1)S(1)}, u32[]{:S(2)}, u32[]{:S(2)}) %collective-permute-start.17) | collective-permute-done | bytes 73760 | tf_op jit(solution)/shard_map/ppermute | solution.py:224
  40.0 0.0 collective-permute-done.18
  40.1 2.9 %collective-permute-start.19 = (bf16[64,2304]{1,0:T(8,128)(2,1)S(1)}, bf16[64,2304]{1,0:T(8,128)(2,1)S(1)}, u32[]{:S(2)}, u32[]{:S(2)}) collective-permute-start(bf16[64,2304]{1,0:T(8,128)(2,1)S(1)} %constant_dynamic-update-slice_fusion.refs_0_), channel_id=1, source_target_pairs={{0,1},{1,0},{2,3},{3,2},{4,5},{5,4},{6,7},{7,6},{8,9},{9,8},{10,11... | collective-permute-start | bytes 884744 | tf_op jit(solution)/shard_map/ppermute | solution.py:224
  43.0 0.9 %product_own.1.refs_2_ = bf16[64,1024]{1,0:T(8,128)(2,1)S(1)} custom-call(bf16[64,2304]{1,0:T(8,128)(2,1)S(1)} %constant_dynamic-update-slice_fusion.refs_0_, bf16[2304,1024]{1,0:T(8,128)(2,1)S(1)} %get-tuple-element.45.refs_1_), custom_call_target="tpu_custom_call" | custom-call | flops 301989888 | bytes 4718592 | tf_op jit(solution)/shard_map/product_own/pallas_call | solution.py:201
  43.9 0.3 collective-permute-done.19.refs_0_
  44.2 1.8 %product_last.1 = bf16[128,1024]{1,0:T(8,128)(2,1)} custom-call(bf16[64,2304]{1,0:T(8,128)(2,1)S(1)} %collective-permute-done.19.refs_0_, bf16[2304,1024]{1,0:T(8,128)(2,1)S(1)} %get-tuple-element.45.refs_1_, bf16[64,1024]{1,0:T(8,128)(2,1)S(1)} %product_own.1.refs_2_, bf16[128,128]{1,0:T(8,128)(2,1)S(1)} %get-tuple-element.46.refs_3_), custom_call_target="tpu_custom_call" | custom-call | flops 301989888 | bytes 4718592 | tf_op jit(solution)/shard_map/product_last/pallas_call | solution.py:201
  (9 shorter events, 0.1 us)
Async XLA Ops:
  0.0 6.1 %copy-start = (s32[128]{0:T(128)S(1)}, s32[128]{0:T(128)}, u32[]{:S(2)}) copy-start(s32[128]{0:T(128)} %param.7) | copy-start | bytes 1540
  2.8 4.8 %collective-permute-start.7 = (bf16[16,2304]{1,0:T(8,128)(2,1)S(1)}, bf16[16,2304]{1,0:T(8,128)(2,1)S(1)}, u32[]{:S(2)}, u32[]{:S(2)}) collective-permute-start(bf16[16,2304]{1,0:T(8,128)(2,1)S(1)} %get-tuple-element.39), channel_id=1, source_target_pairs={{0,1},{1,2},{2,3},{3,4},{4,5},{5,6},{6,7},{7,0},{8,9},{9,10},{10,1... | collective-permute-start | bytes 221192 | tf_op jit(solution)/shard_map/ppermute | solution.py:224
  5.4 3.8 %collective-permute-start.8 = (bf16[16,2304]{1,0:T(8,128)(2,1)S(1)}, bf16[16,2304]{1,0:T(8,128)(2,1)S(1)}, u32[]{:S(2)}, u32[]{:S(2)}) collective-permute-start(bf16[16,2304]{1,0:T(8,128)(2,1)S(1)} %get-tuple-element.40), channel_id=1, source_target_pairs={{0,7},{1,0},{2,1},{3,2},{4,3},{5,4},{6,5},{7,6},{8,15},{9,8},{10,9... | collective-permute-start | bytes 221192 | tf_op jit(solution)/shard_map/ppermute | solution.py:224
  9.3 3.5 %collective-permute-start.9 = (bf16[16,2304]{1,0:T(8,128)(2,1)S(1)}, bf16[16,2304]{1,0:T(8,128)(2,1)S(1)}, u32[]{:S(2)}, u32[]{:S(2)}) collective-permute-start(bf16[16,2304]{1,0:T(8,128)(2,1)S(1)} %settle.1), channel_id=1, source_target_pairs={{0,8},{8,0},{16,24},{24,16},{32,40},{40,32},{48,56},{56,48},{64,72... | collective-permute-start | bytes 221192 | tf_op jit(solution)/shard_map/ppermute | solution.py:230
  12.8 8.7 %collective-permute-start.10 = (bf16[16,2304]{1,0:T(8,128)(2,1)S(1)}, bf16[16,2304]{1,0:T(8,128)(2,1)S(1)}, u32[]{:S(2)}, u32[]{:S(2)}) collective-permute-start(bf16[16,2304]{1,0:T(8,128)(2,1)S(1)} %fusion.7), channel_id=1, source_target_pairs={{0,128},{1,41},{2,130},{3,43},{4,132},{5,45},{6,134},{7,47},{8,136... | collective-permute-start | bytes 221192 | tf_op jit(solution)/shard_map/ppermute | solution.py:271
  19.7 4.9 %collective-permute-start.11 = (bf16[16,2304]{1,0:T(8,128)(2,1)S(1)}, bf16[16,2304]{1,0:T(8,128)(2,1)S(1)}, u32[]{:S(2)}, u32[]{:S(2)}) collective-permute-start(bf16[16,2304]{1,0:T(8,128)(2,1)S(1)} %fusion.7), channel_id=1, source_target_pairs={{0,192},{1,17},{2,194},{3,19},{4,196},{5,21},{6,198},{7,23},{8,200... | collective-permute-start | bytes 221192 | tf_op jit(solution)/shard_map/ppermute | solution.py:271
  20.9 4.4 %collective-permute-start.12 = (bf16[16,2304]{1,0:T(8,128)(2,1)S(1)}, bf16[16,2304]{1,0:T(8,128)(2,1)S(1)}, u32[]{:S(2)}, u32[]{:S(2)}) collective-permute-start(bf16[16,2304]{1,0:T(8,128)(2,1)S(1)} %fusion.7), channel_id=1, source_target_pairs={{0,64},{1,57},{2,66},{3,59},{4,68},{5,61},{6,70},{7,63},{8,72},{9,... | collective-permute-start | bytes 221192 | tf_op jit(solution)/shard_map/ppermute | solution.py:271
  25.4 4.9 %collective-permute-start.13 = (bf16[16,2304]{1,0:T(8,128)(2,1)S(1)}, bf16[16,2304]{1,0:T(8,128)(2,1)S(1)}, u32[]{:S(2)}, u32[]{:S(2)}) collective-permute-start(bf16[16,2304]{1,0:T(8,128)(2,1)S(1)} %get-tuple-element.64), channel_id=1, source_target_pairs={{0,40},{1,193},{2,42},{3,195},{4,44},{5,197},{6,46},{7,199},{8,32}... | collective-permute-start | bytes 221192 | tf_op jit(solution)/shard_map/ppermute | solution.py:271
  28.2 4.7 %collective-permute-start.14 = (bf16[16,2304]{1,0:T(8,128)(2,1)S(1)}, bf16[16,2304]{1,0:T(8,128)(2,1)S(1)}, u32[]{:S(2)}, u32[]{:S(2)}) collective-permute-start(bf16[16,2304]{1,0:T(8,128)(2,1)S(1)} %get-tuple-element.65), channel_id=1, source_target_pairs={{0,56},{1,129},{2,58},{3,131},{4,60},{5,133},{6,62},{7,135},{8,48}... | collective-permute-start | bytes 221192 | tf_op jit(solution)/shard_map/ppermute | solution.py:271
  28.6 4.4 %collective-permute-start.15 = (bf16[16,2304]{1,0:T(8,128)(2,1)S(1)}, bf16[16,2304]{1,0:T(8,128)(2,1)S(1)}, u32[]{:S(2)}, u32[]{:S(2)}) collective-permute-start(bf16[16,2304]{1,0:T(8,128)(2,1)S(1)} %get-tuple-element.66), channel_id=1, source_target_pairs={{0,16},{1,65},{2,18},{3,67},{4,20},{5,69},{6,22},{7,71},{8,24},{9,... | collective-permute-start | bytes 221192 | tf_op jit(solution)/shard_map/ppermute | solution.py:271
  33.1 5.7 %collective-permute-start.16 = (bf16[16,2304]{1,0:T(8,128)(2,1)S(1)}, bf16[16,2304]{1,0:T(8,128)(2,1)S(1)}, u32[]{:S(2)}, u32[]{:S(2)}) collective-permute-start(bf16[16,2304]{1,0:T(8,128)(2,1)S(1)} %fusion.4.own_ref), channel_id=1, source_target_pairs={{0,6},{1,7},{2,4},{3,5},{4,2},{5,3},{6,0},{7,1},{8,14},{9,15},{10,... | collective-permute-start | bytes 221192 | tf_op jit(solution)/shard_map/ppermute | solution.py:224
  35.3 4.7 %collective-permute-start.17 = (bf16[16,2304]{1,0:T(8,128)(2,1)S(1)}, bf16[16,2304]{1,0:T(8,128)(2,1)S(1)}, u32[]{:S(2)}, u32[]{:S(2)}) collective-permute-start(bf16[16,2304]{1,0:T(8,128)(2,1)S(1)} %fusion.4.own_ref), channel_id=1, source_target_pairs={{0,4},{1,5},{2,6},{3,7},{4,0},{5,1},{6,2},{7,3},{8,12},{9,13},{10,... | collective-permute-start | bytes 221192 | tf_op jit(solution)/shard_map/ppermute | solution.py:224
  35.8 4.2 %collective-permute-start.18 = (bf16[16,2304]{1,0:T(8,128)(2,1)S(1)}, bf16[16,2304]{1,0:T(8,128)(2,1)S(1)}, u32[]{:S(2)}, u32[]{:S(2)}) collective-permute-start(bf16[16,2304]{1,0:T(8,128)(2,1)S(1)} %fusion.4.own_ref), channel_id=1, source_target_pairs={{0,2},{1,3},{2,0},{3,1},{4,6},{5,7},{6,4},{7,5},{8,10},{9,11},{10,... | collective-permute-start | bytes 221192 | tf_op jit(solution)/shard_map/ppermute | solution.py:224
  40.1 4.1 %collective-permute-start.19 = (bf16[64,2304]{1,0:T(8,128)(2,1)S(1)}, bf16[64,2304]{1,0:T(8,128)(2,1)S(1)}, u32[]{:S(2)}, u32[]{:S(2)}) collective-permute-start(bf16[64,2304]{1,0:T(8,128)(2,1)S(1)} %constant_dynamic-update-slice_fusion.refs_0_), channel_id=1, source_target_pairs={{0,1},{1,0},{2,3},{3,2},{4,5},{5,4},{6,7},{7,6},{8,9},{9,8},{10,11... | collective-permute-start | bytes 884744 | tf_op jit(solution)/shard_map/ppermute | solution.py:224
